TPU v7x, 512 devices: a whole 4x8x8 slice. The times are simulated.
512 devices in a mesh: tile: 16 (over x, z_lo), fsdp: 32 (over y, z_hi, core).
Axes of the slice: x: 4, y: 8, z: 8 (z_hi: 2, z_lo: 4; z = z_hi * 4 + z_lo), core: 2. Of those that a mesh axis runs over, the one named last changes fastest.
Arguments:
- tokens: bfloat16 [32, 12, 256, 4096], P('fsdp', None, 'tile'), may hold values from -6 to 6
- w_qkv: bfloat16 [4096, 384], P('fsdp'), may hold values from -4 to 4
- w_out: bfloat16 [128, 4096], P(None, 'fsdp'), may hold values from -0.5 to 0.5
- band: int32 [16, 2], P('tile'), may hold values from 1 to 2, as said below
- cotangent: bfloat16 [32, 12, 256, 4096], P('fsdp', None, 'tile'), may hold values from -6 to 6
Outputs:
- d_tokens: bfloat16 [32, 12, 256, 4096], P('fsdp', None, 'tile')
- grad_qkv: float32 [4096, 384], P('fsdp')
- grad_out: float32 [128, 4096], P(None, 'fsdp')
Inputs may be any that keep to these rules, and one draw needn't show every extreme that they name: Every entry is the width of an intersection band in longitude patch columns.
All inputs are finite; a program needn't handle non-finite values.
Results may differ from a plain program's by a relative error of at most 0.03.
Values may be sent and summed in bfloat16 or wider, within the bound.
No kernel may reach another device: no remote copies, remote signals or barrier semaphores. Data moves between devices by JAX's collectives and lax.ppermute only.
A program may use at most 64 MiB of HBM per device.

v0:
```python
import jax
import jax.numpy as jnp
from jax import lax
from jax.sharding import PartitionSpec as P

HALO = 2


EPS = 1e-05


def extended_2(block, sides, width):
    for axis, dim in sides:
        count = lax.axis_size(axis)
        forward = [(i, i + 1) for i in range(count - 1)]
        forward.append((count - 1, 0))
        backward = [(target, source) for source, target in forward]
        low = lax.ppermute(
            lax.slice_in_dim(block, block.shape[dim] - width, None, axis=dim), axis, forward
        )
        high = lax.ppermute(lax.slice_in_dim(block, 0, width, axis=dim), axis, backward)
        block = jnp.concatenate([low, block, high], axis=dim)
    return block


def local(tokens, w_qkv, w_out, band, cotangent):
    samples, lat_rows, lon_cols, features = tokens.shape
    head_dim = w_out.shape[0]
    num_rows = samples * lat_rows * lon_cols
    ext_cols = lon_cols + 2 * HALO
    tok_rows = tokens.reshape(num_rows, features)
    grad_rows = cotangent.reshape(num_rows, features)
    float_rows = tok_rows.astype(jnp.float32)
    inverse = lax.rsqrt(jnp.mean(float_rows * float_rows, axis=-1, keepdims=True) + EPS)
    normed = (float_rows * inverse).astype(jnp.bfloat16)
    part_in = normed
    projected = jnp.dot(
        part_in,
        lax.all_gather(w_qkv, "fsdp", axis=0, tiled=True),
        preferred_element_type=jnp.float32,
    )
    projected = projected.astype(jnp.bfloat16)
    queries = projected[:, :head_dim].reshape(samples, lat_rows * lon_cols, head_dim)
    key_value = projected[:, head_dim:].reshape(samples, lat_rows, lon_cols, 2 * head_dim)
    extended = extended_2(key_value, (("tile", 2),), HALO)
    ext_rows = extended.reshape(samples, lat_rows * ext_cols, 2 * head_dim)
    key_part = ext_rows[..., :head_dim]
    values = ext_rows[..., head_dim:]
    columns = jnp.arange(ext_cols)
    middle = (columns >= HALO) & (columns < lon_cols + HALO)
    left_ok = (columns < HALO) & (HALO - columns <= band[0, 0])
    right_ok = (columns >= lon_cols + HALO) & (columns - lon_cols - HALO + 1 <= band[0, 1])
    usable = jnp.tile(middle | left_ok | right_ok, lat_rows)
    score_scale = head_dim ** (-0.5)
    scores = (
        jnp.einsum("sqh,skh->sqk", queries, key_part, preferred_element_type=jnp.float32)
        * score_scale
    )
    scores = jnp.where(usable[None, None, :], scores, -jnp.inf)
    row_max = jnp.max(scores, axis=-1, keepdims=True)
    exp_scores = jnp.exp(scores - row_max)
    probs_full = exp_scores / jnp.sum(exp_scores, axis=-1, keepdims=True)
    probs_low = probs_full.astype(jnp.bfloat16)
    attended = jnp.einsum(
        "sqk,skh->sqh", probs_low, values, preferred_element_type=jnp.float32
    ).astype(jnp.bfloat16)
    att_rows = attended.reshape(num_rows, head_dim)
    part_in = grad_rows
    d_att = lax.dot_general(
        part_in,
        lax.all_gather(w_out, "fsdp", axis=1, tiled=True),
        (((1,), (1,)), ((), ())),
        preferred_element_type=jnp.float32,
    )
    d_att = d_att.astype(jnp.bfloat16).reshape(samples, lat_rows * lon_cols, head_dim)
    d_probs = jnp.einsum("sqh,skh->sqk", d_att, values, preferred_element_type=jnp.float32)
    row_inner = jnp.sum(probs_full * d_probs, axis=-1, keepdims=True)
    d_scores = (probs_full * (d_probs - row_inner) * score_scale).astype(jnp.bfloat16)
    d_query = jnp.einsum("sqk,skh->sqh", d_scores, key_part, preferred_element_type=jnp.float32)
    d_keys = jnp.einsum("sqk,sqh->skh", d_scores, queries, preferred_element_type=jnp.float32)
    d_values = jnp.einsum("sqk,sqh->skh", probs_low, d_att, preferred_element_type=jnp.float32)
    d_ext = jnp.concatenate([d_keys, d_values], axis=-1).reshape(
        samples, lat_rows, ext_cols, 2 * head_dim
    )
    edge_grads = jnp.concatenate([d_ext[:, :, :HALO], d_ext[:, :, lon_cols + HALO :]], axis=2)
    returned = extended_2(edge_grads.astype(jnp.bfloat16), (("tile", 2),), HALO).astype(
        edge_grads.dtype
    )
    own_grads = d_ext[:, :, HALO : HALO + lon_cols]
    own_grads = own_grads.at[:, :, :HALO].add(returned[:, :, :HALO])
    own_grads = own_grads.at[:, :, lon_cols - HALO :].add(
        returned[:, :, returned.shape[2] - HALO :]
    )
    d_qkv = jnp.concatenate(
        [d_query.reshape(num_rows, head_dim), own_grads.reshape(num_rows, 2 * head_dim)], axis=1
    ).astype(jnp.bfloat16)
    part_in = normed
    first_term = lax.dot_general(
        part_in, d_qkv, (((0,), (0,)), ((), ())), preferred_element_type=jnp.float32
    )
    second_term = lax.dot_general(
        grad_rows, att_rows, (((0,), (0,)), ((), ())), preferred_element_type=jnp.float32
    )
    shares = lax.psum_scatter(
        jnp.concatenate([first_term, second_term], axis=1).astype(jnp.bfloat16),
        "fsdp",
        scatter_dimension=0,
        tiled=True,
    ).astype(jnp.float32)
    shares = lax.psum(shares.astype(jnp.bfloat16), "tile").astype(jnp.float32)
    d_normed = lax.dot_general(
        d_qkv,
        lax.all_gather(w_qkv, "fsdp", axis=0, tiled=True),
        (((1,), (1,)), ((), ())),
        preferred_element_type=jnp.float32,
    )
    d_float = inverse * d_normed - float_rows * inverse**3 * jnp.mean(
        d_normed * float_rows, axis=-1, keepdims=True
    )
    d_tokens = d_float.astype(jnp.bfloat16).reshape(tokens.shape)
    return (d_tokens, shares[:, : 3 * head_dim], shares[:, 3 * head_dim :].T)


def solution(mesh):
    placed = (
        P("fsdp", None, "tile", None),
        P("fsdp", None),
        P(None, "fsdp"),
        P("tile", None),
        P("fsdp", None, "tile", None),
    )
    return jax.shard_map(
        local,
        mesh=mesh,
        in_specs=placed,
        out_specs=(P("fsdp", None, "tile", None), P("fsdp", None), P(None, "fsdp")),
        check_vma=False,
    )
```

profile of v0, /device:TPU:8, one launch (start us, length us, event | category | flops | bytes accessed | tf_op | source)
XLA Modules:
  0.0 554.7 jit_solution(10427950208826814163)
XLA Ops:
  8.7 1.3 fusion.22
  10.0 1.3 and_or_fusion
  11.4 1.8 multiply_reduce_fusion.1
  13.3 1.8 multiply_convert_fusion
  15.1 100.6 %all-gather.3.cloned.1.call-done = bf16[4096,384]{1,0:T(8,128)(2,1)} async-done(((bf16[128,384]{1,0:T(8,128)(2,1)}), bf16[4096,384]{1,0:T(8,128)(2,1)}) %all-gather.3.cloned.1.call-update) | async-done | bytes 3145744 | tf_op jit(solution)/shard_map/all_gather | solution.py:39
  115.7 2.9 convolution_convert_fusion.2
  119.3 2.2 collective-permute-start
  121.5 7.5 %collective-permute-start.1 = (bf16[1,12,2,256]{3,2,1,0:T(2,128)(2,1)S(1)}, bf16[1,12,2,256]{3,2,1,0:T(2,128)(2,1)S(1)}, u32[]{:S(2)}, u32[]{:S(2)}) collective-permute-start(bf16[1,12,2,256]{3,2,1,0:T(2,128)(2,1)S(1)} %get-tuple-element.39), channel_id=1, source_target_pairs={{32,0},{64,32},{96,64},{128,96},{160,128},{192,160},{224,192},{256... | collective-permute-start | bytes 36872 | tf_op jit(solution)/shard_map/ppermute | solution.py:21
  129.0 69.7 %all-gather.5.cloned.1.call-done = bf16[128,4096]{1,0:T(8,128)(2,1)} async-done(((bf16[128,128]{1,0:T(8,128)(2,1)}), bf16[128,4096]{1,0:T(8,128)(2,1)}) %all-gather.5.cloned.1.call-update) | async-done | bytes 1048592 | tf_op jit(solution)/shard_map/all_gather | solution.py:71
  198.7 1.8 convolution_convert_fusion.5
  202.2 1.1 fusion.23
  204.5 1.1 multiply_reduce_fusion.2
  207.7 2.6 fusion
  212.1 2.6 collective-permute-start.2
  214.7 7.2 %collective-permute-start.3 = (bf16[1,12,2,256]{3,2,1,0:T(2,128)(2,1)S(1)}, bf16[1,12,2,256]{3,2,1,0:T(2,128)(2,1)S(1)}, u32[]{:S(2)}, u32[]{:S(2)}) collective-permute-start(bf16[1,12,2,256]{3,2,1,0:T(2,128)(2,1)S(1)} %get-tuple-element.37), channel_id=1, source_target_pairs={{32,0},{64,32},{96,64},{128,96},{160,128},{192,160},{224,192},{256... | collective-permute-start | bytes 36872 | tf_op jit(solution)/shard_map/ppermute | solution.py:21
  222.0 1.3 collective-permute-done.3
  224.7 2.2 pad_maximum_fusion
  226.9 6.5 %copy.11 = bf16[4096,512]{1,0:T(8,128)(2,1)} copy(bf16[4096,512]{0,1:T(8,128)(2,1)} %pad_maximum_fusion) | data formatting | bytes 8388608
  233.5 1.3 copy-done.1
  234.8 4.8 multiply_reduce_fusion
  239.6 141.0 %reduce-scatter.4.cloned.1.call-done = bf16[128,512]{1,0:T(8,128)(2,1)} async-done(((bf16[4096,512]{1,0:T(8,128)(2,1)}), bf16[128,512]{1,0:T(8,128)(2,1)}) %reduce-scatter.4.cloned.1.call-update) | async-done | bytes 131088
  380.6 1.7 copy.12
  382.3 4.0 subtract_convert_fusion
  386.3 158.6 %all-reduce.2.cloned.1.call-done = bf16[128,512]{0,1:T(8,128)(2,1)} async-done(((bf16[128,512]{0,1:T(8,128)(2,1)}), bf16[128,512]{0,1:T(8,128)(2,1)}) %all-reduce.2.cloned.1.call-update) | async-done | bytes 131088 | tf_op jit(solution)/shard_map/psum | solution.py:110
  (48 shorter events, 13.9 us)
Async XLA Ops:
  7.2 191.5 %copy-start = (bf16[1,12,16,4096]{3,2,1,0:T(8,128)(2,1)S(1)}, bf16[1,12,16,4096]{3,2,1,0:T(8,128)(2,1)}, u32[]{:S(2)}) copy-start(bf16[1,12,16,4096]{3,2,1,0:T(8,128)(2,1)} %param.13) | copy-start | bytes 4718596
  7.2 108.5 %all-gather.3.cloned.1.call-start = ((), (), s32[]{:S(2)}) async-start(), calls=%async_computation.1 | async-start | bytes 3244032 | tf_op jit(solution)/shard_map/all_gather | solution.py:39
  7.9 190.8 %all-gather.5.cloned.1.call-start = ((), (), s32[]{:S(2)}) async-start(), calls=%async_computation.2 | async-start | bytes 1081344 | tf_op jit(solution)/shard_map/all_gather | solution.py:71
  8.7 371.9 %reduce-scatter.4.cloned.1.call-start = ((), (), s32[]{:S(2)}) async-start(), calls=%async_computation.4 | async-start | bytes 4325376
  118.6 0.6 copy-start.3
  119.3 81.2 %collective-permute-start = (bf16[1,12,2,256]{3,2,1,0:T(2,128)(2,1)S(1)}, bf16[1,12,2,256]{3,2,1,0:T(2,128)(2,1)S(1)}, u32[]{:S(2)}, u32[]{:S(2)}) collective-permute-start(bf16[1,12,2,256]{3,2,1,0:T(2,128)(2,1)S(1)} %get-tuple-element.38), channel_id=1, source_target_pairs={{0,32},{32,64},{64,96},{96,128},{128,160},{160,192},{192,224},{224... | collective-permute-start | bytes 36872 | tf_op jit(solution)/shard_map/ppermute | solution.py:18
  121.5 79.0 %collective-permute-start.1 = (bf16[1,12,2,256]{3,2,1,0:T(2,128)(2,1)S(1)}, bf16[1,12,2,256]{3,2,1,0:T(2,128)(2,1)S(1)}, u32[]{:S(2)}, u32[]{:S(2)}) collective-permute-start(bf16[1,12,2,256]{3,2,1,0:T(2,128)(2,1)S(1)} %get-tuple-element.39), channel_id=1, source_target_pairs={{32,0},{64,32},{96,64},{128,96},{160,128},{192,160},{224,192},{256... | collective-permute-start | bytes 36872 | tf_op jit(solution)/shard_map/ppermute | solution.py:21
  212.1 9.8 %collective-permute-start.2 = (bf16[1,12,2,256]{3,2,1,0:T(2,128)(2,1)S(1)}, bf16[1,12,2,256]{3,2,1,0:T(2,128)(2,1)S(1)}, u32[]{:S(2)}, u32[]{:S(2)}) collective-permute-start(bf16[1,12,2,256]{3,2,1,0:T(2,128)(2,1)S(1)} %get-tuple-element.36), channel_id=1, source_target_pairs={{0,32},{32,64},{64,96},{96,128},{128,160},{160,192},{192,224},{224... | collective-permute-start | bytes 36872 | tf_op jit(solution)/shard_map/ppermute | solution.py:18
  214.7 8.6 %collective-permute-start.3 = (bf16[1,12,2,256]{3,2,1,0:T(2,128)(2,1)S(1)}, bf16[1,12,2,256]{3,2,1,0:T(2,128)(2,1)S(1)}, u32[]{:S(2)}, u32[]{:S(2)}) collective-permute-start(bf16[1,12,2,256]{3,2,1,0:T(2,128)(2,1)S(1)} %get-tuple-element.37), channel_id=1, source_target_pairs={{32,0},{64,32},{96,64},{128,96},{160,128},{192,160},{224,192},{256... | collective-permute-start | bytes 36872 | tf_op jit(solution)/shard_map/ppermute | solution.py:21
  223.4 1.2 copy-start.2
  233.4 1.4 copy-start.1
  233.4 311.5 %all-reduce.2.cloned.1.call-start = ((), (), s32[]{:S(2)}) async-start(), calls=%async_computation.3 | async-start | bytes 262144 | tf_op jit(solution)/shard_map/psum | solution.py:110
Sparse Core Ops, SparseCore 0:
  11.3 104.3 all-gather.2
  118.8 79.8 all-gather.4
  233.5 147.0 reduce-scatter.3
  384.2 160.6 all-reduce.1
where the time goes:
time: 556 us; the launch traced here: 555 us
  waiting for transfers between devices  473 us (85%)
  starting transfers between devices  19.7 us (4%)
  matrix products  18.2 us (3%)
  local copies, waits for them, and re-layouts  16.7 us (3%)
  between operations  14 us (3%)
  other arithmetic  13.5 us (2%)
    psum x1, waiting for transfers between devices, local(): shares = lax.psum(shares.astype(jnp.bfloat16), 'tile').astype(jnp.float32)  159 us
    unnamed x5, waiting for transfers between devices  142 us
    all_gather x1, waiting for transfers between devices, local(): lax.all_gather(w_qkv, 'fsdp', axis=0, tiled=True)  101 us
    all_gather x1, waiting for transfers between devices, local(): lax.all_gather(w_out, 'fsdp', axis=1, tiled=True)  69.7 us
    ppermute x2, starting transfers between devices, extended_2(): lax.ppermute(lax.slice_in_dim(block, 0, width, axis=dim), axis, backward)  14.7 us
  transfers between devices with their start and end apart: 8, of which 5 were waited for; matrix products, arithmetic and copies ran while one was open for 4% of the time, Pallas kernels for 0%

commit v1 on v0

v1 whole, which is shorter than its diff:
```python
import jax
import jax.numpy as jnp
from jax import lax
from jax.sharding import PartitionSpec as P

HALO = 2
EPS = 1e-05
TILE = ("x", "zlo")
FSDP = ("y", "zhi", "core")
GROUPS = 4


def shift_pairs(count, step):
    return [(i, (i + step) % count) for i in range(count)]


def rms_inverse(rows):
    return lax.rsqrt(jnp.mean(rows * rows, axis=-1, keepdims=True) + EPS)


def gather_weights(w_qkv, w_out):
    x = lax.axis_index("x")
    core = lax.axis_index("core")
    head_dim = w_out.shape[0]
    block = jnp.concatenate([w_qkv, w_out.T], axis=1)
    mine = lax.dynamic_slice_in_dim(block, x * head_dim, head_dim, axis=1)
    spread = lax.all_to_all(
        jnp.broadcast_to(mine[None], (16,) + mine.shape), ("y", "zhi"), 0, 0
    )
    parts = [spread] + [
        lax.ppermute(spread, "x", shift_pairs(GROUPS, step)) for step in range(1, GROUPS)
    ]
    others = [lax.ppermute(part, "core", shift_pairs(2, 1)) for part in parts]
    order = (x - jnp.arange(GROUPS)) % GROUPS
    own = jnp.take(jnp.stack(parts), order, axis=0)
    other = jnp.take(jnp.stack(others), order, axis=0)
    both = jnp.stack([jnp.where(core == 0, own, other), jnp.where(core == 0, other, own)])
    return both.transpose(2, 0, 3, 1, 4).reshape(-1, GROUPS * head_dim)


def reduce_grads(grads):
    x = lax.axis_index("x")
    width = grads.shape[1] // GROUPS
    ordered = grads.reshape(16, 2, 128, GROUPS, width).transpose(1, 3, 0, 2, 4)
    pair = lax.all_to_all(ordered, "core", 0, 0)
    chip = (pair[0].astype(jnp.float32) + pair[1].astype(jnp.float32)).astype(jnp.bfloat16)
    total = lax.dynamic_index_in_dim(chip, x, 0, keepdims=False).astype(jnp.float32)
    for step in range(1, GROUPS):
        away = lax.dynamic_index_in_dim(chip, (x + step) % GROUPS, 0, keepdims=False)
        total = total + lax.ppermute(away, "x", shift_pairs(GROUPS, step)).astype(jnp.float32)
    line = total.astype(jnp.bfloat16).reshape(64, 32, width)
    pieces = lax.all_to_all(line, ("y", "zhi", "zlo"), 0, 0)
    piece = jnp.sum(pieces.astype(jnp.float32), axis=0).astype(jnp.bfloat16)
    full = lax.all_to_all(
        jnp.broadcast_to(piece[None], (16,) + piece.shape), TILE, 0, 0
    )
    return full.reshape(GROUPS, 128, width).astype(jnp.float32)


def local(tokens, w_qkv, w_out, band, cotangent):
    samples, lat_rows, lon_cols, features = tokens.shape
    head_dim = w_out.shape[0]
    num_rows = lat_rows * lon_cols
    edge = lat_rows * HALO
    forward = shift_pairs(16, 1)
    backward = shift_pairs(16, -1)
    low = lax.ppermute(tokens[0, :, lon_cols - HALO :], TILE, forward)
    high = lax.ppermute(tokens[0, :, :HALO], TILE, backward)
    weights = gather_weights(w_qkv, w_out)
    rows = jnp.concatenate(
        [
            tokens.reshape(num_rows, features),
            low.reshape(edge, features),
            high.reshape(edge, features),
        ],
        axis=0,
    )
    grad_rows = cotangent.reshape(num_rows, features)
    float_rows = rows.astype(jnp.float32)
    inverse = rms_inverse(float_rows)
    normed = (float_rows * inverse).astype(jnp.bfloat16)
    w_in = weights[:, : 3 * head_dim]
    w_back = weights[:, 3 * head_dim :]
    projected = jnp.dot(normed, w_in, preferred_element_type=jnp.float32).astype(jnp.bfloat16)
    queries = projected[:num_rows, :head_dim]
    keys = projected[:, head_dim : 2 * head_dim]
    values = projected[:, 2 * head_dim :]
    place = jnp.arange(num_rows + 2 * edge)
    column = (place - num_rows) % HALO
    usable = (
        (place < num_rows)
        | ((place < num_rows + edge) & (HALO - column <= band[0, 0]))
        | ((place >= num_rows + edge) & (column + 1 <= band[0, 1]))
    )
    score_scale = head_dim ** (-0.5)
    scores = (
        lax.dot_general(
            queries, keys, (((1,), (1,)), ((), ())), preferred_element_type=jnp.float32
        )
        * score_scale
    )
    scores = jnp.where(usable[None, :], scores, -jnp.inf)
    exp_scores = jnp.exp(scores - jnp.max(scores, axis=-1, keepdims=True))
    probs_full = exp_scores / jnp.sum(exp_scores, axis=-1, keepdims=True)
    probs_low = probs_full.astype(jnp.bfloat16)
    attended = jnp.dot(probs_low, values, preferred_element_type=jnp.float32).astype(jnp.bfloat16)
    d_att = jnp.dot(grad_rows, w_back, preferred_element_type=jnp.float32).astype(jnp.bfloat16)
    d_probs = lax.dot_general(
        d_att, values, (((1,), (1,)), ((), ())), preferred_element_type=jnp.float32
    )
    row_inner = jnp.sum(probs_full * d_probs, axis=-1, keepdims=True)
    d_scores = (probs_full * (d_probs - row_inner) * score_scale).astype(jnp.bfloat16)
    d_query = jnp.dot(d_scores, keys, preferred_element_type=jnp.float32)
    over_rows = (((0,), (0,)), ((), ()))
    d_keys = lax.dot_general(d_scores, queries, over_rows, preferred_element_type=jnp.float32)
    d_values = lax.dot_general(probs_low, d_att, over_rows, preferred_element_type=jnp.float32)
    d_kv = jnp.concatenate([d_keys, d_values], axis=1)
    edges = d_kv[num_rows:].astype(jnp.bfloat16)
    to_left = lax.ppermute(edges[:edge], TILE, backward)
    to_right = lax.ppermute(edges[edge:], TILE, forward)
    d_ext = jnp.concatenate(
        [jnp.pad(d_query, ((0, 2 * edge), (0, 0))), d_kv], axis=1
    ).astype(jnp.bfloat16)
    first_term = lax.dot_general(normed, d_ext, over_rows, preferred_element_type=jnp.float32)
    second_term = lax.dot_general(
        grad_rows, attended, over_rows, preferred_element_type=jnp.float32
    )
    grads = reduce_grads(jnp.concatenate([first_term, second_term], axis=1).astype(jnp.bfloat16))
    own = d_kv[:num_rows].reshape(lat_rows, lon_cols, 2 * head_dim)
    own = own.at[:, lon_cols - HALO :].add(
        to_left.astype(jnp.float32).reshape(lat_rows, HALO, 2 * head_dim)
    )
    own = own.at[:, :HALO].add(
        to_right.astype(jnp.float32).reshape(lat_rows, HALO, 2 * head_dim)
    )
    d_qkv = jnp.concatenate([d_query, own.reshape(num_rows, 2 * head_dim)], axis=1).astype(
        jnp.bfloat16
    )
    d_normed = lax.dot_general(
        d_qkv, w_in, (((1,), (1,)), ((), ())), preferred_element_type=jnp.float32
    )
    own_inverse = inverse[:num_rows]
    own_rows = float_rows[:num_rows]
    d_float = own_inverse * d_normed - own_rows * own_inverse**3 * jnp.mean(
        d_normed * own_rows, axis=-1, keepdims=True
    )
    d_tokens = d_float.astype(jnp.bfloat16).reshape(tokens.shape)
    grad_qkv = jnp.concatenate([grads[0], grads[1], grads[2]], axis=1)
    return (d_tokens, grad_qkv, grads[3].T)


def solution(mesh):
    inner = jax.sharding.Mesh(
        mesh.devices.reshape(4, 4, 8, 2, 2), ("x", "zlo", "y", "zhi", "core")
    )
    placed = (
        P(FSDP, None, TILE, None),
        P(FSDP, None),
        P(None, FSDP),
        P(TILE, None),
        P(FSDP, None, TILE, None),
    )
    return jax.shard_map(
        local,
        mesh=inner,
        in_specs=placed,
        out_specs=(P(FSDP, None, TILE, None), P(FSDP, None), P(None, FSDP)),
        check_vma=False,
    )
```

time: 556 us -> 229 us (0.41)
  the two profiles are of different devices: /device:TPU:8 before, /device:TPU:16 now
where the time goes in v1:
time: 229 us; the launch traced here: 228 us
  starting transfers between devices  71.1 us (31%)
  waiting for transfers between devices  63.2 us (28%)
  local copies, waits for them, and re-layouts  41.6 us (18%)
  other arithmetic  26.8 us (12%)
  matrix products  15.6 us (7%)
  blocking collectives  8.48 us (4%)
    convert_element_type x2, local copies, waits for them, and re-layouts, local(): jnp.concatenate([first_term, second_term], axis=1).astype(jnp.bfloat16)  18.9 us
    all_to_all x1, starting transfers between devices, gather_weights(): lax.all_to_all(jnp.broadcast_to(mine[None], (16,) + mine.shape), ('y', 'z...  15.9 us
    ppermute x3, waiting for transfers between devices, gather_weights(): lax.ppermute(spread, 'x', shift_pairs(GROUPS, step))  14.8 us
    all_to_all x1, waiting for transfers between devices, reduce_grads(): pieces = lax.all_to_all(line, ('y', 'zhi', 'zlo'), 0, 0)  13.7 us
    all_to_all x1, starting transfers between devices, reduce_grads(): pieces = lax.all_to_all(line, ('y', 'zhi', 'zlo'), 0, 0)  11.8 us
    ppermute x3, waiting for transfers between devices, reduce_grads(): lax.ppermute(away, 'x', shift_pairs(GROUPS, step)).astype(jnp.float32)  10.9 us
    ppermute x3, starting transfers between devices, reduce_grads(): lax.ppermute(away, 'x', shift_pairs(GROUPS, step)).astype(jnp.float32)  9.16 us
    ppermute x3, starting transfers between devices, gather_weights(): lax.ppermute(spread, 'x', shift_pairs(GROUPS, step))  8.7 us
  transfers between devices with their start and end apart: 17, of which 10 were waited for; matrix products, arithmetic and copies ran while one was open for 12% of the time, Pallas kernels for 0%

profile of v1, /device:TPU:16, one launch (start us, length us, event | category | flops | bytes accessed | tf_op | source)
XLA Modules:
  0.0 227.9 jit_solution(6693497036928883992)
XLA Ops:
  3.4 15.9 %all-to-all-start = ((bf16[16,128,128]{2,1,0:T(8,128)(2,1)}), bf16[16,128,128]{2,1,0:T(8,128)(2,1)}, u32[]{:S(2)}, u32[]{:S(2)}) async-start(bf16[16,128,128]{2,1,0:T(8,128)(2,1)} %broadcast_in_dim.26), calls=%async_computation | async-start | bytes 1048576 | tf_op jit(solution)/shard_map/all_to_all | solution.py:27
  21.7 6.6 %collective-permute-start.1 = (bf16[12,2,4096]{2,1,0:T(2,128)(2,1)S(1)}, bf16[12,2,4096]{2,1,0:T(2,128)(2,1)S(1)}, u32[]{:S(2)}, u32[]{:S(2)}) collective-permute-start(bf16[12,2,4096]{2,1,0:T(2,128)(2,1)S(1)} %get-tuple-element.40), channel_id=1, source_target_pairs={{0,480},{32,0},{64,32},{96,64},{128,96},{160,128},{192,160},{224,1... | collective-permute-start | bytes 589832 | tf_op jit(solution)/shard_map/ppermute | solution.py:68
  33.5 7.1 %collective-permute-done.1 = bf16[12,2,4096]{2,1,0:T(2,128)(2,1)S(1)} collective-permute-done((bf16[12,2,4096]{2,1,0:T(2,128)(2,1)S(1)}, bf16[12,2,4096]{2,1,0:T(2,128)(2,1)S(1)}, u32[]{:S(2)}, u32[]{:S(2)}) %collective-permute-start.1) | collective-permute-done | bytes 196640 | tf_op jit(solution)/shard_map/ppermute | solution.py:68
  40.6 6.3 %collective-permute-done = bf16[12,2,4096]{2,1,0:T(2,128)(2,1)} collective-permute-done((bf16[12,2,4096]{2,1,0:T(2,128)(2,1)}, bf16[12,2,4096]{2,1,0:T(2,128)(2,1)}, u32[]{:S(2)}, u32[]{:S(2)}) %collective-permute-start) | collective-permute-done | bytes 196640 | tf_op jit(solution)/shard_map/ppermute | solution.py:67
  48.0 3.5 %collective-permute-start.4 = (bf16[16,128,128]{2,1,0:T(8,128)(2,1)}, bf16[16,128,128]{2,1,0:T(8,128)(2,1)}, u32[]{:S(2)}, u32[]{:S(2)}) collective-permute-start(bf16[16,128,128]{2,1,0:T(8,128)(2,1)} %all-to-all-done), channel_id=1, source_target_pairs={{0,384},{128,0},{256,128},{384,256},{1,385},{129,1},{257,129},{385... | collective-permute-start | bytes 1572872 | tf_op jit(solution)/shard_map/ppermute | solution.py:31
  60.9 4.1 %collective-permute-done.4 = bf16[16,128,128]{2,1,0:T(8,128)(2,1)} collective-permute-done((bf16[16,128,128]{2,1,0:T(8,128)(2,1)}, bf16[16,128,128]{2,1,0:T(8,128)(2,1)}, u32[]{:S(2)}, u32[]{:S(2)}) %collective-permute-start.4) | collective-permute-done | bytes 524320 | tf_op jit(solution)/shard_map/ppermute | solution.py:31
  72.0 7.6 %collective-permute-done.2 = bf16[16,128,128]{2,1,0:T(8,128)(2,1)} collective-permute-done((bf16[16,128,128]{2,1,0:T(8,128)(2,1)}, bf16[16,128,128]{2,1,0:T(8,128)(2,1)}, u32[]{:S(2)}, u32[]{:S(2)}) %collective-permute-start.2) | collective-permute-done | bytes 524320 | tf_op jit(solution)/shard_map/ppermute | solution.py:31
  85.1 3.7 %gather_fusion = bf16[4,16,128,128]{3,2,1,0:T(8,128)(2,1)} fusion(bf16[4,16,128,128]{3,2,1,0:T(8,128)(2,1)} %pad_maximum_fusion.1, s32[1024]{0:T(1024)S(1)} %pad_clamp_fusion), kind=kCustom, calls=%fused_computation.clone | custom fusion | bytes 4194320 | tf_op jit(solution)/shard_map/jit(_take)/gather | solution.py:35
  92.0 3.8 %gather_fusion.1 = bf16[4,16,128,128]{3,2,1,0:T(8,128)(2,1)} fusion(bf16[4,16,128,128]{3,2,1,0:T(8,128)(2,1)} %pad_maximum_fusion.2, s32[1024]{0:T(1024)S(1)} %pad_clamp_fusion), kind=kCustom, calls=%fused_computation.1.clone | custom fusion | bytes 4194320 | tf_op jit(solution)/shard_map/jit(_take)/gather | solution.py:36
  98.8 4.0 %copy.17 = bf16[16,2,128,4,128]{4,3,2,1,0:T(4,128)(2,1)S(1)} copy(bf16[16,2,128,4,128]{4,2,0,3,1:T(8,128)(2,1)S(1)} %maximum_bitcast_fusion) | data formatting | bytes 8388608 | tf_op jit(solution)/shard_map/transpose | solution.py:38
  116.7 7.8 %convert_element_type.82 = bf16[16,2,128,4,128]{2,1,0,4,3:T(2,128)(2,1)} reshape(bf16[4096,512]{0,1:T(8,128)(2,1)} %pad_maximum_fusion) | data formatting | bytes 8388608 | tf_op jit(solution)/shard_map/convert_element_type | solution.py:128
  124.4 11.2 %copy.18 = bf16[16,2,128,4,128]{4,2,0,3,1:T(8,128)(2,1)} copy(bf16[16,2,128,4,128]{2,1,0,4,3:T(2,128)(2,1)} %convert_element_type.82) | data formatting | bytes 8388608 | tf_op jit(solution)/shard_map/convert_element_type | solution.py:128
  135.6 8.5 %all_to_all.20 = bf16[2,4,16,128,128]{4,3,2,1,0:T(8,128)(2,1)S(1)} all-to-all(bf16[2,4,16,128,128]{4,3,2,1,0:T(8,128)(2,1)} %bitcast.64), channel_id=1, replica_groups=mesh['x'=4,'zlo'=4,'y'=8,'zhi'=2,'core'=2] {'core'}, dimensions={0} | all-to-all | bytes 8388608 | tf_op jit(solution)/shard_map/all_to_all | solution.py:45
  146.7 4.5 %collective-permute-start.13 = (bf16[16,128,128]{2,1,0:T(8,128)(2,1)S(1)}, bf16[16,128,128]{2,1,0:T(8,128)(2,1)S(1)}, u32[]{:S(2)}, u32[]{:S(2)}) collective-permute-start(bf16[16,128,128]{2,1,0:T(8,128)(2,1)S(1)} %get-tuple-element.37), channel_id=1, source_target_pairs={{0,384},{128,0},{256,128},{384,256},{1,385},{129,1},{257,129},{385... | collective-permute-start | bytes 1572872 | tf_op jit(solution)/shard_map/ppermute | solution.py:50
  156.0 3.4 %collective-permute-start.9 = (bf16[24,256]{1,0:T(8,128)(2,1)S(1)}, bf16[24,256]{1,0:T(8,128)(2,1)S(1)}, u32[]{:S(2)}, u32[]{:S(2)}) collective-permute-start(bf16[24,256]{1,0:T(8,128)(2,1)S(1)} %get-tuple-element.46), channel_id=1, source_target_pairs={{0,480},{32,0},{64,32},{96,64},{128,96},{160,128},{192,160},{224,1... | collective-permute-start | bytes 36872 | tf_op jit(solution)/shard_map/ppermute | solution.py:119
  161.9 7.0 %collective-permute-done.10 = bf16[24,256]{1,0:T(8,128)(2,1)S(1)} collective-permute-done((bf16[24,256]{1,0:T(8,128)(2,1)S(1)}, bf16[24,256]{1,0:T(8,128)(2,1)S(1)}, u32[]{:S(2)}, u32[]{:S(2)}) %collective-permute-start.10) | collective-permute-done | bytes 12320 | tf_op jit(solution)/shard_map/ppermute | solution.py:120
  168.9 5.0 %collective-permute-done.13 = bf16[16,128,128]{2,1,0:T(8,128)(2,1)S(1)} collective-permute-done((bf16[16,128,128]{2,1,0:T(8,128)(2,1)S(1)}, bf16[16,128,128]{2,1,0:T(8,128)(2,1)S(1)}, u32[]{:S(2)}, u32[]{:S(2)}) %collective-permute-start.13) | collective-permute-done | bytes 524320 | tf_op jit(solution)/shard_map/ppermute | solution.py:50
  173.9 6.0 %collective-permute-done.11 = bf16[16,128,128]{2,1,0:T(8,128)(2,1)} collective-permute-done((bf16[16,128,128]{2,1,0:T(8,128)(2,1)S(1)}, bf16[16,128,128]{2,1,0:T(8,128)(2,1)}, u32[]{:S(2)}, u32[]{:S(2)}) %collective-permute-start.11) | collective-permute-done | bytes 524320 | tf_op jit(solution)/shard_map/ppermute | solution.py:50
  182.4 11.8 %all-to-all-start.2 = ((bf16[64,32,128]{2,1,0:T(8,128)(2,1)}), bf16[64,32,128]{2,1,0:T(8,128)(2,1)S(1)}, u32[]{:S(2)}, u32[]{:S(2)}) async-start(bf16[64,32,128]{2,1,0:T(8,128)(2,1)} %bitcast.29), calls=%async_computation.2 | async-start | bytes 1048576 | tf_op jit(solution)/shard_map/all_to_all | solution.py:52
  194.3 5.8 %multiply_reduce_fusion.1 = (f32[192]{0:T(256)S(1)}, f32[192,4096]{1,0:T(8,128)}) fusion(f32[240,4096]{1,0:T(8,128)} %maximum_convert_fusion, bf16[4096,512]{1,0:T(8,128)(2,1)} %bitcast.67, bf16[192,256]{1,0:T(8,128)(2,1)S(1)} %bitcast.74, bf16[192,128]{1,0:T(8,128)(2,1)S(1)} %copy-done.10), kind=kOutput, calls=%fused_computation.12 | convolution fusion | flops 605847360 | bytes 9585408 | tf_op jit(solution)/shard_map/dot_general | solution.py:139
  200.1 13.7 %all-to-all-done.2 = bf16[64,32,128]{2,1,0:T(8,128)(2,1)S(1)} async-done(((bf16[64,32,128]{2,1,0:T(8,128)(2,1)}), bf16[64,32,128]{2,1,0:T(8,128)(2,1)S(1)}, u32[]{:S(2)}, u32[]{:S(2)}) %all-to-all-start.2) | async-done | bytes 524320 | tf_op jit(solution)/shard_map/all_to_all | solution.py:52
  214.6 3.5 %all-to-all-start.3 = ((bf16[16,32,128]{2,1,0:T(8,128)(2,1)}), bf16[16,32,128]{2,1,0:T(8,128)(2,1)S(1)}, u32[]{:S(2)}, u32[]{:S(2)}) async-start(bf16[16,32,128]{2,1,0:T(8,128)(2,1)} %broadcast_in_dim.42), calls=%async_computation.3 | async-start | bytes 262144 | tf_op jit(solution)/shard_map/all_to_all | solution.py:54
  218.1 5.0 %subtract_convert_fusion = bf16[192,4096]{1,0:T(8,128)(2,1)} fusion(f32[192,4096]{1,0:T(8,128)} %get-tuple-element.54, f32[240,4096]{1,0:T(8,128)} %maximum_convert_fusion, f32[192]{0:T(256)S(1)} %broadcast_multiply_fusion, f32[192]{0:T(256)S(1)} %bitcast.82, f32[192]{0:T(256)S(1)} %bitcast.81), kind=kLoop, calls=%fused_computation.11 | loop fusion | flops 3932160 | bytes 7866624 | tf_op jit(solution)/shard_map/convert_element_type | solution.py:147
  223.1 3.3 %all-to-all-done.3 = bf16[16,32,128]{2,1,0:T(8,128)(2,1)S(1)} async-done(((bf16[16,32,128]{2,1,0:T(8,128)(2,1)}), bf16[16,32,128]{2,1,0:T(8,128)(2,1)S(1)}, u32[]{:S(2)}, u32[]{:S(2)}) %all-to-all-start.3) | async-done | bytes 131104 | tf_op jit(solution)/shard_map/all_to_all | solution.py:54
  (91 shorter events, 67.7 us)
Async XLA Ops:
  0.6 104.1 %copy-start = (bf16[1,12,16,4096]{3,2,1,0:T(8,128)(2,1)S(1)}, bf16[1,12,16,4096]{3,2,1,0:T(8,128)(2,1)}, u32[]{:S(2)}) copy-start(bf16[1,12,16,4096]{3,2,1,0:T(8,128)(2,1)} %param.15) | copy-start | bytes 4718596
  0.6 56.1 %copy-start.4 = (bf16[1,12,16,4096]{3,2,1,0:T(8,128)(2,1)S(1)}, bf16[1,12,16,4096]{3,2,1,0:T(8,128)(2,1)}, u32[]{:S(2)}) copy-start(bf16[1,12,16,4096]{3,2,1,0:T(8,128)(2,1)} %param.11) | copy-start | bytes 4718596
  3.4 44.6 %all-to-all-start = ((bf16[16,128,128]{2,1,0:T(8,128)(2,1)}), bf16[16,128,128]{2,1,0:T(8,128)(2,1)}, u32[]{:S(2)}, u32[]{:S(2)}) async-start(bf16[16,128,128]{2,1,0:T(8,128)(2,1)} %broadcast_in_dim.26), calls=%async_computation | async-start | bytes 1048576 | tf_op jit(solution)/shard_map/all_to_all | solution.py:27
  21.7 18.8 %collective-permute-start.1 = (bf16[12,2,4096]{2,1,0:T(2,128)(2,1)S(1)}, bf16[12,2,4096]{2,1,0:T(2,128)(2,1)S(1)}, u32[]{:S(2)}, u32[]{:S(2)}) collective-permute-start(bf16[12,2,4096]{2,1,0:T(2,128)(2,1)S(1)} %get-tuple-element.40), channel_id=1, source_target_pairs={{0,480},{32,0},{64,32},{96,64},{128,96},{160,128},{192,160},{224,1... | collective-permute-start | bytes 589832 | tf_op jit(solution)/shard_map/ppermute | solution.py:68
  28.4 18.6 %collective-permute-start = (bf16[12,2,4096]{2,1,0:T(2,128)(2,1)}, bf16[12,2,4096]{2,1,0:T(2,128)(2,1)}, u32[]{:S(2)}, u32[]{:S(2)}) collective-permute-start(bf16[12,2,4096]{2,1,0:T(2,128)(2,1)} %get-tuple-element.39), channel_id=1, source_target_pairs={{0,32},{32,64},{64,96},{96,128},{128,160},{160,192},{192,224},{224... | collective-permute-start | bytes 589832 | tf_op jit(solution)/shard_map/ppermute | solution.py:67
  48.0 55.5 %copy-start.6 = (bf16[24,4096]{1,0:T(8,128)(2,1)}, bf16[24,4096]{1,0:T(8,128)(2,1)S(1)}, u32[]{:S(2)}) copy-start(bf16[24,4096]{1,0:T(8,128)(2,1)S(1)} %reshape.197) | copy-start | bytes 589828
  48.0 17.0 %collective-permute-start.4 = (bf16[16,128,128]{2,1,0:T(8,128)(2,1)}, bf16[16,128,128]{2,1,0:T(8,128)(2,1)}, u32[]{:S(2)}, u32[]{:S(2)}) collective-permute-start(bf16[16,128,128]{2,1,0:T(8,128)(2,1)} %all-to-all-done), channel_id=1, source_target_pairs={{0,384},{128,0},{256,128},{384,256},{1,385},{129,1},{257,129},{385... | collective-permute-start | bytes 1572872 | tf_op jit(solution)/shard_map/ppermute | solution.py:31
  51.5 18.6 %collective-permute-start.3 = (bf16[16,128,128]{2,1,0:T(8,128)(2,1)}, bf16[16,128,128]{2,1,0:T(8,128)(2,1)}, u32[]{:S(2)}, u32[]{:S(2)}) collective-permute-start(bf16[16,128,128]{2,1,0:T(8,128)(2,1)} %all-to-all-done), channel_id=1, source_target_pairs={{0,256},{128,384},{256,0},{384,128},{1,257},{129,385},{257,1},{385... | collective-permute-start | bytes 1572872 | tf_op jit(solution)/shard_map/ppermute | solution.py:31
  53.9 25.7 %collective-permute-start.2 = (bf16[16,128,128]{2,1,0:T(8,128)(2,1)}, bf16[16,128,128]{2,1,0:T(8,128)(2,1)}, u32[]{:S(2)}, u32[]{:S(2)}) collective-permute-start(bf16[16,128,128]{2,1,0:T(8,128)(2,1)} %all-to-all-done), channel_id=1, source_target_pairs={{0,128},{128,256},{256,384},{384,0},{1,129},{129,257},{257,385},{3... | collective-permute-start | bytes 1572872 | tf_op jit(solution)/shard_map/ppermute | solution.py:31
  59.0 29.8 %collective-permute-start.5 = (bf16[16,128,128]{2,1,0:T(8,128)(2,1)}, bf16[16,128,128]{2,1,0:T(8,128)(2,1)}, u32[]{:S(2)}, u32[]{:S(2)}) collective-permute-start(bf16[16,128,128]{2,1,0:T(8,128)(2,1)} %all-to-all-done), channel_id=1, source_target_pairs={{0,1},{1,0},{2,3},{3,2},{4,5},{5,4},{6,7},{7,6},{8,9},{9,8},{10,11... | collective-permute-start | bytes 1572872 | tf_op jit(solution)/shard_map/ppermute | solution.py:33
  65.0 23.8 %collective-permute-start.8 = (bf16[16,128,128]{2,1,0:T(8,128)(2,1)}, bf16[16,128,128]{2,1,0:T(8,128)(2,1)}, u32[]{:S(2)}, u32[]{:S(2)}) collective-permute-start(bf16[16,128,128]{2,1,0:T(8,128)(2,1)} %collective-permute-done.4), channel_id=1, source_target_pairs={{0,1},{1,0},{2,3},{3,2},{4,5},{5,4},{6,7},{7,6},{8,9},{9,8},{10,11... | collective-permute-start | bytes 1572872 | tf_op jit(solution)/shard_map/ppermute | solution.py:33
  70.1 18.8 %collective-permute-start.7 = (bf16[16,128,128]{2,1,0:T(8,128)(2,1)}, bf16[16,128,128]{2,1,0:T(8,128)(2,1)}, u32[]{:S(2)}, u32[]{:S(2)}) collective-permute-start(bf16[16,128,128]{2,1,0:T(8,128)(2,1)} %collective-permute-done.3), channel_id=1, source_target_pairs={{0,1},{1,0},{2,3},{3,2},{4,5},{5,4},{6,7},{7,6},{8,9},{9,8},{10,11... | collective-permute-start | bytes 1572872 | tf_op jit(solution)/shard_map/ppermute | solution.py:33
  79.6 9.2 %collective-permute-start.6 = (bf16[16,128,128]{2,1,0:T(8,128)(2,1)}, bf16[16,128,128]{2,1,0:T(8,128)(2,1)}, u32[]{:S(2)}, u32[]{:S(2)}) collective-permute-start(bf16[16,128,128]{2,1,0:T(8,128)(2,1)} %collective-permute-done.2), channel_id=1, source_target_pairs={{0,1},{1,0},{2,3},{3,2},{4,5},{5,4},{6,7},{7,6},{8,9},{9,8},{10,11... | collective-permute-start | bytes 1572872 | tf_op jit(solution)/shard_map/ppermute | solution.py:33
  146.5 9.4 %copy-start.7 = (f32[240,128]{1,0:T(8,128)S(1)}, f32[240,128]{1,0:T(8,128)}, u32[]{:S(2)}) copy-start(f32[240,128]{1,0:T(8,128)} %get-tuple-element.58) | copy-start | bytes 368644
  146.5 9.4 %copy-start.8 = (f32[240,128]{1,0:T(8,128)S(1)}, f32[240,128]{1,0:T(8,128)}, u32[]{:S(2)}) copy-start(f32[240,128]{1,0:T(8,128)} %get-tuple-element.56) | copy-start | bytes 368644
  146.7 47.6 %copy-start.10 = (bf16[192,128]{1,0:T(8,128)(2,1)S(1)}, bf16[192,128]{1,0:T(8,128)(2,1)}, u32[]{:S(2)}) copy-start(bf16[192,128]{1,0:T(8,128)(2,1)} %convolution_convert_fusion.3) | copy-start | bytes 147460
  146.7 27.2 %collective-permute-start.13 = (bf16[16,128,128]{2,1,0:T(8,128)(2,1)S(1)}, bf16[16,128,128]{2,1,0:T(8,128)(2,1)S(1)}, u32[]{:S(2)}, u32[]{:S(2)}) collective-permute-start(bf16[16,128,128]{2,1,0:T(8,128)(2,1)S(1)} %get-tuple-element.37), channel_id=1, source_target_pairs={{0,384},{128,0},{256,128},{384,256},{1,385},{129,1},{257,129},{385... | collective-permute-start | bytes 1572872 | tf_op jit(solution)/shard_map/ppermute | solution.py:50
  151.2 22.7 %collective-permute-start.12 = (bf16[16,128,128]{2,1,0:T(8,128)(2,1)S(1)}, bf16[16,128,128]{2,1,0:T(8,128)(2,1)}, u32[]{:S(2)}, u32[]{:S(2)}) collective-permute-start(bf16[16,128,128]{2,1,0:T(8,128)(2,1)S(1)} %get-tuple-element.38), channel_id=1, source_target_pairs={{0,256},{128,384},{256,0},{384,128},{1,257},{129,385},{257,1},{385... | collective-permute-start | bytes 1572872 | tf_op jit(solution)/shard_map/ppermute | solution.py:50
  153.1 26.8 %collective-permute-start.11 = (bf16[16,128,128]{2,1,0:T(8,128)(2,1)S(1)}, bf16[16,128,128]{2,1,0:T(8,128)(2,1)}, u32[]{:S(2)}, u32[]{:S(2)}) collective-permute-start(bf16[16,128,128]{2,1,0:T(8,128)(2,1)S(1)} %get-tuple-element.36), channel_id=1, source_target_pairs={{0,128},{128,256},{256,384},{384,0},{1,129},{129,257},{257,385},{3... | collective-permute-start | bytes 1572872 | tf_op jit(solution)/shard_map/ppermute | solution.py:50
  156.0 5.9 %collective-permute-start.9 = (bf16[24,256]{1,0:T(8,128)(2,1)S(1)}, bf16[24,256]{1,0:T(8,128)(2,1)S(1)}, u32[]{:S(2)}, u32[]{:S(2)}) collective-permute-start(bf16[24,256]{1,0:T(8,128)(2,1)S(1)} %get-tuple-element.46), channel_id=1, source_target_pairs={{0,480},{32,0},{64,32},{96,64},{128,96},{160,128},{192,160},{224,1... | collective-permute-start | bytes 36872 | tf_op jit(solution)/shard_map/ppermute | solution.py:119
  159.4 9.6 %collective-permute-start.10 = (bf16[24,256]{1,0:T(8,128)(2,1)S(1)}, bf16[24,256]{1,0:T(8,128)(2,1)S(1)}, u32[]{:S(2)}, u32[]{:S(2)}) collective-permute-start(bf16[24,256]{1,0:T(8,128)(2,1)S(1)} %get-tuple-element.45), channel_id=1, source_target_pairs={{0,32},{32,64},{64,96},{96,128},{128,160},{160,192},{192,224},{224... | collective-permute-start | bytes 36872 | tf_op jit(solution)/shard_map/ppermute | solution.py:120
  182.4 31.4 %all-to-all-start.2 = ((bf16[64,32,128]{2,1,0:T(8,128)(2,1)}), bf16[64,32,128]{2,1,0:T(8,128)(2,1)S(1)}, u32[]{:S(2)}, u32[]{:S(2)}) async-start(bf16[64,32,128]{2,1,0:T(8,128)(2,1)} %bitcast.29), calls=%async_computation.2 | async-start | bytes 1048576 | tf_op jit(solution)/shard_map/all_to_all | solution.py:52
  214.6 11.9 %all-to-all-start.3 = ((bf16[16,32,128]{2,1,0:T(8,128)(2,1)}), bf16[16,32,128]{2,1,0:T(8,128)(2,1)S(1)}, u32[]{:S(2)}, u32[]{:S(2)}) async-start(bf16[16,32,128]{2,1,0:T(8,128)(2,1)} %broadcast_in_dim.42), calls=%async_computation.3 | async-start | bytes 262144 | tf_op jit(solution)/shard_map/all_to_all | solution.py:54
  218.1 9.8 %copy-start.1 = (bf16[1,12,16,4096]{3,2,1,0:T(8,128)(2,1)S(1)}, bf16[1,12,16,4096]{3,2,1,0:T(8,128)(2,1)}, u32[]{:S(2)}) copy-start(bf16[1,12,16,4096]{3,2,1,0:T(8,128)(2,1)} %param.15) | copy-start | bytes 4718596
  (5 other events, 13.4 us)

commit v2 on v1

v2 whole, which is shorter than its diff:
```python
import functools

import jax
import jax.numpy as jnp
from jax import lax
from jax.experimental import pallas as pl
from jax.experimental.pallas import tpu as pltpu
from jax.sharding import PartitionSpec as P

HALO = 2
EPS = 1e-05
TILE = ("x", "zlo")
FSDP = ("y", "zhi", "core")
GROUPS = 4
HD = 128
ROWS = 192
EDGE = 24
EXT = ROWS + 2 * EDGE
BLOCKS = 16
CHUNK = 4
VMEM_BYTES = 40 * 1024 * 1024
OVER_ROWS = (((0,), (0,)), ((), ()))
OVER_COLS = (((1,), (1,)), ((), ()))
F32 = jnp.float32
BF16 = jnp.bfloat16


def shift_pairs(count, step):
    return [(i, (i + step) % count) for i in range(count)]


def dot(a, b, dims=(((1,), (0,)), ((), ()))):
    return lax.dot_general(a, b, dims, preferred_element_type=F32)


def feature_block(block, core):
    return pl.ds(pl.multiple_of((2 * block + core) * HD, HD), HD)


def features_of(ref, first, core):
    return jnp.concatenate(
        [ref[:, feature_block(block, core)] for block in range(first, first + CHUNK)], axis=1
    )


def project(rows_ref, own_ref, other_ref, core):
    total = jnp.zeros((rows_ref.shape[0], HD), F32)
    for part, side in ((own_ref, core), (other_ref, 1 - core)):
        for first in range(0, BLOCKS, CHUNK):
            weights = part[first : first + CHUNK].reshape(CHUNK * HD, HD)
            total = total + dot(features_of(rows_ref, first, side), weights)
    return total.astype(BF16)


def store_grads(out_ref, left_qkv, left_out, normed_ref, cot_ref, x, side):
    for first in range(0, BLOCKS, CHUNK):
        qkv = dot(left_qkv, features_of(normed_ref, first, side)).astype(BF16)
        out = dot(left_out, features_of(cot_ref, first, side)).astype(BF16)
        for group in range(GROUPS):
            slot = (group - x + GROUPS) % GROUPS
            for block in range(CHUNK):
                columns = slice(block * HD, (block + 1) * HD)
                if group < 3:
                    value = qkv[group * HD : (group + 1) * HD, columns]
                else:
                    value = out[:, columns]
                out_ref[slot, first + block] = value


def attention_kernel(
    place_ref, band_ref, normed_ref, cot_ref, *refs
):
    own = refs[:GROUPS]
    other = refs[GROUPS : 2 * GROUPS]
    away_ref, left_qkv_ref, left_out_ref, own_grads_ref, edges_ref, proj, datt = refs[2 * GROUPS :]
    x = place_ref[0]
    core = place_ref[1]
    for step in range(GROUPS):
        group = (x - step + GROUPS) % GROUPS

        @pl.when(group == 3)
        def _():
            datt[...] = project(cot_ref, own[step], other[step], core)

        @pl.when(group != 3)
        def _():
            proj[group] = project(normed_ref, own[step], other[step], core)

    queries = proj[0][:ROWS]
    keys = proj[1]
    values = proj[2]
    d_att = datt[...]
    place = lax.broadcasted_iota(jnp.int32, (1, EXT), 1)
    column = (place - ROWS) % HALO
    usable = (
        (place < ROWS)
        | ((place < ROWS + EDGE) & (HALO - column <= band_ref[0, 0]))
        | ((place >= ROWS + EDGE) & (column + 1 <= band_ref[0, 1]))
    )
    scale = HD ** (-0.5)
    scores = jnp.where(usable, dot(queries, keys, OVER_COLS) * scale, -jnp.inf)
    exp_scores = jnp.exp(scores - jnp.max(scores, axis=-1, keepdims=True))
    probs = exp_scores / jnp.sum(exp_scores, axis=-1, keepdims=True)
    probs_low = probs.astype(BF16)
    attended = dot(probs_low, values).astype(BF16)
    d_probs = dot(d_att, values, OVER_COLS)
    inner = jnp.sum(probs * d_probs, axis=-1, keepdims=True)
    d_scores = (probs * (d_probs - inner) * scale).astype(BF16)
    d_query = dot(d_scores, keys)
    d_keys = dot(d_scores, queries, OVER_ROWS)
    d_values = dot(probs_low, d_att, OVER_ROWS)
    own_grads_ref[:, :HD] = d_query
    own_grads_ref[:, HD : 2 * HD] = d_keys[:ROWS]
    own_grads_ref[:, 2 * HD :] = d_values[:ROWS]
    edges_ref[:, :HD] = d_keys[ROWS:].astype(BF16)
    edges_ref[:, HD:] = d_values[ROWS:].astype(BF16)
    d_query_ext = jnp.concatenate([d_query, jnp.zeros((2 * EDGE, HD), F32)], axis=0)
    left_qkv = jnp.concatenate([d_query_ext.T, d_keys.T, d_values.T], axis=0).astype(BF16)
    left_out = attended.astype(F32).T.astype(BF16)
    left_qkv_ref[...] = left_qkv
    left_out_ref[...] = left_out
    store_grads(away_ref, left_qkv, left_out, normed_ref, cot_ref, x, 1 - core)


def own_half_kernel(place_ref, left_qkv_ref, left_out_ref, normed_ref, cot_ref, out_ref):
    store_grads(
        out_ref,
        left_qkv_ref[...],
        left_out_ref[...],
        normed_ref,
        cot_ref,
        place_ref[0],
        place_ref[1],
    )


def tokens_kernel(place_ref, d_qkv_ref, tokens_ref, inverse_ref, *refs):
    own = refs[:GROUPS]
    other = refs[GROUPS : 2 * GROUPS]
    out_ref, d_normed = refs[2 * GROUPS :]
    x = place_ref[0]
    core = place_ref[1]
    left = jnp.concatenate(
        [d_qkv_ref[(x - step + GROUPS) % GROUPS] for step in range(GROUPS)], axis=1
    )
    total = jnp.zeros((ROWS, HD), F32)
    for parts, side in ((own, core), (other, 1 - core)):
        for block in range(BLOCKS):
            weights = jnp.concatenate([part[block] for part in parts], axis=1)
            piece = dot(left, weights, OVER_COLS)
            columns = feature_block(block, side)
            d_normed[:, columns] = piece
            total = total + piece * tokens_ref[:, columns].astype(F32)
    inverse = inverse_ref[...]
    mean = jnp.sum(total, axis=-1, keepdims=True) * (1.0 / (2 * BLOCKS * HD))
    factor = inverse * inverse * inverse * mean
    for block in range(2 * BLOCKS):
        columns = slice(block * HD, (block + 1) * HD)
        out_ref[:, columns] = (
            inverse * d_normed[:, columns] - tokens_ref[:, columns].astype(F32) * factor
        ).astype(BF16)


def call(body, operands, outs, scratch, flops, in_bytes, smem):
    whole = pl.BlockSpec(memory_space=pltpu.VMEM)
    scalars = pl.BlockSpec(memory_space=pltpu.SMEM)
    return pl.pallas_call(
        body,
        in_specs=[scalars] * smem + [whole] * (len(operands) - smem),
        out_specs=[whole] * len(outs),
        out_shape=[jax.ShapeDtypeStruct(shape, dtype) for shape, dtype in outs],
        scratch_shapes=[pltpu.VMEM(shape, dtype) for shape, dtype in scratch],
        compiler_params=pltpu.CompilerParams(vmem_limit_bytes=VMEM_BYTES),
        cost_estimate=pl.CostEstimate(
            flops=flops, bytes_accessed=in_bytes, transcendentals=0
        ),
    )(*operands)


def gather_weights(w_qkv, w_out, x):
    block = jnp.concatenate([w_qkv, w_out.T], axis=1)
    mine = lax.dynamic_slice_in_dim(block, x * HD, HD, axis=1)
    spread = lax.all_to_all(
        jnp.broadcast_to(mine[None], (BLOCKS,) + mine.shape), ("y", "zhi"), 0, 0
    )
    own = [spread] + [
        lax.ppermute(spread, "x", shift_pairs(GROUPS, step)) for step in range(1, GROUPS)
    ]
    other = [lax.ppermute(part, "core", shift_pairs(2, 1)) for part in own]
    return own, other


def local(tokens, w_qkv, w_out, band, cotangent):
    samples, lat_rows, lon_cols, features = tokens.shape
    x = lax.axis_index("x")
    core = lax.axis_index("core")
    place = jnp.stack([x, core]).astype(jnp.int32)
    forward = shift_pairs(16, 1)
    backward = shift_pairs(16, -1)
    own, other = gather_weights(w_qkv, w_out, x)
    tok_rows = tokens.reshape(ROWS, features)
    cot_rows = cotangent.reshape(ROWS, features)
    halo_in, unused = lax.optimization_barrier((tokens[0], own[0]))
    low = lax.ppermute(halo_in[:, lon_cols - HALO :], TILE, forward)
    high = lax.ppermute(halo_in[:, :HALO], TILE, backward)

    def normalise(rows):
        rows = rows.astype(F32)
        inverse = lax.rsqrt(jnp.mean(rows * rows, axis=-1, keepdims=True) + EPS)
        return (rows * inverse).astype(BF16), inverse

    normed_own, inverse = normalise(tok_rows)
    normed_low, unused = normalise(low.reshape(EDGE, features))
    normed_high, unused = normalise(high.reshape(EDGE, features))
    normed = jnp.concatenate([normed_own, normed_low, normed_high], axis=0)

    grad_shape = ((GROUPS, BLOCKS, HD, HD), BF16)
    away, left_qkv, left_out, own_grads, edges = call(
        attention_kernel,
        [place, band, normed, cot_rows, *own, *other],
        [
            grad_shape,
            ((3 * HD, EXT), BF16),
            ((HD, ROWS), BF16),
            ((ROWS, 3 * HD), F32),
            ((2 * EDGE, 2 * HD), BF16),
        ],
        [((3, EXT, HD), BF16), ((ROWS, HD), BF16)],
        3_000_000_000,
        12_000_000,
        2,
    )
    received = lax.ppermute(away, "core", shift_pairs(2, 1))
    (kept,) = call(
        own_half_kernel,
        [place, left_qkv, left_out, normed, cot_rows],
        [grad_shape],
        [],
        500_000_000,
        6_000_000,
        1,
    )
    chip = [
        (kept[step].astype(F32) + received[step].astype(F32)).astype(BF16)
        for step in range(GROUPS)
    ]
    total = chip[0].astype(F32)
    for step in range(1, GROUPS):
        total = total + lax.ppermute(chip[step], "x", shift_pairs(GROUPS, step)).astype(F32)
    line = total.astype(BF16)
    line, edges = lax.optimization_barrier((line, edges))
    pieces = lax.all_to_all(line.reshape(64, 32, HD), ("y", "zhi", "zlo"), 0, 0)
    piece = jnp.sum(pieces.astype(F32), axis=0).astype(BF16)
    full = lax.all_to_all(jnp.broadcast_to(piece[None], (16,) + piece.shape), TILE, 0, 0)
    grads = full.reshape(GROUPS * HD, HD).astype(F32)

    to_left = lax.ppermute(edges[:EDGE], TILE, backward)
    to_right = lax.ppermute(edges[EDGE:], TILE, forward)
    d_kv = own_grads[:, HD:].reshape(lat_rows, lon_cols, 2 * HD)
    d_kv = d_kv.at[:, lon_cols - HALO :].add(
        to_left.astype(F32).reshape(lat_rows, HALO, 2 * HD)
    )
    d_kv = d_kv.at[:, :HALO].add(to_right.astype(F32).reshape(lat_rows, HALO, 2 * HD))
    d_kv = d_kv.reshape(ROWS, 2 * HD)
    d_qkv = jnp.stack(
        [own_grads[:, :HD], d_kv[:, :HD], d_kv[:, HD:], jnp.zeros((ROWS, HD), F32)]
    ).astype(BF16)
    (d_tokens,) = call(
        tokens_kernel,
        [place, d_qkv, tok_rows, inverse, *own, *other],
        [((ROWS, features), BF16)],
        [((ROWS, features), F32)],
        800_000_000,
        8_000_000,
        1,
    )
    return (d_tokens.reshape(tokens.shape), grads[: 3 * HD].T, grads[3 * HD :])


def solution(mesh):
    inner = jax.sharding.Mesh(
        mesh.devices.reshape(4, 4, 8, 2, 2), ("x", "zlo", "y", "zhi", "core")
    )
    placed = (
        P(FSDP, None, TILE, None),
        P(FSDP, None),
        P(None, FSDP),
        P(TILE, None),
        P(FSDP, None, TILE, None),
    )
    return jax.shard_map(
        local,
        mesh=inner,
        in_specs=placed,
        out_specs=(P(FSDP, None, TILE, None), P(FSDP, None), P(None, FSDP)),
        check_vma=False,
    )
```

time: 229 us -> 185 us (0.81)
  the two profiles are of different devices: /device:TPU:16 before, /device:TPU:26 now
where the time goes in v2:
time: 185 us; the launch traced here: 184 us
  starting transfers between devices  79 us (43%)
  waiting for transfers between devices  56.1 us (30%)
  other arithmetic  18.4 us (10%)
  local copies, waits for them, and re-layouts  16.5 us (9%)
  Pallas kernels  12.6 us (7%)
    ppermute x3, waiting for transfers between devices, local(): lax.ppermute(chip[step], 'x', shift_pairs(GROUPS, step)).astype(F32)  20.6 us
    all_to_all x1, waiting for transfers between devices, gather_weights(): lax.all_to_all(jnp.broadcast_to(mine[None], (BLOCKS,) + mine.shape), ('y'...  19.8 us
    all_to_all x1, starting transfers between devices, gather_weights(): lax.all_to_all(jnp.broadcast_to(mine[None], (BLOCKS,) + mine.shape), ('y'...  15.8 us
    pallas_call x3, Pallas kernels, call(): pl.pallas_call(body, in_specs=[scalars] * smem + [whole] * (len(operands)...  12.6 us
    ppermute x3, starting transfers between devices, local(): lax.ppermute(chip[step], 'x', shift_pairs(GROUPS, step)).astype(F32)  10.9 us
    ppermute x3, starting transfers between devices, gather_weights(): lax.ppermute(spread, 'x', shift_pairs(GROUPS, step))  9.73 us
    ppermute x4, starting transfers between devices, gather_weights(): other = [lax.ppermute(part, 'core', shift_pairs(2, 1)) for part in own]  8.15 us
    ppermute x3, waiting for transfers between devices, gather_weights(): lax.ppermute(spread, 'x', shift_pairs(GROUPS, step))  8.02 us
  transfers between devices with their start and end apart: 18, of which 9 were waited for; matrix products, arithmetic and copies ran while one was open for 11% of the time, Pallas kernels for 3%

profile of v2, /device:TPU:26, one launch (start us, length us, event | category | flops | bytes accessed | tf_op | source)
XLA Modules:
  0.0 183.7 jit_solution(12580557555637300316)
XLA Ops:
  3.3 15.8 %all-to-all-start = ((bf16[16,128,128]{2,1,0:T(8,128)(2,1)}), bf16[16,128,128]{2,1,0:T(8,128)(2,1)S(1)}, u32[]{:S(2)}, u32[]{:S(2)}) async-start(bf16[16,128,128]{2,1,0:T(8,128)(2,1)} %broadcast_in_dim.4), calls=%async_computation | async-start | bytes 1048576 | tf_op jit(solution)/shard_map/all_to_all | solution.py:183
  19.6 19.8 %all-to-all-done.refs_0_ = bf16[16,128,128]{2,1,0:T(8,128)(2,1)S(1)} async-done(((bf16[16,128,128]{2,1,0:T(8,128)(2,1)}), bf16[16,128,128]{2,1,0:T(8,128)(2,1)S(1)}, u32[]{:S(2)}, u32[]{:S(2)}) %all-to-all-start) | async-done | bytes 524320 | tf_op jit(solution)/shard_map/all_to_all | solution.py:183
  40.5 3.0 %collective-permute-start = (bf16[12,2,4096]{2,1,0:T(2,128)(2,1)}, bf16[12,2,4096]{2,1,0:T(2,128)(2,1)S(1)}, u32[]{:S(2)}, u32[]{:S(2)}) collective-permute-start(bf16[12,2,4096]{2,1,0:T(2,128)(2,1)} %get-tuple-element.49), channel_id=1, source_target_pairs={{0,32},{32,64},{64,96},{96,128},{128,160},{160,192},{192,224},{224... | collective-permute-start | bytes 589832 | tf_op jit(solution)/shard_map/ppermute | solution.py:204
  45.1 5.5 %collective-permute-start.1 = (bf16[12,2,4096]{2,1,0:T(2,128)(2,1)}, bf16[12,2,4096]{2,1,0:T(2,128)(2,1)S(1)}, u32[]{:S(2)}, u32[]{:S(2)}) collective-permute-start(bf16[12,2,4096]{2,1,0:T(2,128)(2,1)} %get-tuple-element.50), channel_id=1, source_target_pairs={{0,480},{32,0},{64,32},{96,64},{128,96},{160,128},{192,160},{224,1... | collective-permute-start | bytes 589832 | tf_op jit(solution)/shard_map/ppermute | solution.py:205
  50.7 3.4 %collective-permute-start.2 = (bf16[16,128,128]{2,1,0:T(8,128)(2,1)S(1)}, bf16[16,128,128]{2,1,0:T(8,128)(2,1)S(1)}, u32[]{:S(2)}, u32[]{:S(2)}) collective-permute-start(bf16[16,128,128]{2,1,0:T(8,128)(2,1)S(1)} %all-to-all-done.refs_0_), channel_id=1, source_target_pairs={{0,128},{128,256},{256,384},{384,0},{1,129},{129,257},{257,385},{3... | collective-permute-start | bytes 1572872 | tf_op jit(solution)/shard_map/ppermute | solution.py:187
  54.1 4.2 %collective-permute-start.3 = (bf16[16,128,128]{2,1,0:T(8,128)(2,1)S(1)}, bf16[16,128,128]{2,1,0:T(8,128)(2,1)S(1)}, u32[]{:S(2)}, u32[]{:S(2)}) collective-permute-start(bf16[16,128,128]{2,1,0:T(8,128)(2,1)S(1)} %all-to-all-done.refs_0_), channel_id=1, source_target_pairs={{0,256},{128,384},{256,0},{384,128},{1,257},{129,385},{257,1},{385... | collective-permute-start | bytes 1572872 | tf_op jit(solution)/shard_map/ppermute | solution.py:187
  58.3 2.1 %collective-permute-start.4 = (bf16[16,128,128]{2,1,0:T(8,128)(2,1)S(1)}, bf16[16,128,128]{2,1,0:T(8,128)(2,1)}, u32[]{:S(2)}, u32[]{:S(2)}) collective-permute-start(bf16[16,128,128]{2,1,0:T(8,128)(2,1)S(1)} %all-to-all-done.refs_0_), channel_id=1, source_target_pairs={{0,384},{128,0},{256,128},{384,256},{1,385},{129,1},{257,129},{385... | collective-permute-start | bytes 1572872 | tf_op jit(solution)/shard_map/ppermute | solution.py:187
  69.2 2.4 %collective-permute-start.6 = (bf16[16,128,128]{2,1,0:T(8,128)(2,1)S(1)}, bf16[16,128,128]{2,1,0:T(8,128)(2,1)S(1)}, u32[]{:S(2)}, u32[]{:S(2)}) collective-permute-start(bf16[16,128,128]{2,1,0:T(8,128)(2,1)S(1)} %collective-permute-done.2.refs_1_), channel_id=1, source_target_pairs={{0,1},{1,0},{2,3},{3,2},{4,5},{5,4},{6,7},{7,6},{8,9},{9,8},{10,11... | collective-permute-start | bytes 1572872 | tf_op jit(solution)/shard_map/ppermute | solution.py:189
  74.3 7.2 %collective-permute-done.4.refs_3_ = bf16[16,128,128]{2,1,0:T(8,128)(2,1)} collective-permute-done((bf16[16,128,128]{2,1,0:T(8,128)(2,1)S(1)}, bf16[16,128,128]{2,1,0:T(8,128)(2,1)}, u32[]{:S(2)}, u32[]{:S(2)}) %collective-permute-start.4) | collective-permute-done | bytes 524320 | tf_op jit(solution)/shard_map/ppermute | solution.py:187
  85.5 6.2 %shard_map.76 = (bf16[4,16,128,128]{3,2,1,0:T(8,128)(2,1)S(1)}, bf16[384,240]{1,0:T(8,128)(2,1)S(1)}, bf16[128,192]{1,0:T(8,128)(2,1)S(1)}, f32[192,384]{1,0:T(8,128)S(1)}, bf16[48,256]{1,0:T(8,128)(2,1)S(1)}) custom-call(s32[2]{0:T(128)S(1)} %pad_add_fusion.place_ref, s32[1,2]{1,0:T(1,128)S(1)} %copy-done.10, ...), custom_call_target="tpu_custom_call" | custom-call | flops 3000000000 | bytes 12000000 | tf_op jit(solution)/shard_map/pallas_call | solution.py:167
  91.8 2.4 %collective-permute-start.9 = (bf16[4,16,128,128]{3,2,1,0:T(8,128)(2,1)S(1)}, bf16[4,16,128,128]{3,2,1,0:T(8,128)(2,1)S(1)}, u32[]{:S(2)}, u32[]{:S(2)}) collective-permute-start(bf16[4,16,128,128]{3,2,1,0:T(8,128)(2,1)S(1)} %get-tuple-element.39), channel_id=1, source_target_pairs={{0,1},{1,0},{2,3},{3,2},{4,5},{5,4},{6,7},{7,6},{8,9},{9,8},{10,11... | collective-permute-start | bytes 6291464 | tf_op jit(solution)/shard_map/ppermute | solution.py:233
  95.7 2.3 %collective-permute-done.9 = bf16[4,16,128,128]{3,2,1,0:T(8,128)(2,1)S(1)} collective-permute-done((bf16[4,16,128,128]{3,2,1,0:T(8,128)(2,1)S(1)}, bf16[4,16,128,128]{3,2,1,0:T(8,128)(2,1)S(1)}, u32[]{:S(2)}, u32[]{:S(2)}) %collective-permute-start.9) | collective-permute-done | bytes 2097184 | tf_op jit(solution)/shard_map/ppermute | solution.py:233
  99.9 2.5 %collective-permute-start.10 = (bf16[16,128,128]{2,1,0:T(8,128)(2,1)}, bf16[16,128,128]{2,1,0:T(8,128)(2,1)}, u32[]{:S(2)}, u32[]{:S(2)}) collective-permute-start(bf16[16,128,128]{2,1,0:T(8,128)(2,1)} %get-tuple-element.46), channel_id=1, source_target_pairs={{0,128},{128,256},{256,384},{384,0},{1,129},{129,257},{257,385},{3... | collective-permute-start | bytes 1572872 | tf_op jit(solution)/shard_map/ppermute | solution.py:249
  102.4 6.0 %collective-permute-start.11 = (bf16[16,128,128]{2,1,0:T(8,128)(2,1)}, bf16[16,128,128]{2,1,0:T(8,128)(2,1)}, u32[]{:S(2)}, u32[]{:S(2)}) collective-permute-start(bf16[16,128,128]{2,1,0:T(8,128)(2,1)} %get-tuple-element.48), channel_id=1, source_target_pairs={{0,256},{128,384},{256,0},{384,128},{1,257},{129,385},{257,1},{385... | collective-permute-start | bytes 1572872 | tf_op jit(solution)/shard_map/ppermute | solution.py:249
  108.4 2.4 %collective-permute-start.12 = (bf16[16,128,128]{2,1,0:T(8,128)(2,1)}, bf16[16,128,128]{2,1,0:T(8,128)(2,1)}, u32[]{:S(2)}, u32[]{:S(2)}) collective-permute-start(bf16[16,128,128]{2,1,0:T(8,128)(2,1)} %get-tuple-element.47), channel_id=1, source_target_pairs={{0,384},{128,0},{256,128},{384,256},{1,385},{129,1},{257,129},{385... | collective-permute-start | bytes 1572872 | tf_op jit(solution)/shard_map/ppermute | solution.py:249
  111.5 6.0 %collective-permute-done.10 = bf16[16,128,128]{2,1,0:T(8,128)(2,1)} collective-permute-done((bf16[16,128,128]{2,1,0:T(8,128)(2,1)}, bf16[16,128,128]{2,1,0:T(8,128)(2,1)}, u32[]{:S(2)}, u32[]{:S(2)}) %collective-permute-start.10) | collective-permute-done | bytes 524320 | tf_op jit(solution)/shard_map/ppermute | solution.py:249
  117.5 4.0 %collective-permute-done.11 = bf16[16,128,128]{2,1,0:T(8,128)(2,1)} collective-permute-done((bf16[16,128,128]{2,1,0:T(8,128)(2,1)}, bf16[16,128,128]{2,1,0:T(8,128)(2,1)}, u32[]{:S(2)}, u32[]{:S(2)}) %collective-permute-start.11) | collective-permute-done | bytes 524320 | tf_op jit(solution)/shard_map/ppermute | solution.py:249
  121.5 10.6 %collective-permute-done.12 = bf16[16,128,128]{2,1,0:T(8,128)(2,1)} collective-permute-done((bf16[16,128,128]{2,1,0:T(8,128)(2,1)}, bf16[16,128,128]{2,1,0:T(8,128)(2,1)}, u32[]{:S(2)}, u32[]{:S(2)}) %collective-permute-start.12) | collective-permute-done | bytes 524320 | tf_op jit(solution)/shard_map/ppermute | solution.py:249
  132.1 2.9 %fusion.2 = bf16[16,128,128]{2,1,0:T(8,128)(2,1)} fusion(bf16[16,128,128]{2,1,0:T(8,128)(2,1)} %collective-permute-done.12, bf16[16,128,128]{2,1,0:T(8,128)(2,1)} %collective-permute-done.11, bf16[16,128,128]{2,1,0:T(8,128)(2,1)} %collective-permute-done.10, bf16[4,16,128,128]{3,2,1,0:T(8,128)(2,1)} %copy-done.11, bf16[4,16,128,128]{3,2,1,0:T(8,128)(2,1)} %copy-done.1), kind=kLoop, calls=%fused_computation.6 | loop fusion | flops 3145728 | bytes 3145728 | tf_op jit(solution)/shard_map/convert_element_type | solution.py:250
  135.0 7.8 %all-to-all-start.1 = ((bf16[64,32,128]{2,1,0:T(8,128)(2,1)}), bf16[64,32,128]{2,1,0:T(8,128)(2,1)}, u32[]{:S(2)}, u32[]{:S(2)}) async-start(bf16[64,32,128]{2,1,0:T(8,128)(2,1)} %bitcast.37), calls=%async_computation.1 | async-start | bytes 1048576 | tf_op jit(solution)/shard_map/all_to_all | solution.py:252
  143.6 6.4 %collective-permute-start.13 = (bf16[24,256]{1,0:T(8,128)(2,1)S(1)}, bf16[24,256]{1,0:T(8,128)(2,1)}, u32[]{:S(2)}, u32[]{:S(2)}) collective-permute-start(bf16[24,256]{1,0:T(8,128)(2,1)S(1)} %get-tuple-element.54), channel_id=1, source_target_pairs={{0,480},{32,0},{64,32},{96,64},{128,96},{160,128},{192,160},{224,1... | collective-permute-start | bytes 36872 | tf_op jit(solution)/shard_map/ppermute | solution.py:257
  153.9 5.3 %collective-permute-done.14 = bf16[24,256]{1,0:T(8,128)(2,1)} collective-permute-done((bf16[24,256]{1,0:T(8,128)(2,1)S(1)}, bf16[24,256]{1,0:T(8,128)(2,1)}, u32[]{:S(2)}, u32[]{:S(2)}) %collective-permute-start.14) | collective-permute-done | bytes 12320 | tf_op jit(solution)/shard_map/ppermute | solution.py:258
  165.8 7.4 %all-to-all-start.2 = ((bf16[16,32,128]{2,1,0:T(8,128)(2,1)}), bf16[16,32,128]{2,1,0:T(8,128)(2,1)S(1)}, u32[]{:S(2)}, u32[]{:S(2)}) async-start(bf16[16,32,128]{2,1,0:T(8,128)(2,1)} %broadcast_in_dim.5), calls=%async_computation.2 | async-start | bytes 262144 | tf_op jit(solution)/shard_map/all_to_all | solution.py:254
  177.3 4.9 %shard_map.78 = bf16[192,4096]{1,0:T(8,128)(2,1)} custom-call(s32[2]{0:T(128)S(1)} %pad_add_fusion.place_ref, bf16[4,192,128]{2,1,0:T(8,128)(2,1)S(1)} %maximum_maximum_fusion.d_qkv_ref, bf16[192,4096]{1,0:T(8,128)(2,1)S(1)} %bitcast.34, f32[192,1]{1,0:T(8,128)S(1)} %rsqrt.36.inverse_ref, bf16[16,128,128]{2,1,0:T(8,128)(2,1)S(1)} %all-to-all-done.refs_0_, ...), custom_call_target="tpu_custom_call" | custom-call | flops 800000000 | bytes 8000000 | tf_op jit(solution)/shard_map/pallas_call | solution.py:167
  (80 shorter events, 42.0 us)
Async XLA Ops:
  0.6 18.5 %copy-start = (bf16[1,12,16,4096]{3,2,1,0:T(8,128)(2,1)S(1)}, bf16[1,12,16,4096]{3,2,1,0:T(8,128)(2,1)}, u32[]{:S(2)}) copy-start(bf16[1,12,16,4096]{3,2,1,0:T(8,128)(2,1)} %param.9) | copy-start | bytes 4718596
  3.3 36.0 %all-to-all-start = ((bf16[16,128,128]{2,1,0:T(8,128)(2,1)}), bf16[16,128,128]{2,1,0:T(8,128)(2,1)S(1)}, u32[]{:S(2)}, u32[]{:S(2)}) async-start(bf16[16,128,128]{2,1,0:T(8,128)(2,1)} %broadcast_in_dim.4), calls=%async_computation | async-start | bytes 1048576 | tf_op jit(solution)/shard_map/all_to_all | solution.py:183
  40.5 19.9 %collective-permute-start = (bf16[12,2,4096]{2,1,0:T(2,128)(2,1)}, bf16[12,2,4096]{2,1,0:T(2,128)(2,1)S(1)}, u32[]{:S(2)}, u32[]{:S(2)}) collective-permute-start(bf16[12,2,4096]{2,1,0:T(2,128)(2,1)} %get-tuple-element.49), channel_id=1, source_target_pairs={{0,32},{32,64},{64,96},{96,128},{128,160},{160,192},{192,224},{224... | collective-permute-start | bytes 589832 | tf_op jit(solution)/shard_map/ppermute | solution.py:204
  45.1 19.5 %collective-permute-start.1 = (bf16[12,2,4096]{2,1,0:T(2,128)(2,1)}, bf16[12,2,4096]{2,1,0:T(2,128)(2,1)S(1)}, u32[]{:S(2)}, u32[]{:S(2)}) collective-permute-start(bf16[12,2,4096]{2,1,0:T(2,128)(2,1)} %get-tuple-element.50), channel_id=1, source_target_pairs={{0,480},{32,0},{64,32},{96,64},{128,96},{160,128},{192,160},{224,1... | collective-permute-start | bytes 589832 | tf_op jit(solution)/shard_map/ppermute | solution.py:205
  50.7 18.5 %collective-permute-start.2 = (bf16[16,128,128]{2,1,0:T(8,128)(2,1)S(1)}, bf16[16,128,128]{2,1,0:T(8,128)(2,1)S(1)}, u32[]{:S(2)}, u32[]{:S(2)}) collective-permute-start(bf16[16,128,128]{2,1,0:T(8,128)(2,1)S(1)} %all-to-all-done.refs_0_), channel_id=1, source_target_pairs={{0,128},{128,256},{256,384},{384,0},{1,129},{129,257},{257,385},{3... | collective-permute-start | bytes 1572872 | tf_op jit(solution)/shard_map/ppermute | solution.py:187
  54.1 18.3 %collective-permute-start.3 = (bf16[16,128,128]{2,1,0:T(8,128)(2,1)S(1)}, bf16[16,128,128]{2,1,0:T(8,128)(2,1)S(1)}, u32[]{:S(2)}, u32[]{:S(2)}) collective-permute-start(bf16[16,128,128]{2,1,0:T(8,128)(2,1)S(1)} %all-to-all-done.refs_0_), channel_id=1, source_target_pairs={{0,256},{128,384},{256,0},{384,128},{1,257},{129,385},{257,1},{385... | collective-permute-start | bytes 1572872 | tf_op jit(solution)/shard_map/ppermute | solution.py:187
  58.3 23.2 %collective-permute-start.4 = (bf16[16,128,128]{2,1,0:T(8,128)(2,1)S(1)}, bf16[16,128,128]{2,1,0:T(8,128)(2,1)}, u32[]{:S(2)}, u32[]{:S(2)}) collective-permute-start(bf16[16,128,128]{2,1,0:T(8,128)(2,1)S(1)} %all-to-all-done.refs_0_), channel_id=1, source_target_pairs={{0,384},{128,0},{256,128},{384,256},{1,385},{129,1},{257,129},{385... | collective-permute-start | bytes 1572872 | tf_op jit(solution)/shard_map/ppermute | solution.py:187
  60.5 24.9 %collective-permute-start.5 = (bf16[16,128,128]{2,1,0:T(8,128)(2,1)S(1)}, bf16[16,128,128]{2,1,0:T(8,128)(2,1)}, u32[]{:S(2)}, u32[]{:S(2)}) collective-permute-start(bf16[16,128,128]{2,1,0:T(8,128)(2,1)S(1)} %all-to-all-done.refs_0_), channel_id=1, source_target_pairs={{0,1},{1,0},{2,3},{3,2},{4,5},{5,4},{6,7},{7,6},{8,9},{9,8},{10,11... | collective-permute-start | bytes 1572872 | tf_op jit(solution)/shard_map/ppermute | solution.py:189
  69.2 16.2 %collective-permute-start.6 = (bf16[16,128,128]{2,1,0:T(8,128)(2,1)S(1)}, bf16[16,128,128]{2,1,0:T(8,128)(2,1)S(1)}, u32[]{:S(2)}, u32[]{:S(2)}) collective-permute-start(bf16[16,128,128]{2,1,0:T(8,128)(2,1)S(1)} %collective-permute-done.2.refs_1_), channel_id=1, source_target_pairs={{0,1},{1,0},{2,3},{3,2},{4,5},{5,4},{6,7},{7,6},{8,9},{9,8},{10,11... | collective-permute-start | bytes 1572872 | tf_op jit(solution)/shard_map/ppermute | solution.py:189
  72.4 13.0 %collective-permute-start.7 = (bf16[16,128,128]{2,1,0:T(8,128)(2,1)S(1)}, bf16[16,128,128]{2,1,0:T(8,128)(2,1)S(1)}, u32[]{:S(2)}, u32[]{:S(2)}) collective-permute-start(bf16[16,128,128]{2,1,0:T(8,128)(2,1)S(1)} %collective-permute-done.3.refs_2_), channel_id=1, source_target_pairs={{0,1},{1,0},{2,3},{3,2},{4,5},{5,4},{6,7},{7,6},{8,9},{9,8},{10,11... | collective-permute-start | bytes 1572872 | tf_op jit(solution)/shard_map/ppermute | solution.py:189
  81.5 4.0 %collective-permute-start.8 = (bf16[16,128,128]{2,1,0:T(8,128)(2,1)}, bf16[16,128,128]{2,1,0:T(8,128)(2,1)S(1)}, u32[]{:S(2)}, u32[]{:S(2)}) collective-permute-start(bf16[16,128,128]{2,1,0:T(8,128)(2,1)} %collective-permute-done.4.refs_3_), channel_id=1, source_target_pairs={{0,1},{1,0},{2,3},{3,2},{4,5},{5,4},{6,7},{7,6},{8,9},{9,8},{10,11... | collective-permute-start | bytes 1572872 | tf_op jit(solution)/shard_map/ppermute | solution.py:189
  85.4 6.4 %copy-start.3 = (bf16[16,128,128]{2,1,0:T(8,128)(2,1)}, bf16[16,128,128]{2,1,0:T(8,128)(2,1)S(1)}, u32[]{:S(2)}) copy-start(bf16[16,128,128]{2,1,0:T(8,128)(2,1)S(1)} %collective-permute-done.6.refs_5_) | copy-start | bytes 1572868
  85.4 6.4 %copy-start.5 = (bf16[16,128,128]{2,1,0:T(8,128)(2,1)}, bf16[16,128,128]{2,1,0:T(8,128)(2,1)S(1)}, u32[]{:S(2)}) copy-start(bf16[16,128,128]{2,1,0:T(8,128)(2,1)S(1)} %collective-permute-done.7.refs_6_) | copy-start | bytes 1572868
  85.5 6.3 %copy-start.7 = (bf16[16,128,128]{2,1,0:T(8,128)(2,1)}, bf16[16,128,128]{2,1,0:T(8,128)(2,1)S(1)}, u32[]{:S(2)}) copy-start(bf16[16,128,128]{2,1,0:T(8,128)(2,1)S(1)} %collective-permute-done.8.refs_7_) | copy-start | bytes 1572868
  91.8 3.9 %copy-start.9 = (bf16[48,256]{1,0:T(8,128)(2,1)}, bf16[48,256]{1,0:T(8,128)(2,1)S(1)}, u32[]{:S(2)}) copy-start(bf16[48,256]{1,0:T(8,128)(2,1)S(1)} %get-tuple-element.41) | copy-start | bytes 73732
  91.8 6.2 %collective-permute-start.9 = (bf16[4,16,128,128]{3,2,1,0:T(8,128)(2,1)S(1)}, bf16[4,16,128,128]{3,2,1,0:T(8,128)(2,1)S(1)}, u32[]{:S(2)}, u32[]{:S(2)}) collective-permute-start(bf16[4,16,128,128]{3,2,1,0:T(8,128)(2,1)S(1)} %get-tuple-element.39), channel_id=1, source_target_pairs={{0,1},{1,0},{2,3},{3,2},{4,5},{5,4},{6,7},{7,6},{8,9},{9,8},{10,11... | collective-permute-start | bytes 6291464 | tf_op jit(solution)/shard_map/ppermute | solution.py:233
  95.7 4.2 %copy-start.1 = (bf16[4,16,128,128]{3,2,1,0:T(8,128)(2,1)}, bf16[4,16,128,128]{3,2,1,0:T(8,128)(2,1)S(1)}, u32[]{:S(2)}) copy-start(bf16[4,16,128,128]{3,2,1,0:T(8,128)(2,1)S(1)} %shard_map.77) | copy-start | bytes 6291460
  99.9 17.5 %collective-permute-start.10 = (bf16[16,128,128]{2,1,0:T(8,128)(2,1)}, bf16[16,128,128]{2,1,0:T(8,128)(2,1)}, u32[]{:S(2)}, u32[]{:S(2)}) collective-permute-start(bf16[16,128,128]{2,1,0:T(8,128)(2,1)} %get-tuple-element.46), channel_id=1, source_target_pairs={{0,128},{128,256},{256,384},{384,0},{1,129},{129,257},{257,385},{3... | collective-permute-start | bytes 1572872 | tf_op jit(solution)/shard_map/ppermute | solution.py:249
  102.4 19.0 %collective-permute-start.11 = (bf16[16,128,128]{2,1,0:T(8,128)(2,1)}, bf16[16,128,128]{2,1,0:T(8,128)(2,1)}, u32[]{:S(2)}, u32[]{:S(2)}) collective-permute-start(bf16[16,128,128]{2,1,0:T(8,128)(2,1)} %get-tuple-element.48), channel_id=1, source_target_pairs={{0,256},{128,384},{256,0},{384,128},{1,257},{129,385},{257,1},{385... | collective-permute-start | bytes 1572872 | tf_op jit(solution)/shard_map/ppermute | solution.py:249
  108.4 23.7 %collective-permute-start.12 = (bf16[16,128,128]{2,1,0:T(8,128)(2,1)}, bf16[16,128,128]{2,1,0:T(8,128)(2,1)}, u32[]{:S(2)}, u32[]{:S(2)}) collective-permute-start(bf16[16,128,128]{2,1,0:T(8,128)(2,1)} %get-tuple-element.47), channel_id=1, source_target_pairs={{0,384},{128,0},{256,128},{384,256},{1,385},{129,1},{257,129},{385... | collective-permute-start | bytes 1572872 | tf_op jit(solution)/shard_map/ppermute | solution.py:249
  135.0 29.0 %all-to-all-start.1 = ((bf16[64,32,128]{2,1,0:T(8,128)(2,1)}), bf16[64,32,128]{2,1,0:T(8,128)(2,1)}, u32[]{:S(2)}, u32[]{:S(2)}) async-start(bf16[64,32,128]{2,1,0:T(8,128)(2,1)} %bitcast.37), calls=%async_computation.1 | async-start | bytes 1048576 | tf_op jit(solution)/shard_map/all_to_all | solution.py:252
  143.6 9.6 %collective-permute-start.13 = (bf16[24,256]{1,0:T(8,128)(2,1)S(1)}, bf16[24,256]{1,0:T(8,128)(2,1)}, u32[]{:S(2)}, u32[]{:S(2)}) collective-permute-start(bf16[24,256]{1,0:T(8,128)(2,1)S(1)} %get-tuple-element.54), channel_id=1, source_target_pairs={{0,480},{32,0},{64,32},{96,64},{128,96},{160,128},{192,160},{224,1... | collective-permute-start | bytes 36872 | tf_op jit(solution)/shard_map/ppermute | solution.py:257
  150.0 9.3 %collective-permute-start.14 = (bf16[24,256]{1,0:T(8,128)(2,1)S(1)}, bf16[24,256]{1,0:T(8,128)(2,1)}, u32[]{:S(2)}, u32[]{:S(2)}) collective-permute-start(bf16[24,256]{1,0:T(8,128)(2,1)S(1)} %get-tuple-element.53), channel_id=1, source_target_pairs={{0,32},{32,64},{64,96},{96,128},{128,160},{160,192},{192,224},{224... | collective-permute-start | bytes 36872 | tf_op jit(solution)/shard_map/ppermute | solution.py:258
  165.8 16.4 %all-to-all-start.2 = ((bf16[16,32,128]{2,1,0:T(8,128)(2,1)}), bf16[16,32,128]{2,1,0:T(8,128)(2,1)S(1)}, u32[]{:S(2)}, u32[]{:S(2)}) async-start(bf16[16,32,128]{2,1,0:T(8,128)(2,1)} %broadcast_in_dim.5), calls=%async_computation.2 | async-start | bytes 262144 | tf_op jit(solution)/shard_map/all_to_all | solution.py:254
  (7 other events, 10.7 us)

commit v3 on v2

v3 whole, which is shorter than its diff:
```python
import functools

import jax
import jax.numpy as jnp
from jax import lax
from jax.experimental import pallas as pl
from jax.experimental.pallas import tpu as pltpu
from jax.sharding import PartitionSpec as P

HALO = 2
EPS = 1e-05
TILE = ("x", "zlo")
FSDP = ("y", "zhi", "core")
GROUPS = 4
HD = 128
ROWS = 192
EDGE = 24
PAD = 32
EXT = ROWS + 2 * PAD
STEPS = (2, 1, 3)
BLOCKS = 16
CHUNK = 4
VMEM_BYTES = 40 * 1024 * 1024
OVER_ROWS = (((0,), (0,)), ((), ()))
OVER_COLS = (((1,), (1,)), ((), ()))
F32 = jnp.float32
BF16 = jnp.bfloat16


def shift_pairs(count, step):
    return [(i, (i + step) % count) for i in range(count)]


def dot(a, b, dims=(((1,), (0,)), ((), ()))):
    return lax.dot_general(a, b, dims, preferred_element_type=F32)


def feature_block(block, core):
    return pl.ds(pl.multiple_of((2 * block + core) * HD, HD), HD)


def features_of(refs, first, core):
    columns = [
        jnp.concatenate([ref[:, feature_block(block, core)] for ref in refs], axis=0)
        for block in range(first, first + CHUNK)
    ]
    return jnp.concatenate(columns, axis=1)


def edge_chooser(shape, row_axis):
    row = lax.broadcasted_iota(jnp.int32, shape, row_axis)
    edge = lax.broadcasted_iota(jnp.int32, shape, 1 - row_axis)
    column = row % 16
    base = (row // 16) * HALO
    last = (column >= 16 - HALO) & (edge == base + column - (16 - HALO))
    first = (column < HALO) & (edge == base + column)
    return first, last


def as_weights(mask):
    return jnp.where(mask, 1.0, 0.0).astype(BF16)


def normalise_kernel(tokens_ref, normed_ref, inverse_ref, first_ref, last_ref):
    total = jnp.zeros((ROWS, HD), F32)
    for block in range(2 * BLOCKS):
        piece = tokens_ref[:, block * HD : (block + 1) * HD].astype(F32)
        total = total + piece * piece
    mean = jnp.sum(total, axis=-1, keepdims=True) * (1.0 / (2 * BLOCKS * HD))
    inverse = lax.rsqrt(mean + EPS)
    inverse_ref[...] = inverse
    first, last = edge_chooser((PAD, ROWS), 1)
    first, last = as_weights(first), as_weights(last)
    for block in range(0, 2 * BLOCKS, CHUNK):
        columns = slice(block * HD, (block + CHUNK) * HD)
        piece = (tokens_ref[:, columns].astype(F32) * inverse).astype(BF16)
        normed_ref[:, columns] = piece
        first_ref[:, columns] = dot(first, piece).astype(BF16)
        last_ref[:, columns] = dot(last, piece).astype(BF16)


def project(rows_refs, parts, core):
    total = None
    for part, side in zip(parts, (core, 1 - core)):
        for first in range(0, BLOCKS, CHUNK):
            term = dot(features_of(rows_refs, first, side), part(first))
            total = term if total is None else total + term
    return total.astype(BF16)


def columns_of(refs):
    def weights(first):
        return jnp.concatenate(
            [ref[first : first + CHUNK].reshape(CHUNK * HD, HD) for ref in refs], axis=1
        )

    return weights


def pick(values, index):
    chosen = values[0]
    for place in range(1, len(values)):
        chosen = jnp.where(index == place, values[place], chosen)
    return chosen


def project_back(rows_refs, parts, core):
    total = None
    for ref, side in zip(parts, (core, 1 - core)):
        for first in range(0, BLOCKS, CHUNK):
            blocks = [ref[block] for block in range(first, first + CHUNK)]
            term = dot(
                features_of(rows_refs, first, side), jnp.concatenate(blocks, axis=1), OVER_COLS
            )
            total = term if total is None else total + term
    return total.astype(BF16)


def store_grads(first_ref, rest_ref, left_qkv, left_out, normed_refs, cot_ref, x, side):
    for first in range(0, BLOCKS, CHUNK):
        qkv = dot(left_qkv, features_of(normed_refs, first, side)).astype(BF16)
        out = dot(left_out, features_of([cot_ref], first, side)).astype(BF16)
        groups = [qkv[:HD], qkv[HD : 2 * HD], qkv[2 * HD :], out]
        for block in range(CHUNK):
            columns = slice(block * HD, (block + 1) * HD)
            values = [value[:, columns] for value in groups]
            first_ref[first + block] = pick(values, x)
            for step in range(1, GROUPS):
                rest_ref[step - 1, first + block] = pick(values[step:] + values[:step], x)


def attention_kernel(place_ref, band_ref, normed_ref, low_ref, high_ref, cot_ref, *refs):
    own, other = refs[:GROUPS], refs[GROUPS : 2 * GROUPS]
    (
        away_first_ref,
        away_rest_ref,
        left_qkv_ref,
        left_out_ref,
        own_grads_ref,
        low_back_ref,
        high_back_ref,
        proj,
        datt,
    ) = refs[2 * GROUPS :]
    x = place_ref[0]
    core = place_ref[1]
    normed_refs = [normed_ref, low_ref, high_ref]

    for position in range(GROUPS):
        steps = [(position - group) % GROUPS for group in range(GROUPS)]

        @pl.when(x == position)
        def _():
            proj[...] = project(
                normed_refs,
                (
                    columns_of([own[step] for step in steps[:3]]),
                    columns_of([other[step] for step in steps[:3]]),
                ),
                core,
            )
            datt[...] = project_back([cot_ref], (own[steps[3]], other[steps[3]]), core)

    queries = proj[:ROWS, :HD]
    keys = proj[:, HD : 2 * HD]
    values = proj[:, 2 * HD :]
    d_att = datt[...]
    place = lax.broadcasted_iota(jnp.int32, (1, EXT), 1)
    column = (place - ROWS) % HALO
    low = (place >= ROWS) & (place < ROWS + EDGE)
    high = (place >= ROWS + PAD) & (place < ROWS + PAD + EDGE)
    usable = (
        (place < ROWS)
        | (low & (HALO - column <= band_ref[0, 0]))
        | (high & (column + 1 <= band_ref[0, 1]))
    )
    scale = HD ** (-0.5)
    scores = jnp.where(usable, dot(queries, keys, OVER_COLS) * scale, -jnp.inf)
    exp_scores = jnp.exp(scores - jnp.max(scores, axis=-1, keepdims=True))
    probs = exp_scores / jnp.sum(exp_scores, axis=-1, keepdims=True)
    probs_low = probs.astype(BF16)
    attended = dot(probs_low, values).astype(BF16)
    d_probs = dot(d_att, values, OVER_COLS)
    inner = jnp.sum(probs * d_probs, axis=-1, keepdims=True)
    d_scores = (probs * (d_probs - inner) * scale).astype(BF16)
    d_query = dot(d_scores, keys)
    d_keys = dot(d_scores, queries, OVER_ROWS)
    d_values = dot(probs_low, d_att, OVER_ROWS)
    own_grads_ref[:, :HD] = d_query
    own_grads_ref[:, HD : 2 * HD] = d_keys[:ROWS]
    own_grads_ref[:, 2 * HD :] = d_values[:ROWS]
    for ref, start in ((low_back_ref, ROWS), (high_back_ref, ROWS + PAD)):
        ref[:, :HD] = d_keys[start : start + PAD].astype(BF16)
        ref[:, HD:] = d_values[start : start + PAD].astype(BF16)
    d_query_ext = jnp.concatenate([d_query, jnp.zeros((2 * PAD, HD), F32)], axis=0)
    left_qkv = jnp.concatenate([d_query_ext.T, d_keys.T, d_values.T], axis=0).astype(BF16)
    left_out = attended.astype(F32).T.astype(BF16)
    left_qkv_ref[...] = left_qkv
    left_out_ref[...] = left_out
    store_grads(
        away_first_ref, away_rest_ref, left_qkv, left_out, normed_refs, cot_ref, x, 1 - core
    )


def own_half_kernel(place_ref, left_qkv_ref, left_out_ref, *refs):
    normed_refs, cot_ref, first_ref, rest_ref = refs[:3], refs[3], refs[4], refs[5]
    store_grads(
        first_ref,
        rest_ref,
        left_qkv_ref[...],
        left_out_ref[...],
        normed_refs,
        cot_ref,
        place_ref[0],
        place_ref[1],
    )


def spread_kernel(place_ref, w_qkv_ref, w_out_ref, out_ref):
    columns = [w_qkv_ref[:, group * HD : (group + 1) * HD] for group in range(3)]
    mine = pick(columns + [w_out_ref[...]], place_ref[0])
    for block in range(BLOCKS):
        out_ref[block] = mine


def piece_kernel(pieces_ref, out_ref):
    total = pieces_ref[0].astype(F32)
    for source in range(1, pieces_ref.shape[0]):
        total = total + pieces_ref[source].astype(F32)
    total = total.astype(BF16)
    for target in range(out_ref.shape[0]):
        out_ref[target] = total


def final_kernel(full_ref, qkv_ref, out_ref):
    for group in range(GROUPS):
        value = jnp.concatenate(
            [full_ref[4 * group + quarter].astype(F32) for quarter in range(4)], axis=0
        )
        if group < 3:
            qkv_ref[:, group * HD : (group + 1) * HD] = value.T
        else:
            out_ref[...] = value


def line_kernel(*refs):
    for block in range(BLOCKS):
        total = refs[0][block].astype(F32)
        for ref in refs[1:-1]:
            total = total + ref[block].astype(F32)
        refs[-1][block] = total.astype(BF16)


def tokens_kernel(
    place_ref, grads_ref, from_left_ref, from_right_ref, tokens_ref, inverse_ref, *refs
):
    own, other = refs[:GROUPS], refs[GROUPS : 2 * GROUPS]
    out_ref, d_normed, d_qkv = refs[2 * GROUPS :]
    x = place_ref[0]
    core = place_ref[1]
    first, last = edge_chooser((ROWS, PAD), 0)
    d_kv = (
        grads_ref[:, HD:]
        + dot(as_weights(first), from_left_ref[...])
        + dot(as_weights(last), from_right_ref[...])
    )
    d_qkv[0] = grads_ref[:, :HD].astype(BF16)
    d_qkv[1] = d_kv[:, :HD].astype(BF16)
    d_qkv[2] = d_kv[:, HD:].astype(BF16)
    d_qkv[3] = jnp.zeros((ROWS, HD), BF16)
    left = jnp.concatenate(
        [d_qkv[(x - step + GROUPS) % GROUPS] for step in range(GROUPS)], axis=1
    )
    total = jnp.zeros((ROWS, HD), F32)
    for parts, side in ((own, core), (other, 1 - core)):
        for block in range(BLOCKS):
            weights = jnp.concatenate([part[block] for part in parts], axis=1)
            piece = dot(left, weights, OVER_COLS)
            columns = feature_block(block, side)
            d_normed[:, columns] = piece
            total = total + piece * tokens_ref[:, columns].astype(F32)
    inverse = inverse_ref[...]
    mean = jnp.sum(total, axis=-1, keepdims=True) * (1.0 / (2 * BLOCKS * HD))
    factor = inverse * inverse * inverse * mean
    for block in range(2 * BLOCKS):
        columns = slice(block * HD, (block + 1) * HD)
        out_ref[:, columns] = (
            inverse * d_normed[:, columns] - tokens_ref[:, columns].astype(F32) * factor
        ).astype(BF16)


def call(body, operands, outs, scratch, flops, in_bytes, smem):
    whole = pl.BlockSpec(memory_space=pltpu.VMEM)
    scalars = pl.BlockSpec(memory_space=pltpu.SMEM)
    return pl.pallas_call(
        body,
        in_specs=[scalars] * smem + [whole] * (len(operands) - smem),
        out_specs=[whole] * len(outs),
        out_shape=[jax.ShapeDtypeStruct(shape, dtype) for shape, dtype in outs],
        scratch_shapes=[pltpu.VMEM(shape, dtype) for shape, dtype in scratch],
        compiler_params=pltpu.CompilerParams(vmem_limit_bytes=VMEM_BYTES),
        cost_estimate=pl.CostEstimate(
            flops=flops, bytes_accessed=in_bytes, transcendentals=0
        ),
    )(*operands)


def local(tokens, w_qkv, w_out, band, cotangent):
    samples, lat_rows, lon_cols, features = tokens.shape
    place = jnp.stack([lax.axis_index("x"), lax.axis_index("core")]).astype(jnp.int32)
    forward = shift_pairs(16, 1)
    backward = shift_pairs(16, -1)
    swap = shift_pairs(2, 1)
    tok_rows = tokens.reshape(ROWS, features)
    cot_rows = cotangent.reshape(ROWS, features)
    (spread,) = call(
        spread_kernel, [place, w_qkv, w_out], [((BLOCKS, HD, HD), BF16)], [], 1_000_000, 500_000, 1
    )
    spread = lax.all_to_all(spread, ("y", "zhi"), 0, 0)
    steps = {step: lax.ppermute(spread, "x", shift_pairs(GROUPS, step)) for step in STEPS}
    own = [spread, steps[1], steps[2], steps[3]]
    late_rows, unused = lax.optimization_barrier((tok_rows, spread))
    normed_own, inverse, first, last = call(
        normalise_kernel,
        [late_rows],
        [
            ((ROWS, features), BF16),
            ((ROWS, 1), F32),
            ((PAD, features), BF16),
            ((PAD, features), BF16),
        ],
        [],
        200_000_000,
        3_000_000,
        0,
    )
    low = lax.ppermute(last, TILE, forward)
    high = lax.ppermute(first, TILE, backward)
    own[3], low, high = lax.optimization_barrier((own[3], low, high))
    normed = [normed_own, low, high]
    other = [lax.ppermute(part, "core", swap) for part in own]

    first_shape = ((BLOCKS, HD, HD), BF16)
    rest_shape = ((GROUPS - 1, BLOCKS, HD, HD), BF16)
    away_first, away_rest, left_qkv, left_out, own_grads, low_back, high_back = call(
        attention_kernel,
        [place, band, *normed, cot_rows, *own, *other],
        [
            first_shape,
            rest_shape,
            ((3 * HD, EXT), BF16),
            ((HD, ROWS), BF16),
            ((ROWS, 3 * HD), F32),
            ((PAD, 2 * HD), BF16),
            ((PAD, 2 * HD), BF16),
        ],
        [((EXT, 3 * HD), BF16), ((ROWS, HD), BF16)],
        3_000_000_000,
        12_000_000,
        2,
    )
    got_rest = lax.ppermute(away_rest, "core", swap)
    got_first = lax.ppermute(away_first, "core", swap)
    kept_first, kept_rest = call(
        own_half_kernel,
        [place, left_qkv, left_out, *normed, cot_rows],
        [first_shape, rest_shape],
        [],
        500_000_000,
        6_000_000,
        1,
    )
    sent = [
        (kept_rest[step].astype(F32) + got_rest[step].astype(F32)).astype(BF16)
        for step in range(GROUPS - 1)
    ]
    sent, low_back, high_back = lax.optimization_barrier((sent, low_back, high_back))
    arrived = [
        lax.ppermute(sent[step - 1], "x", shift_pairs(GROUPS, step)) for step in STEPS
    ]
    from_right = lax.ppermute(low_back, TILE, backward)
    from_left = lax.ppermute(high_back, TILE, forward)
    (line,) = call(
        line_kernel,
        [kept_first, got_first, *arrived],
        [first_shape],
        [],
        2_000_000,
        3_000_000,
        0,
    )
    line, from_left, from_right = lax.optimization_barrier((line, from_left, from_right))
    pieces = lax.all_to_all(line.reshape(64, 32, HD), ("y", "zhi", "zlo"), 0, 0)
    (d_tokens,) = call(
        tokens_kernel,
        [place, own_grads, from_left, from_right, tok_rows, inverse, *own, *other],
        [((ROWS, features), BF16)],
        [((ROWS, features), F32), ((GROUPS, ROWS, HD), BF16)],
        800_000_000,
        8_000_000,
        1,
    )
    pieces, d_tokens = lax.optimization_barrier((pieces, d_tokens))
    (piece,) = call(
        piece_kernel, [pieces], [((16, 32, HD), BF16)], [], 1_000_000, 1_000_000, 0
    )
    full = lax.all_to_all(piece, TILE, 0, 0)
    grad_qkv, grad_out = call(
        final_kernel, [full], [((HD, 3 * HD), F32), ((HD, HD), F32)], [], 1_000_000, 500_000, 0
    )
    return (d_tokens.reshape(tokens.shape), grad_qkv, grad_out)


def solution(mesh):
    inner = jax.sharding.Mesh(
        mesh.devices.reshape(4, 4, 8, 2, 2), ("x", "zlo", "y", "zhi", "core")
    )
    placed = (
        P(FSDP, None, TILE, None),
        P(FSDP, None),
        P(None, FSDP),
        P(TILE, None),
        P(FSDP, None, TILE, None),
    )
    return jax.shard_map(
        local,
        mesh=inner,
        in_specs=placed,
        out_specs=(P(FSDP, None, TILE, None), P(FSDP, None), P(None, FSDP)),
        check_vma=False,
    )
```

time: 185 us -> 166 us (0.90)
  the two profiles are of different devices: /device:TPU:26 before, /device:TPU:8 now
where the time goes in v3:
time: 166 us; the launch traced here: 165 us
  starting transfers between devices  60.2 us (36%)
  blocking collectives  49 us (30%)
  waiting for transfers between devices  30 us (18%)
  Pallas kernels  14.2 us (9%)
  local copies, waits for them, and re-layouts  10 us (6%)
    all_to_all x1, blocking collectives, local(): spread = lax.all_to_all(spread, ('y', 'zhi'), 0, 0)  36.4 us
    pallas_call x8, Pallas kernels, call(): pl.pallas_call(body, in_specs=[scalars] * smem + [whole] * (len(operands)...  14.2 us
    all_to_all x1, blocking collectives, local(): full = lax.all_to_all(piece, TILE, 0, 0)  12.7 us
    ppermute x3, starting transfers between devices, local(): lax.ppermute(spread, 'x', shift_pairs(GROUPS, step))  10.2 us
    unnamed x42, local copies, waits for them, and re-layouts  10 us
    ppermute x3, starting transfers between devices, local(): lax.ppermute(sent[step - 1], 'x', shift_pairs(GROUPS, step))  9.76 us
    ppermute x3, waiting for transfers between devices, local(): lax.ppermute(sent[step - 1], 'x', shift_pairs(GROUPS, step))  9.68 us
    ppermute x4, starting transfers between devices, local(): other = [lax.ppermute(part, 'core', swap) for part in own]  8.35 us
  transfers between devices with their start and end apart: 17, of which 6 were waited for; matrix products, arithmetic and copies ran while one was open for 0% of the time, Pallas kernels for 5%

profile of v3, /device:TPU:8, one launch (start us, length us, event | category | flops | bytes accessed | tf_op | source)
XLA Modules:
  0.0 165.1 jit_solution(10573464450525193091)
XLA Ops:
  3.1 36.4 %all_to_all.15.refs_0_ = bf16[16,128,128]{2,1,0:T(8,128)(2,1)S(1)} all-to-all(bf16[16,128,128]{2,1,0:T(8,128)(2,1)S(1)} %shard_map.76), channel_id=1, replica_groups=mesh['x'=4,'zlo'=4,'y'=8,'zhi'=2,'core'=2] {'y','zhi'}, dimensions={0} | all-to-all | bytes 1048576 | tf_op jit(solution)/shard_map/all_to_all | solution.py:319
  39.5 4.7 %collective-permute-start = (bf16[16,128,128]{2,1,0:T(8,128)(2,1)S(1)}, bf16[16,128,128]{2,1,0:T(8,128)(2,1)S(1)}, u32[]{:S(2)}, u32[]{:S(2)}) collective-permute-start(bf16[16,128,128]{2,1,0:T(8,128)(2,1)S(1)} %all_to_all.15.refs_0_), channel_id=1, source_target_pairs={{0,384},{128,0},{256,128},{384,256},{1,385},{129,1},{257,129},{385... | collective-permute-start | bytes 1572872 | tf_op jit(solution)/shard_map/ppermute | solution.py:320
  44.2 2.7 %collective-permute-start.4 = (bf16[16,128,128]{2,1,0:T(8,128)(2,1)S(1)}, bf16[16,128,128]{2,1,0:T(8,128)(2,1)S(1)}, u32[]{:S(2)}, u32[]{:S(2)}) collective-permute-start(bf16[16,128,128]{2,1,0:T(8,128)(2,1)S(1)} %all_to_all.15.refs_0_), channel_id=1, source_target_pairs={{0,256},{128,384},{256,0},{384,128},{1,257},{129,385},{257,1},{385... | collective-permute-start | bytes 1572872 | tf_op jit(solution)/shard_map/ppermute | solution.py:320
  46.9 2.8 %collective-permute-start.3 = (bf16[16,128,128]{2,1,0:T(8,128)(2,1)S(1)}, bf16[16,128,128]{2,1,0:T(8,128)(2,1)S(1)}, u32[]{:S(2)}, u32[]{:S(2)}) collective-permute-start(bf16[16,128,128]{2,1,0:T(8,128)(2,1)S(1)} %all_to_all.15.refs_0_), channel_id=1, source_target_pairs={{0,128},{128,256},{256,384},{384,0},{1,129},{129,257},{257,385},{3... | collective-permute-start | bytes 1572872 | tf_op jit(solution)/shard_map/ppermute | solution.py:320
  50.8 2.7 %collective-permute-start.1 = (bf16[32,4096]{1,0:T(8,128)(2,1)S(1)}, bf16[32,4096]{1,0:T(8,128)(2,1)S(1)}, u32[]{:S(2)}, u32[]{:S(2)}) collective-permute-start(bf16[32,4096]{1,0:T(8,128)(2,1)S(1)} %get-tuple-element.34), channel_id=1, source_target_pairs={{0,32},{32,64},{64,96},{96,128},{128,160},{160,192},{192,224},{224... | collective-permute-start | bytes 786440 | tf_op jit(solution)/shard_map/ppermute | solution.py:337
  53.5 7.1 %collective-permute-start.2 = (bf16[32,4096]{1,0:T(8,128)(2,1)S(1)}, bf16[32,4096]{1,0:T(8,128)(2,1)S(1)}, u32[]{:S(2)}, u32[]{:S(2)}) collective-permute-start(bf16[32,4096]{1,0:T(8,128)(2,1)S(1)} %get-tuple-element.35), channel_id=1, source_target_pairs={{0,480},{32,0},{64,32},{96,64},{128,96},{160,128},{192,160},{224,1... | collective-permute-start | bytes 786440 | tf_op jit(solution)/shard_map/ppermute | solution.py:338
  60.5 5.3 %collective-permute-done.1.low_ref.refs_1_ = bf16[32,4096]{1,0:T(8,128)(2,1)S(1)} collective-permute-done((bf16[32,4096]{1,0:T(8,128)(2,1)S(1)}, bf16[32,4096]{1,0:T(8,128)(2,1)S(1)}, u32[]{:S(2)}, u32[]{:S(2)}) %collective-permute-start.1) | collective-permute-done | bytes 262176 | tf_op jit(solution)/shard_map/ppermute | solution.py:337
  68.1 2.1 %collective-permute-start.7 = (bf16[16,128,128]{2,1,0:T(8,128)(2,1)S(1)}, bf16[16,128,128]{2,1,0:T(8,128)(2,1)S(1)}, u32[]{:S(2)}, u32[]{:S(2)}) collective-permute-start(bf16[16,128,128]{2,1,0:T(8,128)(2,1)S(1)} %collective-permute-done.4.refs_2_), channel_id=1, source_target_pairs={{0,1},{1,0},{2,3},{3,2},{4,5},{5,4},{6,7},{7,6},{8,9},{9,8},{10,11... | collective-permute-start | bytes 1572872 | tf_op jit(solution)/shard_map/ppermute | solution.py:341
  70.2 6.8 %collective-permute-done.3.refs_1_ = bf16[16,128,128]{2,1,0:T(8,128)(2,1)S(1)} collective-permute-done((bf16[16,128,128]{2,1,0:T(8,128)(2,1)S(1)}, bf16[16,128,128]{2,1,0:T(8,128)(2,1)S(1)}, u32[]{:S(2)}, u32[]{:S(2)}) %collective-permute-start.3) | collective-permute-done | bytes 524320 | tf_op jit(solution)/shard_map/ppermute | solution.py:320
  77.0 1.9 %collective-permute-start.6 = (bf16[16,128,128]{2,1,0:T(8,128)(2,1)S(1)}, bf16[16,128,128]{2,1,0:T(8,128)(2,1)S(1)}, u32[]{:S(2)}, u32[]{:S(2)}) collective-permute-start(bf16[16,128,128]{2,1,0:T(8,128)(2,1)S(1)} %collective-permute-done.3.refs_1_), channel_id=1, source_target_pairs={{0,1},{1,0},{2,3},{3,2},{4,5},{5,4},{6,7},{7,6},{8,9},{9,8},{10,11... | collective-permute-start | bytes 1572872 | tf_op jit(solution)/shard_map/ppermute | solution.py:341
  78.9 2.4 %collective-permute-start.8 = (bf16[16,128,128]{2,1,0:T(8,128)(2,1)S(1)}, bf16[16,128,128]{2,1,0:T(8,128)(2,1)S(1)}, u32[]{:S(2)}, u32[]{:S(2)}) collective-permute-start(bf16[16,128,128]{2,1,0:T(8,128)(2,1)S(1)} %collective-permute-done.refs_3_), channel_id=1, source_target_pairs={{0,1},{1,0},{2,3},{3,2},{4,5},{5,4},{6,7},{7,6},{8,9},{9,8},{10,11... | collective-permute-start | bytes 1572872 | tf_op jit(solution)/shard_map/ppermute | solution.py:341
  82.9 4.3 %shard_map.78 = (bf16[16,128,128]{2,1,0:T(8,128)(2,1)S(1)}, bf16[3,16,128,128]{3,2,1,0:T(8,128)(2,1)S(1)}, bf16[384,256]{1,0:T(8,128)(2,1)S(1)}, bf16[128,192]{1...) custom-call(s32[2]{0:T(128)S(1)} %pad_add_fusion.place_ref, ...), custom_call_target="tpu_custom_call" | custom-call | flops 3000000000 | bytes 12000000 | tf_op jit(solution)/shard_map/pallas_call | solution.py:295
  87.2 2.3 %collective-permute-start.10 = (bf16[3,16,128,128]{3,2,1,0:T(8,128)(2,1)S(1)}, bf16[3,16,128,128]{3,2,1,0:T(8,128)(2,1)S(1)}, u32[]{:S(2)}, u32[]{:S(2)}) collective-permute-start(bf16[3,16,128,128]{3,2,1,0:T(8,128)(2,1)S(1)} %get-tuple-element.44), channel_id=1, source_target_pairs={{0,1},{1,0},{2,3},{3,2},{4,5},{5,4},{6,7},{7,6},{8,9},{9,8},{10,11... | collective-permute-start | bytes 4718600 | tf_op jit(solution)/shard_map/ppermute | solution.py:362
  89.5 2.2 %collective-permute-start.9 = (bf16[16,128,128]{2,1,0:T(8,128)(2,1)S(1)}, bf16[16,128,128]{2,1,0:T(8,128)(2,1)S(1)}, u32[]{:S(2)}, u32[]{:S(2)}) collective-permute-start(bf16[16,128,128]{2,1,0:T(8,128)(2,1)S(1)} %get-tuple-element.42), channel_id=1, source_target_pairs={{0,1},{1,0},{2,3},{3,2},{4,5},{5,4},{6,7},{7,6},{8,9},{9,8},{10,11... | collective-permute-start | bytes 1572872 | tf_op jit(solution)/shard_map/ppermute | solution.py:363
  94.1 2.7 %collective-permute-start.11 = (bf16[16,128,128]{2,1,0:T(8,128)(2,1)S(1)}, bf16[16,128,128]{2,1,0:T(8,128)(2,1)S(1)}, u32[]{:S(2)}, u32[]{:S(2)}) collective-permute-start(bf16[16,128,128]{2,1,0:T(8,128)(2,1)S(1)} %get-tuple-element.47), channel_id=1, source_target_pairs={{0,256},{128,384},{256,0},{384,128},{1,257},{129,385},{257,1},{385... | collective-permute-start | bytes 1572872 | tf_op jit(solution)/shard_map/ppermute | solution.py:379
  96.8 2.6 %collective-permute-start.12 = (bf16[16,128,128]{2,1,0:T(8,128)(2,1)S(1)}, bf16[16,128,128]{2,1,0:T(8,128)(2,1)S(1)}, u32[]{:S(2)}, u32[]{:S(2)}) collective-permute-start(bf16[16,128,128]{2,1,0:T(8,128)(2,1)S(1)} %get-tuple-element.48), channel_id=1, source_target_pairs={{0,128},{128,256},{256,384},{384,0},{1,129},{129,257},{257,385},{3... | collective-permute-start | bytes 1572872 | tf_op jit(solution)/shard_map/ppermute | solution.py:379
  99.4 4.5 %collective-permute-start.13 = (bf16[16,128,128]{2,1,0:T(8,128)(2,1)S(1)}, bf16[16,128,128]{2,1,0:T(8,128)(2,1)S(1)}, u32[]{:S(2)}, u32[]{:S(2)}) collective-permute-start(bf16[16,128,128]{2,1,0:T(8,128)(2,1)S(1)} %get-tuple-element.49), channel_id=1, source_target_pairs={{0,384},{128,0},{256,128},{384,256},{1,385},{129,1},{257,129},{385... | collective-permute-start | bytes 1572872 | tf_op jit(solution)/shard_map/ppermute | solution.py:379
  103.9 1.9 %collective-permute-start.14 = (bf16[32,256]{1,0:T(8,128)(2,1)S(1)}, bf16[32,256]{1,0:T(8,128)(2,1)S(1)}, u32[]{:S(2)}, u32[]{:S(2)}) collective-permute-start(bf16[32,256]{1,0:T(8,128)(2,1)S(1)} %get-tuple-element.50), channel_id=1, source_target_pairs={{0,32},{32,64},{64,96},{96,128},{128,160},{160,192},{192,224},{224... | collective-permute-start | bytes 49160 | tf_op jit(solution)/shard_map/ppermute | solution.py:382
  105.8 7.8 %collective-permute-start.15 = (bf16[32,256]{1,0:T(8,128)(2,1)S(1)}, bf16[32,256]{1,0:T(8,128)(2,1)S(1)}, u32[]{:S(2)}, u32[]{:S(2)}) collective-permute-start(bf16[32,256]{1,0:T(8,128)(2,1)S(1)} %get-tuple-element.51), channel_id=1, source_target_pairs={{0,480},{32,0},{64,32},{96,64},{128,96},{160,128},{192,160},{224,1... | collective-permute-start | bytes 49160 | tf_op jit(solution)/shard_map/ppermute | solution.py:381
  113.6 9.7 %collective-permute-done.12.refs_3_ = bf16[16,128,128]{2,1,0:T(8,128)(2,1)S(1)} collective-permute-done((bf16[16,128,128]{2,1,0:T(8,128)(2,1)S(1)}, bf16[16,128,128]{2,1,0:T(8,128)(2,1)S(1)}, u32[]{:S(2)}, u32[]{:S(2)}) %collective-permute-start.12) | collective-permute-done | bytes 524320 | tf_op jit(solution)/shard_map/ppermute | solution.py:379
  125.1 7.9 %all-to-all-start.1 = ((bf16[64,32,128]{2,1,0:T(8,128)(2,1)}), bf16[64,32,128]{2,1,0:T(8,128)(2,1)S(1)}, u32[]{:S(2)}, u32[]{:S(2)}) async-start(bf16[64,32,128]{2,1,0:T(8,128)(2,1)} %bitcast.7), calls=%async_computation.1 | async-start | bytes 1048576 | tf_op jit(solution)/shard_map/all_to_all | solution.py:393
  140.6 4.5 %shard_map.81 = bf16[192,4096]{1,0:T(8,128)(2,1)} custom-call(s32[2]{0:T(128)S(1)} %copy-done.19, f32[192,384]{1,0:T(8,128)S(1)} %get-tuple-element.53.grads_ref, bf16[32,256]{1,0:T(8,128)(2,1)S(1)} %collective-permute-done.14.from_left_ref, bf16[32,256]{1,0:T(8,128)(2,1)S(1)} %copy-done.17, bf16[192,4096]{1,0:T(8,128)(2,1)S(1)} %bitcast.13, ...), custom_call_target="tpu_custom_call" | custom-call | flops 800000000 | bytes 8000000 | tf_op jit(solution)/shard_map/pallas_call | solution.py:295
  145.1 6.4 %all-to-all-done.1.pieces_ref = bf16[64,32,128]{2,1,0:T(8,128)(2,1)S(1)} async-done(((bf16[64,32,128]{2,1,0:T(8,128)(2,1)}), bf16[64,32,128]{2,1,0:T(8,128)(2,1)S(1)}, u32[]{:S(2)}, u32[]{:S(2)}) %all-to-all-start.1) | async-done | bytes 524320 | tf_op jit(solution)/shard_map/all_to_all | solution.py:393
  151.6 12.7 %all_to_all.16.full_ref = bf16[16,32,128]{2,1,0:T(8,128)(2,1)S(1)} all-to-all(bf16[16,32,128]{2,1,0:T(8,128)(2,1)S(1)} %shard_map.82), channel_id=1, replica_groups=mesh['x'=4,'zlo'=4,'y'=8,'zhi'=2,'core'=2] {'x','zlo'}, dimensions={0} | all-to-all | bytes 262144 | tf_op jit(solution)/shard_map/all_to_all | solution.py:407
  (64 shorter events, 19.8 us)
Async XLA Ops:
  0.6 49.1 %copy-start = (bf16[1,12,16,4096]{3,2,1,0:T(8,128)(2,1)S(1)}, bf16[1,12,16,4096]{3,2,1,0:T(8,128)(2,1)}, u32[]{:S(2)}) copy-start(bf16[1,12,16,4096]{3,2,1,0:T(8,128)(2,1)} %param.5) | copy-start | bytes 4718596
  2.5 89.3 %copy-start.18 = (s32[2]{0:T(128)}, s32[2]{0:T(128)S(1)}, u32[]{:S(2)}) copy-start(s32[2]{0:T(128)S(1)} %pad_add_fusion.place_ref) | copy-start | bytes 28
  2.5 80.4 %copy-start.1 = (bf16[1,12,16,4096]{3,2,1,0:T(8,128)(2,1)S(1)}, bf16[1,12,16,4096]{3,2,1,0:T(8,128)(2,1)}, u32[]{:S(2)}) copy-start(bf16[1,12,16,4096]{3,2,1,0:T(8,128)(2,1)} %param.9) | copy-start | bytes 4718596
  2.5 80.4 %copy-start.20 = (s32[1,2]{1,0:T(1,128)S(1)}, s32[1,2]{1,0:T(1,128)}, u32[]{:S(2)}) copy-start(s32[1,2]{1,0:T(1,128)} %band_ref.1) | copy-start | bytes 28
  39.5 28.3 %collective-permute-start = (bf16[16,128,128]{2,1,0:T(8,128)(2,1)S(1)}, bf16[16,128,128]{2,1,0:T(8,128)(2,1)S(1)}, u32[]{:S(2)}, u32[]{:S(2)}) collective-permute-start(bf16[16,128,128]{2,1,0:T(8,128)(2,1)S(1)} %all_to_all.15.refs_0_), channel_id=1, source_target_pairs={{0,384},{128,0},{256,128},{384,256},{1,385},{129,1},{257,129},{385... | collective-permute-start | bytes 1572872 | tf_op jit(solution)/shard_map/ppermute | solution.py:320
  44.2 23.9 %collective-permute-start.4 = (bf16[16,128,128]{2,1,0:T(8,128)(2,1)S(1)}, bf16[16,128,128]{2,1,0:T(8,128)(2,1)S(1)}, u32[]{:S(2)}, u32[]{:S(2)}) collective-permute-start(bf16[16,128,128]{2,1,0:T(8,128)(2,1)S(1)} %all_to_all.15.refs_0_), channel_id=1, source_target_pairs={{0,256},{128,384},{256,0},{384,128},{1,257},{129,385},{257,1},{385... | collective-permute-start | bytes 1572872 | tf_op jit(solution)/shard_map/ppermute | solution.py:320
  46.9 30.1 %collective-permute-start.3 = (bf16[16,128,128]{2,1,0:T(8,128)(2,1)S(1)}, bf16[16,128,128]{2,1,0:T(8,128)(2,1)S(1)}, u32[]{:S(2)}, u32[]{:S(2)}) collective-permute-start(bf16[16,128,128]{2,1,0:T(8,128)(2,1)S(1)} %all_to_all.15.refs_0_), channel_id=1, source_target_pairs={{0,128},{128,256},{256,384},{384,0},{1,129},{129,257},{257,385},{3... | collective-permute-start | bytes 1572872 | tf_op jit(solution)/shard_map/ppermute | solution.py:320
  50.8 15.1 %collective-permute-start.1 = (bf16[32,4096]{1,0:T(8,128)(2,1)S(1)}, bf16[32,4096]{1,0:T(8,128)(2,1)S(1)}, u32[]{:S(2)}, u32[]{:S(2)}) collective-permute-start(bf16[32,4096]{1,0:T(8,128)(2,1)S(1)} %get-tuple-element.34), channel_id=1, source_target_pairs={{0,32},{32,64},{64,96},{96,128},{128,160},{160,192},{192,224},{224... | collective-permute-start | bytes 786440 | tf_op jit(solution)/shard_map/ppermute | solution.py:337
  53.5 14.3 %collective-permute-start.2 = (bf16[32,4096]{1,0:T(8,128)(2,1)S(1)}, bf16[32,4096]{1,0:T(8,128)(2,1)S(1)}, u32[]{:S(2)}, u32[]{:S(2)}) collective-permute-start(bf16[32,4096]{1,0:T(8,128)(2,1)S(1)} %get-tuple-element.35), channel_id=1, source_target_pairs={{0,480},{32,0},{64,32},{96,64},{128,96},{160,128},{192,160},{224,1... | collective-permute-start | bytes 786440 | tf_op jit(solution)/shard_map/ppermute | solution.py:338
  65.8 15.5 %collective-permute-start.5 = (bf16[16,128,128]{2,1,0:T(8,128)(2,1)S(1)}, bf16[16,128,128]{2,1,0:T(8,128)(2,1)S(1)}, u32[]{:S(2)}, u32[]{:S(2)}) collective-permute-start(bf16[16,128,128]{2,1,0:T(8,128)(2,1)S(1)} %all_to_all.15.refs_0_), channel_id=1, source_target_pairs={{0,1},{1,0},{2,3},{3,2},{4,5},{5,4},{6,7},{7,6},{8,9},{9,8},{10,11... | collective-permute-start | bytes 1572872 | tf_op jit(solution)/shard_map/ppermute | solution.py:341
  68.1 19.1 %copy-start.2 = (bf16[16,128,128]{2,1,0:T(8,128)(2,1)}, bf16[16,128,128]{2,1,0:T(8,128)(2,1)S(1)}, u32[]{:S(2)}) copy-start(bf16[16,128,128]{2,1,0:T(8,128)(2,1)S(1)} %collective-permute-done.4.refs_2_) | copy-start | bytes 1572868
  68.1 13.3 %collective-permute-start.7 = (bf16[16,128,128]{2,1,0:T(8,128)(2,1)S(1)}, bf16[16,128,128]{2,1,0:T(8,128)(2,1)S(1)}, u32[]{:S(2)}, u32[]{:S(2)}) collective-permute-start(bf16[16,128,128]{2,1,0:T(8,128)(2,1)S(1)} %collective-permute-done.4.refs_2_), channel_id=1, source_target_pairs={{0,1},{1,0},{2,3},{3,2},{4,5},{5,4},{6,7},{7,6},{8,9},{9,8},{10,11... | collective-permute-start | bytes 1572872 | tf_op jit(solution)/shard_map/ppermute | solution.py:341
  77.0 10.2 %copy-start.4 = (bf16[16,128,128]{2,1,0:T(8,128)(2,1)}, bf16[16,128,128]{2,1,0:T(8,128)(2,1)S(1)}, u32[]{:S(2)}) copy-start(bf16[16,128,128]{2,1,0:T(8,128)(2,1)S(1)} %collective-permute-done.3.refs_1_) | copy-start | bytes 1572868
  77.0 4.4 %collective-permute-start.6 = (bf16[16,128,128]{2,1,0:T(8,128)(2,1)S(1)}, bf16[16,128,128]{2,1,0:T(8,128)(2,1)S(1)}, u32[]{:S(2)}, u32[]{:S(2)}) collective-permute-start(bf16[16,128,128]{2,1,0:T(8,128)(2,1)S(1)} %collective-permute-done.3.refs_1_), channel_id=1, source_target_pairs={{0,1},{1,0},{2,3},{3,2},{4,5},{5,4},{6,7},{7,6},{8,9},{9,8},{10,11... | collective-permute-start | bytes 1572872 | tf_op jit(solution)/shard_map/ppermute | solution.py:341
  78.9 3.9 %collective-permute-start.8 = (bf16[16,128,128]{2,1,0:T(8,128)(2,1)S(1)}, bf16[16,128,128]{2,1,0:T(8,128)(2,1)S(1)}, u32[]{:S(2)}, u32[]{:S(2)}) collective-permute-start(bf16[16,128,128]{2,1,0:T(8,128)(2,1)S(1)} %collective-permute-done.refs_3_), channel_id=1, source_target_pairs={{0,1},{1,0},{2,3},{3,2},{4,5},{5,4},{6,7},{7,6},{8,9},{9,8},{10,11... | collective-permute-start | bytes 1572872 | tf_op jit(solution)/shard_map/ppermute | solution.py:341
  81.3 5.9 %copy-start.6 = (bf16[16,128,128]{2,1,0:T(8,128)(2,1)}, bf16[16,128,128]{2,1,0:T(8,128)(2,1)S(1)}, u32[]{:S(2)}) copy-start(bf16[16,128,128]{2,1,0:T(8,128)(2,1)S(1)} %collective-permute-done.5.refs_4_) | copy-start | bytes 1572868
  87.2 6.3 %collective-permute-start.10 = (bf16[3,16,128,128]{3,2,1,0:T(8,128)(2,1)S(1)}, bf16[3,16,128,128]{3,2,1,0:T(8,128)(2,1)S(1)}, u32[]{:S(2)}, u32[]{:S(2)}) collective-permute-start(bf16[3,16,128,128]{3,2,1,0:T(8,128)(2,1)S(1)} %get-tuple-element.44), channel_id=1, source_target_pairs={{0,1},{1,0},{2,3},{3,2},{4,5},{5,4},{6,7},{7,6},{8,9},{9,8},{10,11... | collective-permute-start | bytes 4718600 | tf_op jit(solution)/shard_map/ppermute | solution.py:362
  89.5 16.2 %collective-permute-start.9 = (bf16[16,128,128]{2,1,0:T(8,128)(2,1)S(1)}, bf16[16,128,128]{2,1,0:T(8,128)(2,1)S(1)}, u32[]{:S(2)}, u32[]{:S(2)}) collective-permute-start(bf16[16,128,128]{2,1,0:T(8,128)(2,1)S(1)} %get-tuple-element.42), channel_id=1, source_target_pairs={{0,1},{1,0},{2,3},{3,2},{4,5},{5,4},{6,7},{7,6},{8,9},{9,8},{10,11... | collective-permute-start | bytes 1572872 | tf_op jit(solution)/shard_map/ppermute | solution.py:363
  94.1 19.6 %collective-permute-start.11 = (bf16[16,128,128]{2,1,0:T(8,128)(2,1)S(1)}, bf16[16,128,128]{2,1,0:T(8,128)(2,1)S(1)}, u32[]{:S(2)}, u32[]{:S(2)}) collective-permute-start(bf16[16,128,128]{2,1,0:T(8,128)(2,1)S(1)} %get-tuple-element.47), channel_id=1, source_target_pairs={{0,256},{128,384},{256,0},{384,128},{1,257},{129,385},{257,1},{385... | collective-permute-start | bytes 1572872 | tf_op jit(solution)/shard_map/ppermute | solution.py:379
  96.8 26.5 %collective-permute-start.12 = (bf16[16,128,128]{2,1,0:T(8,128)(2,1)S(1)}, bf16[16,128,128]{2,1,0:T(8,128)(2,1)S(1)}, u32[]{:S(2)}, u32[]{:S(2)}) collective-permute-start(bf16[16,128,128]{2,1,0:T(8,128)(2,1)S(1)} %get-tuple-element.48), channel_id=1, source_target_pairs={{0,128},{128,256},{256,384},{384,0},{1,129},{129,257},{257,385},{3... | collective-permute-start | bytes 1572872 | tf_op jit(solution)/shard_map/ppermute | solution.py:379
  99.4 24.0 %collective-permute-start.13 = (bf16[16,128,128]{2,1,0:T(8,128)(2,1)S(1)}, bf16[16,128,128]{2,1,0:T(8,128)(2,1)S(1)}, u32[]{:S(2)}, u32[]{:S(2)}) collective-permute-start(bf16[16,128,128]{2,1,0:T(8,128)(2,1)S(1)} %get-tuple-element.49), channel_id=1, source_target_pairs={{0,384},{128,0},{256,128},{384,256},{1,385},{129,1},{257,129},{385... | collective-permute-start | bytes 1572872 | tf_op jit(solution)/shard_map/ppermute | solution.py:379
  103.9 20.6 %collective-permute-start.14 = (bf16[32,256]{1,0:T(8,128)(2,1)S(1)}, bf16[32,256]{1,0:T(8,128)(2,1)S(1)}, u32[]{:S(2)}, u32[]{:S(2)}) collective-permute-start(bf16[32,256]{1,0:T(8,128)(2,1)S(1)} %get-tuple-element.50), channel_id=1, source_target_pairs={{0,32},{32,64},{64,96},{96,128},{128,160},{160,192},{192,224},{224... | collective-permute-start | bytes 49160 | tf_op jit(solution)/shard_map/ppermute | solution.py:382
  105.8 18.7 %collective-permute-start.15 = (bf16[32,256]{1,0:T(8,128)(2,1)S(1)}, bf16[32,256]{1,0:T(8,128)(2,1)S(1)}, u32[]{:S(2)}, u32[]{:S(2)}) collective-permute-start(bf16[32,256]{1,0:T(8,128)(2,1)S(1)} %get-tuple-element.51), channel_id=1, source_target_pairs={{0,480},{32,0},{64,32},{96,64},{128,96},{160,128},{192,160},{224,1... | collective-permute-start | bytes 49160 | tf_op jit(solution)/shard_map/ppermute | solution.py:381
  125.1 26.4 %all-to-all-start.1 = ((bf16[64,32,128]{2,1,0:T(8,128)(2,1)}), bf16[64,32,128]{2,1,0:T(8,128)(2,1)S(1)}, u32[]{:S(2)}, u32[]{:S(2)}) async-start(bf16[64,32,128]{2,1,0:T(8,128)(2,1)} %bitcast.7), calls=%async_computation.1 | async-start | bytes 1048576 | tf_op jit(solution)/shard_map/all_to_all | solution.py:393
  (14 other events, 26.0 us)

commit v4 on v3

--- a/solution.py
+++ b/solution.py
@@ -36,7 +36,8 @@
 
 
 def feature_block(block, core):
-    return pl.ds(pl.multiple_of((2 * block + core) * HD, HD), HD)
+    zhi, y = divmod(block, 8)
+    return pl.ds(pl.multiple_of((2 * (2 * y + zhi) + core) * HD, HD), HD)
 
 
 def features_of(refs, first, core):
@@ -216,9 +217,17 @@
     )
 
 
-def spread_kernel(place_ref, w_qkv_ref, w_out_ref, out_ref):
-    columns = [w_qkv_ref[:, group * HD : (group + 1) * HD] for group in range(3)]
-    mine = pick(columns + [w_out_ref[...]], place_ref[0])
+def spread_kernel(place_ref, w_qkv_ref, w_out_ref, out_ref, qkv_block, out_block, sems):
+    copies = [
+        pltpu.make_async_copy(w_qkv_ref, qkv_block, sems.at[0]),
+        pltpu.make_async_copy(w_out_ref, out_block, sems.at[1]),
+    ]
+    for copy in copies:
+        copy.start()
+    for copy in copies:
+        copy.wait()
+    columns = [qkv_block[:, group * HD : (group + 1) * HD] for group in range(3)]
+    mine = pick(columns + [out_block[...]], place_ref[0])
     for block in range(BLOCKS):
         out_ref[block] = mine
 
@@ -235,7 +244,7 @@
 def final_kernel(full_ref, qkv_ref, out_ref):
     for group in range(GROUPS):
         value = jnp.concatenate(
-            [full_ref[4 * group + quarter].astype(F32) for quarter in range(4)], axis=0
+            [full_ref[4 * quarter + group].astype(F32) for quarter in range(4)], axis=0
         )
         if group < 3:
             qkv_ref[:, group * HD : (group + 1) * HD] = value.T
@@ -248,7 +257,9 @@
         total = refs[0][block].astype(F32)
         for ref in refs[1:-1]:
             total = total + ref[block].astype(F32)
-        refs[-1][block] = total.astype(BF16)
+        total = total.astype(BF16)
+        for quarter in range(4):
+            refs[-1][quarter, block] = total[quarter * 32 : (quarter + 1) * 32]
 
 
 def tokens_kernel(
@@ -305,6 +316,13 @@
     )(*operands)
 
 
+def mirrored_groups():
+    return [
+        [y * 8 + (3 - zlo if zhi else zlo) * 2 + zhi for zhi in range(2) for y in range(8)]
+        for zlo in range(4)
+    ]
+
+
 def local(tokens, w_qkv, w_out, band, cotangent):
     samples, lat_rows, lon_cols, features = tokens.shape
     place = jnp.stack([lax.axis_index("x"), lax.axis_index("core")]).astype(jnp.int32)
@@ -313,10 +331,26 @@
     swap = shift_pairs(2, 1)
     tok_rows = tokens.reshape(ROWS, features)
     cot_rows = cotangent.reshape(ROWS, features)
-    (spread,) = call(
-        spread_kernel, [place, w_qkv, w_out], [((BLOCKS, HD, HD), BF16)], [], 1_000_000, 500_000, 1
-    )
-    spread = lax.all_to_all(spread, ("y", "zhi"), 0, 0)
+    spread = pl.pallas_call(
+        spread_kernel,
+        in_specs=[
+            pl.BlockSpec(memory_space=pltpu.SMEM),
+            pl.BlockSpec(memory_space=pl.ANY),
+            pl.BlockSpec(memory_space=pl.ANY),
+        ],
+        out_specs=pl.BlockSpec(memory_space=pltpu.VMEM),
+        out_shape=jax.ShapeDtypeStruct((BLOCKS, HD, HD), BF16),
+        scratch_shapes=[
+            pltpu.VMEM((HD, 3 * HD), BF16),
+            pltpu.VMEM((HD, HD), BF16),
+            pltpu.SemaphoreType.DMA((2,)),
+        ],
+        compiler_params=pltpu.CompilerParams(vmem_limit_bytes=VMEM_BYTES),
+        cost_estimate=pl.CostEstimate(flops=0, bytes_accessed=700_000, transcendentals=0),
+    )(place, w_qkv, w_out)
+    spread = lax.all_to_all(
+        spread, ("y", "zlo", "zhi"), 0, 0, axis_index_groups=mirrored_groups()
+    )
     steps = {step: lax.ppermute(spread, "x", shift_pairs(GROUPS, step)) for step in STEPS}
     own = [spread, steps[1], steps[2], steps[3]]
     late_rows, unused = lax.optimization_barrier((tok_rows, spread))
@@ -336,7 +370,7 @@
     )
     low = lax.ppermute(last, TILE, forward)
     high = lax.ppermute(first, TILE, backward)
-    own[3], low, high = lax.optimization_barrier((own[3], low, high))
+    own[2], low, high = lax.optimization_barrier((own[2], low, high))
     normed = [normed_own, low, high]
     other = [lax.ppermute(part, "core", swap) for part in own]
 
@@ -380,17 +414,7 @@
     ]
     from_right = lax.ppermute(low_back, TILE, backward)
     from_left = lax.ppermute(high_back, TILE, forward)
-    (line,) = call(
-        line_kernel,
-        [kept_first, got_first, *arrived],
-        [first_shape],
-        [],
-        2_000_000,
-        3_000_000,
-        0,
-    )
-    line, from_left, from_right = lax.optimization_barrier((line, from_left, from_right))
-    pieces = lax.all_to_all(line.reshape(64, 32, HD), ("y", "zhi", "zlo"), 0, 0)
+    from_left, from_right = lax.optimization_barrier((from_left, from_right))
     (d_tokens,) = call(
         tokens_kernel,
         [place, own_grads, from_left, from_right, tok_rows, inverse, *own, *other],
@@ -400,11 +424,21 @@
         8_000_000,
         1,
     )
-    pieces, d_tokens = lax.optimization_barrier((pieces, d_tokens))
+    (line,) = call(
+        line_kernel,
+        [kept_first, got_first, *arrived],
+        [((4, BLOCKS, 32, HD), BF16)],
+        [],
+        2_000_000,
+        3_000_000,
+        0,
+    )
+    line, d_tokens = lax.optimization_barrier((line, d_tokens))
+    pieces = lax.all_to_all(line.reshape(64, 32, HD), ("zlo", "zhi", "y"), 0, 0)
     (piece,) = call(
         piece_kernel, [pieces], [((16, 32, HD), BF16)], [], 1_000_000, 1_000_000, 0
     )
-    full = lax.all_to_all(piece, TILE, 0, 0)
+    full = lax.all_to_all(piece, ("zlo", "x"), 0, 0)
     grad_qkv, grad_out = call(
         final_kernel, [full], [((HD, 3 * HD), F32), ((HD, HD), F32)], [], 1_000_000, 500_000, 0
     )

time: 166 us -> 158 us (0.952)
  blocking collectives: 49 us -> 71.5 us
  waiting for transfers between devices: 30 us -> 19 us
  starting transfers between devices: 60.2 us -> 49.5 us
  local copies, waits for them, and re-layouts: 10 us -> 1.76 us
    all_to_all x2 -> x3, blocking collectives: 49 us -> 71.5 us  [the longest x1 31.9 us: local(): lax.all_to_all(spread, ('y', 'zlo', 'zhi'), 0, 0, axis_index_groups=mirro...]
    ppermute x3, waiting for transfers between devices: 9.68 us -> 0.01 us  [local(): lax.ppermute(sent[step - 1], 'x', shift_pairs(GROUPS, step))]
    unnamed x42 -> x10, local copies, waits for them, and re-layouts: 10 us -> 1.76 us
    all_to_all x1 -> x0, starting transfers between devices: 7.92 us -> none  [local(): pieces = lax.all_to_all(line.reshape(64, 32, HD), ('y', 'zhi', 'zlo'), 0, 0)]
    ppermute x1, waiting for transfers between devices: 0.01 us -> 7.72 us  [local(): from_left = lax.ppermute(high_back, TILE, forward)]
    all_to_all x1 -> x0, waiting for transfers between devices: 6.41 us -> none  [local(): pieces = lax.all_to_all(line.reshape(64, 32, HD), ('y', 'zhi', 'zlo'), 0, 0)]
    ppermute x1, starting transfers between devices: 7.83 us -> 1.91 us  [local(): from_right = lax.ppermute(low_back, TILE, backward)]
    ppermute x3, waiting for transfers between devices: 7.09 us -> 1.64 us  [local(): lax.ppermute(spread, 'x', shift_pairs(GROUPS, step))]
  transfers between devices with their start and end apart: 17 -> 16, of which waited for: 6 -> 5; matrix products, arithmetic and copies ran while one was open for 0% -> 0% of each run, Pallas kernels for 5% -> 5%
where the time goes in v4:
time: 158 us; the launch traced here: 157 us
  blocking collectives  71.5 us (45%)
  starting transfers between devices  49.5 us (31%)
  waiting for transfers between devices  19 us (12%)
  Pallas kernels  13.7 us (9%)
  local copies, waits for them, and re-layouts  1.76 us (1%)
    all_to_all x1, blocking collectives, local(): lax.all_to_all(spread, ('y', 'zlo', 'zhi'), 0, 0, axis_index_groups=mirro...  31.9 us
    all_to_all x1, blocking collectives, local(): pieces = lax.all_to_all(line.reshape(64, 32, HD), ('zlo', 'zhi', 'y'), 0, 0)  25.1 us
    all_to_all x1, blocking collectives, local(): full = lax.all_to_all(piece, ('zlo', 'x'), 0, 0)  14.4 us
    pallas_call x7, Pallas kernels, call(): pl.pallas_call(body, in_specs=[scalars] * smem + [whole] * (len(operands)...  12.8 us
    ppermute x3, starting transfers between devices, local(): lax.ppermute(sent[step - 1], 'x', shift_pairs(GROUPS, step))  12 us
    ppermute x3, starting transfers between devices, local(): lax.ppermute(spread, 'x', shift_pairs(GROUPS, step))  10.8 us
    ppermute x4, starting transfers between devices, local(): other = [lax.ppermute(part, 'core', swap) for part in own]  8.63 us
    ppermute x1, waiting for transfers between devices, local(): from_left = lax.ppermute(high_back, TILE, forward)  7.72 us
  transfers between devices with their start and end apart: 16, of which 5 were waited for; matrix products, arithmetic and copies ran while one was open for 0% of the time, Pallas kernels for 5%

profile of v4, /device:TPU:8, one launch (start us, length us, event | category | flops | bytes accessed | tf_op | source)
XLA Modules:
  0.0 156.9 jit_solution(4208956967732773597)
XLA Ops:
  3.3 31.9 %all_to_all.15.refs_0_ = bf16[16,128,128]{2,1,0:T(8,128)(2,1)S(1)} all-to-all(bf16[16,128,128]{2,1,0:T(8,128)(2,1)S(1)} %shard_map.76), channel_id=1, replica_groups={{0,4,8,12,16,20,24,28,98,102,106,110,114,118,122,126},{32,36,40,44,48,5..., dimensions={0} | all-to-all | bytes 1048576 | tf_op jit(solution)/shard_map/all_to_all | solution.py:351
  35.2 4.9 %collective-permute-start = (bf16[16,128,128]{2,1,0:T(8,128)(2,1)S(1)}, bf16[16,128,128]{2,1,0:T(8,128)(2,1)S(1)}, u32[]{:S(2)}, u32[]{:S(2)}) collective-permute-start(bf16[16,128,128]{2,1,0:T(8,128)(2,1)S(1)} %all_to_all.15.refs_0_), channel_id=1, source_target_pairs={{0,256},{128,384},{256,0},{384,128},{1,257},{129,385},{257,1},{385... | collective-permute-start | bytes 1572872 | tf_op jit(solution)/shard_map/ppermute | solution.py:354
  40.2 3.0 %collective-permute-start.4 = (bf16[16,128,128]{2,1,0:T(8,128)(2,1)S(1)}, bf16[16,128,128]{2,1,0:T(8,128)(2,1)S(1)}, u32[]{:S(2)}, u32[]{:S(2)}) collective-permute-start(bf16[16,128,128]{2,1,0:T(8,128)(2,1)S(1)} %all_to_all.15.refs_0_), channel_id=1, source_target_pairs={{0,384},{128,0},{256,128},{384,256},{1,385},{129,1},{257,129},{385... | collective-permute-start | bytes 1572872 | tf_op jit(solution)/shard_map/ppermute | solution.py:354
  43.2 2.8 %collective-permute-start.3 = (bf16[16,128,128]{2,1,0:T(8,128)(2,1)S(1)}, bf16[16,128,128]{2,1,0:T(8,128)(2,1)S(1)}, u32[]{:S(2)}, u32[]{:S(2)}) collective-permute-start(bf16[16,128,128]{2,1,0:T(8,128)(2,1)S(1)} %all_to_all.15.refs_0_), channel_id=1, source_target_pairs={{0,128},{128,256},{256,384},{384,0},{1,129},{129,257},{257,385},{3... | collective-permute-start | bytes 1572872 | tf_op jit(solution)/shard_map/ppermute | solution.py:354
  47.1 5.1 %collective-permute-start.1 = (bf16[32,4096]{1,0:T(8,128)(2,1)S(1)}, bf16[32,4096]{1,0:T(8,128)(2,1)S(1)}, u32[]{:S(2)}, u32[]{:S(2)}) collective-permute-start(bf16[32,4096]{1,0:T(8,128)(2,1)S(1)} %get-tuple-element.33), channel_id=1, source_target_pairs={{0,32},{32,64},{64,96},{96,128},{128,160},{160,192},{192,224},{224... | collective-permute-start | bytes 786440 | tf_op jit(solution)/shard_map/ppermute | solution.py:371
  52.3 4.6 %collective-permute-start.2 = (bf16[32,4096]{1,0:T(8,128)(2,1)S(1)}, bf16[32,4096]{1,0:T(8,128)(2,1)S(1)}, u32[]{:S(2)}, u32[]{:S(2)}) collective-permute-start(bf16[32,4096]{1,0:T(8,128)(2,1)S(1)} %get-tuple-element.34), channel_id=1, source_target_pairs={{0,480},{32,0},{64,32},{96,64},{128,96},{160,128},{192,160},{224,1... | collective-permute-start | bytes 786440 | tf_op jit(solution)/shard_map/ppermute | solution.py:372
  56.9 4.4 %collective-permute-done.1.low_ref.refs_1_ = bf16[32,4096]{1,0:T(8,128)(2,1)S(1)} collective-permute-done((bf16[32,4096]{1,0:T(8,128)(2,1)S(1)}, bf16[32,4096]{1,0:T(8,128)(2,1)S(1)}, u32[]{:S(2)}, u32[]{:S(2)}) %collective-permute-start.1) | collective-permute-done | bytes 262176 | tf_op jit(solution)/shard_map/ppermute | solution.py:371
  61.3 1.9 %collective-permute-start.5 = (bf16[16,128,128]{2,1,0:T(8,128)(2,1)S(1)}, bf16[16,128,128]{2,1,0:T(8,128)(2,1)S(1)}, u32[]{:S(2)}, u32[]{:S(2)}) collective-permute-start(bf16[16,128,128]{2,1,0:T(8,128)(2,1)S(1)} %all_to_all.15.refs_0_), channel_id=1, source_target_pairs={{0,1},{1,0},{2,3},{3,2},{4,5},{5,4},{6,7},{7,6},{8,9},{9,8},{10,11... | collective-permute-start | bytes 1572872 | tf_op jit(solution)/shard_map/ppermute | solution.py:375
  63.3 2.4 %collective-permute-start.8 = (bf16[16,128,128]{2,1,0:T(8,128)(2,1)S(1)}, bf16[16,128,128]{2,1,0:T(8,128)(2,1)S(1)}, u32[]{:S(2)}, u32[]{:S(2)}) collective-permute-start(bf16[16,128,128]{2,1,0:T(8,128)(2,1)S(1)} %collective-permute-done.4.refs_3_), channel_id=1, source_target_pairs={{0,1},{1,0},{2,3},{3,2},{4,5},{5,4},{6,7},{7,6},{8,9},{9,8},{10,11... | collective-permute-start | bytes 1572872 | tf_op jit(solution)/shard_map/ppermute | solution.py:375
  67.3 1.9 %collective-permute-start.6 = (bf16[16,128,128]{2,1,0:T(8,128)(2,1)S(1)}, bf16[16,128,128]{2,1,0:T(8,128)(2,1)S(1)}, u32[]{:S(2)}, u32[]{:S(2)}) collective-permute-start(bf16[16,128,128]{2,1,0:T(8,128)(2,1)S(1)} %collective-permute-done.3.refs_1_), channel_id=1, source_target_pairs={{0,1},{1,0},{2,3},{3,2},{4,5},{5,4},{6,7},{7,6},{8,9},{9,8},{10,11... | collective-permute-start | bytes 1572872 | tf_op jit(solution)/shard_map/ppermute | solution.py:375
  69.2 2.4 %collective-permute-start.7 = (bf16[16,128,128]{2,1,0:T(8,128)(2,1)S(1)}, bf16[16,128,128]{2,1,0:T(8,128)(2,1)S(1)}, u32[]{:S(2)}, u32[]{:S(2)}) collective-permute-start(bf16[16,128,128]{2,1,0:T(8,128)(2,1)S(1)} %collective-permute-done.refs_2_), channel_id=1, source_target_pairs={{0,1},{1,0},{2,3},{3,2},{4,5},{5,4},{6,7},{7,6},{8,9},{9,8},{10,11... | collective-permute-start | bytes 1572872 | tf_op jit(solution)/shard_map/ppermute | solution.py:375
  73.2 4.3 %shard_map.78 = (bf16[16,128,128]{2,1,0:T(8,128)(2,1)S(1)}, bf16[3,16,128,128]{3,2,1,0:T(8,128)(2,1)S(1)}, bf16[384,256]{1,0:T(8,128)(2,1)S(1)}, bf16[128,192]{1...) custom-call(s32[2]{0:T(128)S(1)} %pad_add_fusion.place_ref, ...), custom_call_target="tpu_custom_call" | custom-call | flops 3000000000 | bytes 12000000 | tf_op jit(solution)/shard_map/pallas_call | solution.py:306
  77.5 2.3 %collective-permute-start.10 = (bf16[3,16,128,128]{3,2,1,0:T(8,128)(2,1)S(1)}, bf16[3,16,128,128]{3,2,1,0:T(8,128)(2,1)S(1)}, u32[]{:S(2)}, u32[]{:S(2)}) collective-permute-start(bf16[3,16,128,128]{3,2,1,0:T(8,128)(2,1)S(1)} %get-tuple-element.43), channel_id=1, source_target_pairs={{0,1},{1,0},{2,3},{3,2},{4,5},{5,4},{6,7},{7,6},{8,9},{9,8},{10,11... | collective-permute-start | bytes 4718600 | tf_op jit(solution)/shard_map/ppermute | solution.py:396
  79.8 2.2 %collective-permute-start.9 = (bf16[16,128,128]{2,1,0:T(8,128)(2,1)S(1)}, bf16[16,128,128]{2,1,0:T(8,128)(2,1)S(1)}, u32[]{:S(2)}, u32[]{:S(2)}) collective-permute-start(bf16[16,128,128]{2,1,0:T(8,128)(2,1)S(1)} %get-tuple-element.41), channel_id=1, source_target_pairs={{0,1},{1,0},{2,3},{3,2},{4,5},{5,4},{6,7},{7,6},{8,9},{9,8},{10,11... | collective-permute-start | bytes 1572872 | tf_op jit(solution)/shard_map/ppermute | solution.py:397
  84.3 5.0 %collective-permute-start.11 = (bf16[16,128,128]{2,1,0:T(8,128)(2,1)S(1)}, bf16[16,128,128]{2,1,0:T(8,128)(2,1)S(1)}, u32[]{:S(2)}, u32[]{:S(2)}) collective-permute-start(bf16[16,128,128]{2,1,0:T(8,128)(2,1)S(1)} %get-tuple-element.46), channel_id=1, source_target_pairs={{0,256},{128,384},{256,0},{384,128},{1,257},{129,385},{257,1},{385... | collective-permute-start | bytes 1572872 | tf_op jit(solution)/shard_map/ppermute | solution.py:413
  89.3 1.9 %collective-permute-start.12 = (bf16[16,128,128]{2,1,0:T(8,128)(2,1)S(1)}, bf16[16,128,128]{2,1,0:T(8,128)(2,1)S(1)}, u32[]{:S(2)}, u32[]{:S(2)}) collective-permute-start(bf16[16,128,128]{2,1,0:T(8,128)(2,1)S(1)} %get-tuple-element.47), channel_id=1, source_target_pairs={{0,128},{128,256},{256,384},{384,0},{1,129},{129,257},{257,385},{3... | collective-permute-start | bytes 1572872 | tf_op jit(solution)/shard_map/ppermute | solution.py:413
  91.2 5.1 %collective-permute-start.13 = (bf16[16,128,128]{2,1,0:T(8,128)(2,1)S(1)}, bf16[16,128,128]{2,1,0:T(8,128)(2,1)S(1)}, u32[]{:S(2)}, u32[]{:S(2)}) collective-permute-start(bf16[16,128,128]{2,1,0:T(8,128)(2,1)S(1)} %get-tuple-element.48), channel_id=1, source_target_pairs={{0,384},{128,0},{256,128},{384,256},{1,385},{129,1},{257,129},{385... | collective-permute-start | bytes 1572872 | tf_op jit(solution)/shard_map/ppermute | solution.py:413
  96.3 1.9 %collective-permute-start.14 = (bf16[32,256]{1,0:T(8,128)(2,1)S(1)}, bf16[32,256]{1,0:T(8,128)(2,1)S(1)}, u32[]{:S(2)}, u32[]{:S(2)}) collective-permute-start(bf16[32,256]{1,0:T(8,128)(2,1)S(1)} %get-tuple-element.50), channel_id=1, source_target_pairs={{0,32},{32,64},{64,96},{96,128},{128,160},{160,192},{192,224},{224... | collective-permute-start | bytes 49160 | tf_op jit(solution)/shard_map/ppermute | solution.py:416
  98.3 7.7 %collective-permute-done.14.from_left_ref = bf16[32,256]{1,0:T(8,128)(2,1)S(1)} collective-permute-done((bf16[32,256]{1,0:T(8,128)(2,1)S(1)}, bf16[32,256]{1,0:T(8,128)(2,1)S(1)}, u32[]{:S(2)}, u32[]{:S(2)}) %collective-permute-start.14) | collective-permute-done | bytes 16416 | tf_op jit(solution)/shard_map/ppermute | solution.py:416
  106.0 1.9 %collective-permute-start.15 = (bf16[32,256]{1,0:T(8,128)(2,1)S(1)}, bf16[32,256]{1,0:T(8,128)(2,1)S(1)}, u32[]{:S(2)}, u32[]{:S(2)}) collective-permute-start(bf16[32,256]{1,0:T(8,128)(2,1)S(1)} %get-tuple-element.51), channel_id=1, source_target_pairs={{0,480},{32,0},{64,32},{96,64},{128,96},{160,128},{192,160},{224,1... | collective-permute-start | bytes 49160 | tf_op jit(solution)/shard_map/ppermute | solution.py:415
  107.9 3.7 %collective-permute-done.15.from_right_ref = bf16[32,256]{1,0:T(8,128)(2,1)S(1)} collective-permute-done((bf16[32,256]{1,0:T(8,128)(2,1)S(1)}, bf16[32,256]{1,0:T(8,128)(2,1)S(1)}, u32[]{:S(2)}, u32[]{:S(2)}) %collective-permute-start.15) | collective-permute-done | bytes 16416 | tf_op jit(solution)/shard_map/ppermute | solution.py:415
  111.6 4.5 %shard_map.81 = bf16[192,4096]{1,0:T(8,128)(2,1)} custom-call(s32[2]{0:T(128)S(1)} %pad_add_fusion.place_ref, f32[192,384]{1,0:T(8,128)S(1)} %get-tuple-element.49.grads_ref, bf16[32,256]{1,0:T(8,128)(2,1)S(1)} %collective-permute-done.14.from_left_ref, bf16[32,256]{1,0:T(8,128)(2,1)S(1)} %collective-permute-done.15.from_right_ref, ...), custom_call_target="tpu_custom_call" | custom-call | flops 800000000 | bytes 8000000 | tf_op jit(solution)/shard_map/pallas_call | solution.py:306
  116.4 25.1 %all_to_all.16.pieces_ref = bf16[64,32,128]{2,1,0:T(8,128)(2,1)S(1)} all-to-all(bf16[64,32,128]{2,1,0:T(8,128)(2,1)S(1)} %bitcast.14), channel_id=1, replica_groups=mesh['x'=4,'zlo'=4,'y'=8,'zhi'=2,'core'=2] {'zlo','zhi','y'}, dimensions={0} | all-to-all | bytes 1048576 | tf_op jit(solution)/shard_map/all_to_all | solution.py:437
  141.7 14.4 %all_to_all.17.full_ref = bf16[16,32,128]{2,1,0:T(8,128)(2,1)S(1)} all-to-all(bf16[16,32,128]{2,1,0:T(8,128)(2,1)S(1)} %shard_map.82), channel_id=1, replica_groups=mesh['x'=4,'zlo'=4,'y'=8,'zhi'=2,'core'=2] {'zlo','x'}, dimensions={0} | all-to-all | bytes 262144 | tf_op jit(solution)/shard_map/all_to_all | solution.py:441
  (31 shorter events, 10.4 us)
Async XLA Ops:
  0.6 45.4 %copy-start = (bf16[1,12,16,4096]{3,2,1,0:T(8,128)(2,1)S(1)}, bf16[1,12,16,4096]{3,2,1,0:T(8,128)(2,1)}, u32[]{:S(2)}) copy-start(bf16[1,12,16,4096]{3,2,1,0:T(8,128)(2,1)} %param.5) | copy-start | bytes 4718596
  0.7 1.0 copy-start.2
  1.7 0.8 copy-start.3
  2.5 70.7 %copy-start.1 = (bf16[1,12,16,4096]{3,2,1,0:T(8,128)(2,1)S(1)}, bf16[1,12,16,4096]{3,2,1,0:T(8,128)(2,1)}, u32[]{:S(2)}) copy-start(bf16[1,12,16,4096]{3,2,1,0:T(8,128)(2,1)} %param.9) | copy-start | bytes 4718596
  2.5 70.7 %copy-start.4 = (s32[1,2]{1,0:T(1,128)S(1)}, s32[1,2]{1,0:T(1,128)}, u32[]{:S(2)}) copy-start(s32[1,2]{1,0:T(1,128)} %band_ref.1) | copy-start | bytes 28
  35.2 28.0 %collective-permute-start = (bf16[16,128,128]{2,1,0:T(8,128)(2,1)S(1)}, bf16[16,128,128]{2,1,0:T(8,128)(2,1)S(1)}, u32[]{:S(2)}, u32[]{:S(2)}) collective-permute-start(bf16[16,128,128]{2,1,0:T(8,128)(2,1)S(1)} %all_to_all.15.refs_0_), channel_id=1, source_target_pairs={{0,256},{128,384},{256,0},{384,128},{1,257},{129,385},{257,1},{385... | collective-permute-start | bytes 1572872 | tf_op jit(solution)/shard_map/ppermute | solution.py:354
  40.2 23.1 %collective-permute-start.4 = (bf16[16,128,128]{2,1,0:T(8,128)(2,1)S(1)}, bf16[16,128,128]{2,1,0:T(8,128)(2,1)S(1)}, u32[]{:S(2)}, u32[]{:S(2)}) collective-permute-start(bf16[16,128,128]{2,1,0:T(8,128)(2,1)S(1)} %all_to_all.15.refs_0_), channel_id=1, source_target_pairs={{0,384},{128,0},{256,128},{384,256},{1,385},{129,1},{257,129},{385... | collective-permute-start | bytes 1572872 | tf_op jit(solution)/shard_map/ppermute | solution.py:354
  43.2 24.1 %collective-permute-start.3 = (bf16[16,128,128]{2,1,0:T(8,128)(2,1)S(1)}, bf16[16,128,128]{2,1,0:T(8,128)(2,1)S(1)}, u32[]{:S(2)}, u32[]{:S(2)}) collective-permute-start(bf16[16,128,128]{2,1,0:T(8,128)(2,1)S(1)} %all_to_all.15.refs_0_), channel_id=1, source_target_pairs={{0,128},{128,256},{256,384},{384,0},{1,129},{129,257},{257,385},{3... | collective-permute-start | bytes 1572872 | tf_op jit(solution)/shard_map/ppermute | solution.py:354
  47.1 14.2 %collective-permute-start.1 = (bf16[32,4096]{1,0:T(8,128)(2,1)S(1)}, bf16[32,4096]{1,0:T(8,128)(2,1)S(1)}, u32[]{:S(2)}, u32[]{:S(2)}) collective-permute-start(bf16[32,4096]{1,0:T(8,128)(2,1)S(1)} %get-tuple-element.33), channel_id=1, source_target_pairs={{0,32},{32,64},{64,96},{96,128},{128,160},{160,192},{192,224},{224... | collective-permute-start | bytes 786440 | tf_op jit(solution)/shard_map/ppermute | solution.py:371
  52.3 11.0 %collective-permute-start.2 = (bf16[32,4096]{1,0:T(8,128)(2,1)S(1)}, bf16[32,4096]{1,0:T(8,128)(2,1)S(1)}, u32[]{:S(2)}, u32[]{:S(2)}) collective-permute-start(bf16[32,4096]{1,0:T(8,128)(2,1)S(1)} %get-tuple-element.34), channel_id=1, source_target_pairs={{0,480},{32,0},{64,32},{96,64},{128,96},{160,128},{192,160},{224,1... | collective-permute-start | bytes 786440 | tf_op jit(solution)/shard_map/ppermute | solution.py:372
  61.3 10.3 %collective-permute-start.5 = (bf16[16,128,128]{2,1,0:T(8,128)(2,1)S(1)}, bf16[16,128,128]{2,1,0:T(8,128)(2,1)S(1)}, u32[]{:S(2)}, u32[]{:S(2)}) collective-permute-start(bf16[16,128,128]{2,1,0:T(8,128)(2,1)S(1)} %all_to_all.15.refs_0_), channel_id=1, source_target_pairs={{0,1},{1,0},{2,3},{3,2},{4,5},{5,4},{6,7},{7,6},{8,9},{9,8},{10,11... | collective-permute-start | bytes 1572872 | tf_op jit(solution)/shard_map/ppermute | solution.py:375
  63.3 8.4 %collective-permute-start.8 = (bf16[16,128,128]{2,1,0:T(8,128)(2,1)S(1)}, bf16[16,128,128]{2,1,0:T(8,128)(2,1)S(1)}, u32[]{:S(2)}, u32[]{:S(2)}) collective-permute-start(bf16[16,128,128]{2,1,0:T(8,128)(2,1)S(1)} %collective-permute-done.4.refs_3_), channel_id=1, source_target_pairs={{0,1},{1,0},{2,3},{3,2},{4,5},{5,4},{6,7},{7,6},{8,9},{9,8},{10,11... | collective-permute-start | bytes 1572872 | tf_op jit(solution)/shard_map/ppermute | solution.py:375
  67.3 4.4 %collective-permute-start.6 = (bf16[16,128,128]{2,1,0:T(8,128)(2,1)S(1)}, bf16[16,128,128]{2,1,0:T(8,128)(2,1)S(1)}, u32[]{:S(2)}, u32[]{:S(2)}) collective-permute-start(bf16[16,128,128]{2,1,0:T(8,128)(2,1)S(1)} %collective-permute-done.3.refs_1_), channel_id=1, source_target_pairs={{0,1},{1,0},{2,3},{3,2},{4,5},{5,4},{6,7},{7,6},{8,9},{9,8},{10,11... | collective-permute-start | bytes 1572872 | tf_op jit(solution)/shard_map/ppermute | solution.py:375
  69.2 3.9 %collective-permute-start.7 = (bf16[16,128,128]{2,1,0:T(8,128)(2,1)S(1)}, bf16[16,128,128]{2,1,0:T(8,128)(2,1)S(1)}, u32[]{:S(2)}, u32[]{:S(2)}) collective-permute-start(bf16[16,128,128]{2,1,0:T(8,128)(2,1)S(1)} %collective-permute-done.refs_2_), channel_id=1, source_target_pairs={{0,1},{1,0},{2,3},{3,2},{4,5},{5,4},{6,7},{7,6},{8,9},{9,8},{10,11... | collective-permute-start | bytes 1572872 | tf_op jit(solution)/shard_map/ppermute | solution.py:375
  77.5 6.3 %collective-permute-start.10 = (bf16[3,16,128,128]{3,2,1,0:T(8,128)(2,1)S(1)}, bf16[3,16,128,128]{3,2,1,0:T(8,128)(2,1)S(1)}, u32[]{:S(2)}, u32[]{:S(2)}) collective-permute-start(bf16[3,16,128,128]{3,2,1,0:T(8,128)(2,1)S(1)} %get-tuple-element.43), channel_id=1, source_target_pairs={{0,1},{1,0},{2,3},{3,2},{4,5},{5,4},{6,7},{7,6},{8,9},{9,8},{10,11... | collective-permute-start | bytes 4718600 | tf_op jit(solution)/shard_map/ppermute | solution.py:396
  79.8 36.3 %collective-permute-start.9 = (bf16[16,128,128]{2,1,0:T(8,128)(2,1)S(1)}, bf16[16,128,128]{2,1,0:T(8,128)(2,1)S(1)}, u32[]{:S(2)}, u32[]{:S(2)}) collective-permute-start(bf16[16,128,128]{2,1,0:T(8,128)(2,1)S(1)} %get-tuple-element.41), channel_id=1, source_target_pairs={{0,1},{1,0},{2,3},{3,2},{4,5},{5,4},{6,7},{7,6},{8,9},{9,8},{10,11... | collective-permute-start | bytes 1572872 | tf_op jit(solution)/shard_map/ppermute | solution.py:397
  84.3 31.8 %collective-permute-start.11 = (bf16[16,128,128]{2,1,0:T(8,128)(2,1)S(1)}, bf16[16,128,128]{2,1,0:T(8,128)(2,1)S(1)}, u32[]{:S(2)}, u32[]{:S(2)}) collective-permute-start(bf16[16,128,128]{2,1,0:T(8,128)(2,1)S(1)} %get-tuple-element.46), channel_id=1, source_target_pairs={{0,256},{128,384},{256,0},{384,128},{1,257},{129,385},{257,1},{385... | collective-permute-start | bytes 1572872 | tf_op jit(solution)/shard_map/ppermute | solution.py:413
  89.3 26.8 %collective-permute-start.12 = (bf16[16,128,128]{2,1,0:T(8,128)(2,1)S(1)}, bf16[16,128,128]{2,1,0:T(8,128)(2,1)S(1)}, u32[]{:S(2)}, u32[]{:S(2)}) collective-permute-start(bf16[16,128,128]{2,1,0:T(8,128)(2,1)S(1)} %get-tuple-element.47), channel_id=1, source_target_pairs={{0,128},{128,256},{256,384},{384,0},{1,129},{129,257},{257,385},{3... | collective-permute-start | bytes 1572872 | tf_op jit(solution)/shard_map/ppermute | solution.py:413
  91.2 24.9 %collective-permute-start.13 = (bf16[16,128,128]{2,1,0:T(8,128)(2,1)S(1)}, bf16[16,128,128]{2,1,0:T(8,128)(2,1)S(1)}, u32[]{:S(2)}, u32[]{:S(2)}) collective-permute-start(bf16[16,128,128]{2,1,0:T(8,128)(2,1)S(1)} %get-tuple-element.48), channel_id=1, source_target_pairs={{0,384},{128,0},{256,128},{384,256},{1,385},{129,1},{257,129},{385... | collective-permute-start | bytes 1572872 | tf_op jit(solution)/shard_map/ppermute | solution.py:413
  96.3 9.6 %collective-permute-start.14 = (bf16[32,256]{1,0:T(8,128)(2,1)S(1)}, bf16[32,256]{1,0:T(8,128)(2,1)S(1)}, u32[]{:S(2)}, u32[]{:S(2)}) collective-permute-start(bf16[32,256]{1,0:T(8,128)(2,1)S(1)} %get-tuple-element.50), channel_id=1, source_target_pairs={{0,32},{32,64},{64,96},{96,128},{128,160},{160,192},{192,224},{224... | collective-permute-start | bytes 49160 | tf_op jit(solution)/shard_map/ppermute | solution.py:416
  106.0 5.6 %collective-permute-start.15 = (bf16[32,256]{1,0:T(8,128)(2,1)S(1)}, bf16[32,256]{1,0:T(8,128)(2,1)S(1)}, u32[]{:S(2)}, u32[]{:S(2)}) collective-permute-start(bf16[32,256]{1,0:T(8,128)(2,1)S(1)} %get-tuple-element.51), channel_id=1, source_target_pairs={{0,480},{32,0},{64,32},{96,64},{128,96},{160,128},{192,160},{224,1... | collective-permute-start | bytes 49160 | tf_op jit(solution)/shard_map/ppermute | solution.py:415

commit v5 on v4

--- a/solution.py
+++ b/solution.py
@@ -244,7 +244,11 @@
 def final_kernel(full_ref, qkv_ref, out_ref):
     for group in range(GROUPS):
         value = jnp.concatenate(
-            [full_ref[4 * quarter + group].astype(F32) for quarter in range(4)], axis=0
+            [
+                full_ref[4 * quarter + (group - 2 * inner_line(quarter)) % GROUPS].astype(F32)
+                for quarter in range(4)
+            ],
+            axis=0,
         )
         if group < 3:
             qkv_ref[:, group * HD : (group + 1) * HD] = value.T
@@ -316,6 +320,28 @@
     )(*operands)
 
 
+def inner_line(zlo):
+    return (zlo + 1) // 2 % 2
+
+
+def send(value, step):
+    if step == 2:
+        return lax.ppermute(value, "zlo", [(0, 1), (1, 0), (2, 3), (3, 2)])
+    return lax.ppermute(value, "x", shift_pairs(GROUPS, step))
+
+
+def line_groups():
+    return [
+        [
+            (((held - 2 * inner_line(zlo)) % GROUPS * 8 + y) * 4 + zlo) * 2 + zhi
+            for zlo in range(4)
+            for zhi in range(2)
+            for y in range(8)
+        ]
+        for held in range(GROUPS)
+    ]
+
+
 def mirrored_groups():
     return [
         [y * 8 + (3 - zlo if zhi else zlo) * 2 + zhi for zhi in range(2) for y in range(8)]
@@ -325,7 +351,8 @@
 
 def local(tokens, w_qkv, w_out, band, cotangent):
     samples, lat_rows, lon_cols, features = tokens.shape
-    place = jnp.stack([lax.axis_index("x"), lax.axis_index("core")]).astype(jnp.int32)
+    held = (lax.axis_index("x") + 2 * inner_line(lax.axis_index("zlo"))) % GROUPS
+    place = jnp.stack([held, lax.axis_index("core")]).astype(jnp.int32)
     forward = shift_pairs(16, 1)
     backward = shift_pairs(16, -1)
     swap = shift_pairs(2, 1)
@@ -351,9 +378,10 @@
     spread = lax.all_to_all(
         spread, ("y", "zlo", "zhi"), 0, 0, axis_index_groups=mirrored_groups()
     )
-    steps = {step: lax.ppermute(spread, "x", shift_pairs(GROUPS, step)) for step in STEPS}
+    steps = {step: send(spread, step) for step in STEPS}
     own = [spread, steps[1], steps[2], steps[3]]
-    late_rows, unused = lax.optimization_barrier((tok_rows, spread))
+    passed = lax.ppermute(spread, "core", swap)
+    late_rows, passed = lax.optimization_barrier((tok_rows, passed))
     normed_own, inverse, first, last = call(
         normalise_kernel,
         [late_rows],
@@ -370,9 +398,9 @@
     )
     low = lax.ppermute(last, TILE, forward)
     high = lax.ppermute(first, TILE, backward)
-    own[2], low, high = lax.optimization_barrier((own[2], low, high))
+    own[3], low, high = lax.optimization_barrier((own[3], low, high))
     normed = [normed_own, low, high]
-    other = [lax.ppermute(part, "core", swap) for part in own]
+    other = [passed] + [lax.ppermute(part, "core", swap) for part in own[1:]]
 
     first_shape = ((BLOCKS, HD, HD), BF16)
     rest_shape = ((GROUPS - 1, BLOCKS, HD, HD), BF16)
@@ -408,13 +436,28 @@
         (kept_rest[step].astype(F32) + got_rest[step].astype(F32)).astype(BF16)
         for step in range(GROUPS - 1)
     ]
-    sent, low_back, high_back = lax.optimization_barrier((sent, low_back, high_back))
     arrived = [
-        lax.ppermute(sent[step - 1], "x", shift_pairs(GROUPS, step)) for step in STEPS
+        send(sent[step - 1], step) for step in STEPS
     ]
     from_right = lax.ppermute(low_back, TILE, backward)
     from_left = lax.ppermute(high_back, TILE, forward)
-    from_left, from_right = lax.optimization_barrier((from_left, from_right))
+    (line,) = call(
+        line_kernel,
+        [kept_first, got_first, *arrived],
+        [((4, BLOCKS, 32, HD), BF16)],
+        [],
+        2_000_000,
+        3_000_000,
+        0,
+    )
+    line, from_left, from_right = lax.optimization_barrier((line, from_left, from_right))
+    pieces = lax.all_to_all(
+        line.reshape(64, 32, HD),
+        ("x", "y", "zlo", "zhi"),
+        0,
+        0,
+        axis_index_groups=line_groups(),
+    )
     (d_tokens,) = call(
         tokens_kernel,
         [place, own_grads, from_left, from_right, tok_rows, inverse, *own, *other],
@@ -424,17 +467,7 @@
         8_000_000,
         1,
     )
-    (line,) = call(
-        line_kernel,
-        [kept_first, got_first, *arrived],
-        [((4, BLOCKS, 32, HD), BF16)],
-        [],
-        2_000_000,
-        3_000_000,
-        0,
-    )
-    line, d_tokens = lax.optimization_barrier((line, d_tokens))
-    pieces = lax.all_to_all(line.reshape(64, 32, HD), ("zlo", "zhi", "y"), 0, 0)
+    pieces, d_tokens = lax.optimization_barrier((pieces, d_tokens))
     (piece,) = call(
         piece_kernel, [pieces], [((16, 32, HD), BF16)], [], 1_000_000, 1_000_000, 0
     )

time: 158 us -> 150 us (0.949)
  blocking collectives: 71.5 us -> 46.6 us
  starting transfers between devices: 49.5 us -> 58.5 us
  local copies, waits for them, and re-layouts: 1.76 us -> 10 us
    all_to_all x1 -> x0, blocking collectives: 25.1 us -> none  [local(): pieces = lax.all_to_all(line.reshape(64, 32, HD), ('zlo', 'zhi', 'y'), 0, 0)]
    unnamed x10 -> x42, local copies, waits for them, and re-layouts: 1.76 us -> 10 us
    all_to_all x0 -> x1, waiting for transfers between devices: none -> 6.44 us  [local(): lax.all_to_all(line.reshape(64, 32, HD), ('x', 'y', 'zlo', 'zhi'), 0, 0,...]
    all_to_all x0 -> x1, starting transfers between devices: none -> 6.32 us  [local(): lax.all_to_all(line.reshape(64, 32, HD), ('x', 'y', 'zlo', 'zhi'), 0, 0,...]
    ppermute x1, waiting for transfers between devices: 7.72 us -> 2.79 us  [local(): from_left = lax.ppermute(high_back, TILE, forward)]
    ppermute x10, waiting for transfers between devices: 3.14 us -> 7.76 us  [the longest x4 4.98 us: send(): return lax.ppermute(value, 'x', shift_pairs(GROUPS, step))]
    ppermute x1, starting transfers between devices: 1.91 us -> 6.37 us  [local(): from_right = lax.ppermute(low_back, TILE, backward)]
    ppermute x1, waiting for transfers between devices: 4.44 us -> 0.01 us  [local(): low = lax.ppermute(last, TILE, forward)]
  transfers between devices with their start and end apart: 16 -> 17, of which waited for: 5 -> 7; matrix products, arithmetic and copies ran while one was open for 0% -> 0% of each run, Pallas kernels for 5% -> 6%
where the time goes in v5:
time: 150 us; the launch traced here: 149 us
  starting transfers between devices  58.5 us (39%)
  blocking collectives  46.6 us (31%)
  waiting for transfers between devices  17.8 us (12%)
  Pallas kernels  14.5 us (10%)
  local copies, waits for them, and re-layouts  10 us (7%)
    all_to_all x1, blocking collectives, local(): lax.all_to_all(spread, ('y', 'zlo', 'zhi'), 0, 0, axis_index_groups=mirro...  31.9 us
    all_to_all x1, blocking collectives, local(): full = lax.all_to_all(piece, ('zlo', 'x'), 0, 0)  14.6 us
    pallas_call x7, Pallas kernels, call(): pl.pallas_call(body, in_specs=[scalars] * smem + [whole] * (len(operands)...  13.7 us
    ppermute x4, starting transfers between devices, send(): return lax.ppermute(value, 'x', shift_pairs(GROUPS, step))  12.9 us
    unnamed x42, local copies, waits for them, and re-layouts  10 us
    ppermute x1, starting transfers between devices, local(): high = lax.ppermute(first, TILE, backward)  7.83 us
    ppermute x2, starting transfers between devices, send(): return lax.ppermute(value, 'zlo', [(0, 1), (1, 0), (2, 3), (3, 2)])  7.62 us
    all_to_all x1, waiting for transfers between devices, local(): lax.all_to_all(line.reshape(64, 32, HD), ('x', 'y', 'zlo', 'zhi'), 0, 0,...  6.44 us
  transfers between devices with their start and end apart: 17, of which 7 were waited for; matrix products, arithmetic and copies ran while one was open for 0% of the time, Pallas kernels for 6%

profile of v5, /device:TPU:8, one launch (start us, length us, event | category | flops | bytes accessed | tf_op | source)
XLA Modules:
  0.0 149.0 jit_solution(4022705468407862290)
XLA Ops:
  3.4 31.9 %all_to_all.15.refs_0_ = bf16[16,128,128]{2,1,0:T(8,128)(2,1)S(1)} all-to-all(bf16[16,128,128]{2,1,0:T(8,128)(2,1)S(1)} %shard_map.76), channel_id=1, replica_groups={{0,4,8,12,16,20,24,28,98,102,106,110,114,118,122,126},{32,36,40,44,48,5..., dimensions={0} | all-to-all | bytes 1048576 | tf_op jit(solution)/shard_map/all_to_all | solution.py:378
  35.3 1.9 %collective-permute-start = (bf16[16,128,128]{2,1,0:T(8,128)(2,1)S(1)}, bf16[16,128,128]{2,1,0:T(8,128)(2,1)S(1)}, u32[]{:S(2)}, u32[]{:S(2)}) collective-permute-start(bf16[16,128,128]{2,1,0:T(8,128)(2,1)S(1)} %all_to_all.15.refs_0_), channel_id=1, source_target_pairs={{0,1},{1,0},{2,3},{3,2},{4,5},{5,4},{6,7},{7,6},{8,9},{9,8},{10,11... | collective-permute-start | bytes 1572872 | tf_op jit(solution)/shard_map/ppermute | solution.py:383
  37.2 5.2 %collective-permute-start.5 = (bf16[16,128,128]{2,1,0:T(8,128)(2,1)S(1)}, bf16[16,128,128]{2,1,0:T(8,128)(2,1)S(1)}, u32[]{:S(2)}, u32[]{:S(2)}) collective-permute-start(bf16[16,128,128]{2,1,0:T(8,128)(2,1)S(1)} %all_to_all.15.refs_0_), channel_id=1, source_target_pairs={{0,32},{32,0},{64,96},{96,64},{1,33},{33,1},{65,97},{97,65},{2,34}... | collective-permute-start | bytes 1572872 | tf_op jit(solution)/shard_map/ppermute | solution.py:329
  42.3 3.4 %collective-permute-start.4 = (bf16[16,128,128]{2,1,0:T(8,128)(2,1)S(1)}, bf16[16,128,128]{2,1,0:T(8,128)(2,1)S(1)}, u32[]{:S(2)}, u32[]{:S(2)}) collective-permute-start(bf16[16,128,128]{2,1,0:T(8,128)(2,1)S(1)} %all_to_all.15.refs_0_), channel_id=1, source_target_pairs={{0,128},{128,256},{256,384},{384,0},{1,129},{129,257},{257,385},{3... | collective-permute-start | bytes 1572872 | tf_op jit(solution)/shard_map/ppermute | solution.py:330
  45.8 3.7 %collective-permute-start.1 = (bf16[16,128,128]{2,1,0:T(8,128)(2,1)S(1)}, bf16[16,128,128]{2,1,0:T(8,128)(2,1)S(1)}, u32[]{:S(2)}, u32[]{:S(2)}) collective-permute-start(bf16[16,128,128]{2,1,0:T(8,128)(2,1)S(1)} %all_to_all.15.refs_0_), channel_id=1, source_target_pairs={{0,384},{128,0},{256,128},{384,256},{1,385},{129,1},{257,129},{385... | collective-permute-start | bytes 1572872 | tf_op jit(solution)/shard_map/ppermute | solution.py:330
  50.5 1.9 %collective-permute-start.2 = (bf16[32,4096]{1,0:T(8,128)(2,1)S(1)}, bf16[32,4096]{1,0:T(8,128)(2,1)S(1)}, u32[]{:S(2)}, u32[]{:S(2)}) collective-permute-start(bf16[32,4096]{1,0:T(8,128)(2,1)S(1)} %get-tuple-element.30), channel_id=1, source_target_pairs={{0,32},{32,64},{64,96},{96,128},{128,160},{160,192},{192,224},{224... | collective-permute-start | bytes 786440 | tf_op jit(solution)/shard_map/ppermute | solution.py:399
  52.4 7.8 %collective-permute-start.3 = (bf16[32,4096]{1,0:T(8,128)(2,1)S(1)}, bf16[32,4096]{1,0:T(8,128)(2,1)S(1)}, u32[]{:S(2)}, u32[]{:S(2)}) collective-permute-start(bf16[32,4096]{1,0:T(8,128)(2,1)S(1)} %get-tuple-element.31), channel_id=1, source_target_pairs={{0,480},{32,0},{64,32},{96,64},{128,96},{160,128},{192,160},{224,1... | collective-permute-start | bytes 786440 | tf_op jit(solution)/shard_map/ppermute | solution.py:400
  60.3 1.9 %collective-permute-start.7 = (bf16[16,128,128]{2,1,0:T(8,128)(2,1)S(1)}, bf16[16,128,128]{2,1,0:T(8,128)(2,1)S(1)}, u32[]{:S(2)}, u32[]{:S(2)}) collective-permute-start(bf16[16,128,128]{2,1,0:T(8,128)(2,1)S(1)} %collective-permute-done.5.refs_2_), channel_id=1, source_target_pairs={{0,1},{1,0},{2,3},{3,2},{4,5},{5,4},{6,7},{7,6},{8,9},{9,8},{10,11... | collective-permute-start | bytes 1572872 | tf_op jit(solution)/shard_map/ppermute | solution.py:403
  62.2 2.4 %collective-permute-done.4.refs_1_ = bf16[16,128,128]{2,1,0:T(8,128)(2,1)S(1)} collective-permute-done((bf16[16,128,128]{2,1,0:T(8,128)(2,1)S(1)}, bf16[16,128,128]{2,1,0:T(8,128)(2,1)S(1)}, u32[]{:S(2)}, u32[]{:S(2)}) %collective-permute-start.4) | collective-permute-done | bytes 524320 | tf_op jit(solution)/shard_map/ppermute | solution.py:330
  64.7 1.9 %collective-permute-start.6 = (bf16[16,128,128]{2,1,0:T(8,128)(2,1)S(1)}, bf16[16,128,128]{2,1,0:T(8,128)(2,1)S(1)}, u32[]{:S(2)}, u32[]{:S(2)}) collective-permute-start(bf16[16,128,128]{2,1,0:T(8,128)(2,1)S(1)} %collective-permute-done.4.refs_1_), channel_id=1, source_target_pairs={{0,1},{1,0},{2,3},{3,2},{4,5},{5,4},{6,7},{7,6},{8,9},{9,8},{10,11... | collective-permute-start | bytes 1572872 | tf_op jit(solution)/shard_map/ppermute | solution.py:403
  71.2 4.3 %shard_map.78 = (bf16[16,128,128]{2,1,0:T(8,128)(2,1)S(1)}, bf16[3,16,128,128]{3,2,1,0:T(8,128)(2,1)S(1)}, bf16[384,256]{1,0:T(8,128)(2,1)S(1)}, bf16[128,192]{1...) custom-call(s32[2]{0:T(128)S(1)} %pad_add_fusion.place_ref, ...), custom_call_target="tpu_custom_call" | custom-call | flops 3000000000 | bytes 12000000 | tf_op jit(solution)/shard_map/pallas_call | solution.py:310
  75.6 2.0 %collective-permute-start.10 = (bf16[3,16,128,128]{3,2,1,0:T(8,128)(2,1)S(1)}, bf16[3,16,128,128]{3,2,1,0:T(8,128)(2,1)S(1)}, u32[]{:S(2)}, u32[]{:S(2)}) collective-permute-start(bf16[3,16,128,128]{3,2,1,0:T(8,128)(2,1)S(1)} %get-tuple-element.41), channel_id=1, source_target_pairs={{0,1},{1,0},{2,3},{3,2},{4,5},{5,4},{6,7},{7,6},{8,9},{9,8},{10,11... | collective-permute-start | bytes 4718600 | tf_op jit(solution)/shard_map/ppermute | solution.py:424
  77.7 2.5 %collective-permute-start.9 = (bf16[16,128,128]{2,1,0:T(8,128)(2,1)S(1)}, bf16[16,128,128]{2,1,0:T(8,128)(2,1)S(1)}, u32[]{:S(2)}, u32[]{:S(2)}) collective-permute-start(bf16[16,128,128]{2,1,0:T(8,128)(2,1)S(1)} %get-tuple-element.39), channel_id=1, source_target_pairs={{0,1},{1,0},{2,3},{3,2},{4,5},{5,4},{6,7},{7,6},{8,9},{9,8},{10,11... | collective-permute-start | bytes 1572872 | tf_op jit(solution)/shard_map/ppermute | solution.py:425
  82.5 3.9 %collective-permute-start.13 = (bf16[16,128,128]{2,1,0:T(8,128)(2,1)S(1)}, bf16[16,128,128]{2,1,0:T(8,128)(2,1)S(1)}, u32[]{:S(2)}, u32[]{:S(2)}) collective-permute-start(bf16[16,128,128]{2,1,0:T(8,128)(2,1)S(1)} %get-tuple-element.53), channel_id=1, source_target_pairs={{0,384},{128,0},{256,128},{384,256},{1,385},{129,1},{257,129},{385... | collective-permute-start | bytes 1572872 | tf_op jit(solution)/shard_map/ppermute | solution.py:330
  86.4 2.0 %collective-permute-start.12 = (bf16[16,128,128]{2,1,0:T(8,128)(2,1)S(1)}, bf16[16,128,128]{2,1,0:T(8,128)(2,1)S(1)}, u32[]{:S(2)}, u32[]{:S(2)}) collective-permute-start(bf16[16,128,128]{2,1,0:T(8,128)(2,1)S(1)} %get-tuple-element.54), channel_id=1, source_target_pairs={{0,128},{128,256},{256,384},{384,0},{1,129},{129,257},{257,385},{3... | collective-permute-start | bytes 1572872 | tf_op jit(solution)/shard_map/ppermute | solution.py:330
  88.3 2.5 %collective-permute-start.11 = (bf16[16,128,128]{2,1,0:T(8,128)(2,1)S(1)}, bf16[16,128,128]{2,1,0:T(8,128)(2,1)S(1)}, u32[]{:S(2)}, u32[]{:S(2)}) collective-permute-start(bf16[16,128,128]{2,1,0:T(8,128)(2,1)S(1)} %get-tuple-element.55), channel_id=1, source_target_pairs={{0,32},{32,0},{64,96},{96,64},{1,33},{33,1},{65,97},{97,65},{2,34}... | collective-permute-start | bytes 1572872 | tf_op jit(solution)/shard_map/ppermute | solution.py:329
  90.8 3.4 %collective-permute-start.14 = (bf16[32,256]{1,0:T(8,128)(2,1)S(1)}, bf16[32,256]{1,0:T(8,128)(2,1)S(1)}, u32[]{:S(2)}, u32[]{:S(2)}) collective-permute-start(bf16[32,256]{1,0:T(8,128)(2,1)S(1)} %get-tuple-element.42), channel_id=1, source_target_pairs={{0,32},{32,64},{64,96},{96,128},{128,160},{160,192},{192,224},{224... | collective-permute-start | bytes 49160 | tf_op jit(solution)/shard_map/ppermute | solution.py:443
  94.2 6.4 %collective-permute-start.15 = (bf16[32,256]{1,0:T(8,128)(2,1)S(1)}, bf16[32,256]{1,0:T(8,128)(2,1)S(1)}, u32[]{:S(2)}, u32[]{:S(2)}) collective-permute-start(bf16[32,256]{1,0:T(8,128)(2,1)S(1)} %get-tuple-element.43), channel_id=1, source_target_pairs={{0,480},{32,0},{64,32},{96,64},{128,96},{160,128},{192,160},{224,1... | collective-permute-start | bytes 49160 | tf_op jit(solution)/shard_map/ppermute | solution.py:442
  100.6 2.5 %collective-permute-done.12.refs_3_ = bf16[16,128,128]{2,1,0:T(8,128)(2,1)S(1)} collective-permute-done((bf16[16,128,128]{2,1,0:T(8,128)(2,1)S(1)}, bf16[16,128,128]{2,1,0:T(8,128)(2,1)S(1)}, u32[]{:S(2)}, u32[]{:S(2)}) %collective-permute-start.12) | collective-permute-done | bytes 524320 | tf_op jit(solution)/shard_map/ppermute | solution.py:330
  105.2 2.8 %collective-permute-done.14.from_left_ref = bf16[32,256]{1,0:T(8,128)(2,1)S(1)} collective-permute-done((bf16[32,256]{1,0:T(8,128)(2,1)S(1)}, bf16[32,256]{1,0:T(8,128)(2,1)S(1)}, u32[]{:S(2)}, u32[]{:S(2)}) %collective-permute-start.14) | collective-permute-done | bytes 16416 | tf_op jit(solution)/shard_map/ppermute | solution.py:443
  108.6 6.3 %all-to-all-start.1 = ((bf16[64,32,128]{2,1,0:T(8,128)(2,1)}), bf16[64,32,128]{2,1,0:T(8,128)(2,1)S(1)}, u32[]{:S(2)}, u32[]{:S(2)}) async-start(bf16[64,32,128]{2,1,0:T(8,128)(2,1)} %bitcast.7), calls=%async_computation.1 | async-start | bytes 1048576 | tf_op jit(solution)/shard_map/all_to_all | solution.py:454
  122.6 4.5 %shard_map.81 = bf16[192,4096]{1,0:T(8,128)(2,1)} custom-call(s32[2]{0:T(128)S(1)} %copy-done.19, f32[192,384]{1,0:T(8,128)S(1)} %get-tuple-element.45.grads_ref, bf16[32,256]{1,0:T(8,128)(2,1)S(1)} %collective-permute-done.14.from_left_ref, bf16[32,256]{1,0:T(8,128)(2,1)S(1)} %copy-done.17, bf16[192,4096]{1,0:T(8,128)(2,1)S(1)} %bitcast.13, ...), custom_call_target="tpu_custom_call" | custom-call | flops 800000000 | bytes 8000000 | tf_op jit(solution)/shard_map/pallas_call | solution.py:310
  127.0 6.4 %all-to-all-done.1.pieces_ref = bf16[64,32,128]{2,1,0:T(8,128)(2,1)S(1)} async-done(((bf16[64,32,128]{2,1,0:T(8,128)(2,1)}), bf16[64,32,128]{2,1,0:T(8,128)(2,1)S(1)}, u32[]{:S(2)}, u32[]{:S(2)}) %all-to-all-start.1) | async-done | bytes 524320 | tf_op jit(solution)/shard_map/all_to_all | solution.py:454
  133.6 14.6 %all_to_all.16.full_ref = bf16[16,32,128]{2,1,0:T(8,128)(2,1)S(1)} all-to-all(bf16[16,32,128]{2,1,0:T(8,128)(2,1)S(1)} %shard_map.82), channel_id=1, replica_groups=mesh['x'=4,'zlo'=4,'y'=8,'zhi'=2,'core'=2] {'zlo','x'}, dimensions={0} | all-to-all | bytes 262144 | tf_op jit(solution)/shard_map/all_to_all | solution.py:474
  (64 shorter events, 21.8 us)
Async XLA Ops:
  0.6 48.8 %copy-start = (bf16[1,12,16,4096]{3,2,1,0:T(8,128)(2,1)S(1)}, bf16[1,12,16,4096]{3,2,1,0:T(8,128)(2,1)}, u32[]{:S(2)}) copy-start(bf16[1,12,16,4096]{3,2,1,0:T(8,128)(2,1)} %param.5) | copy-start | bytes 4718596
  2.5 77.6 %copy-start.18 = (s32[2]{0:T(128)}, s32[2]{0:T(128)S(1)}, u32[]{:S(2)}) copy-start(s32[2]{0:T(128)S(1)} %pad_add_fusion.place_ref) | copy-start | bytes 28
  2.5 68.7 %copy-start.1 = (bf16[1,12,16,4096]{3,2,1,0:T(8,128)(2,1)S(1)}, bf16[1,12,16,4096]{3,2,1,0:T(8,128)(2,1)}, u32[]{:S(2)}) copy-start(bf16[1,12,16,4096]{3,2,1,0:T(8,128)(2,1)} %param.9) | copy-start | bytes 4718596
  2.5 68.7 %copy-start.20 = (s32[1,2]{1,0:T(1,128)S(1)}, s32[1,2]{1,0:T(1,128)}, u32[]{:S(2)}) copy-start(s32[1,2]{1,0:T(1,128)} %band_ref.1) | copy-start | bytes 28
  35.3 14.1 %collective-permute-start = (bf16[16,128,128]{2,1,0:T(8,128)(2,1)S(1)}, bf16[16,128,128]{2,1,0:T(8,128)(2,1)S(1)}, u32[]{:S(2)}, u32[]{:S(2)}) collective-permute-start(bf16[16,128,128]{2,1,0:T(8,128)(2,1)S(1)} %all_to_all.15.refs_0_), channel_id=1, source_target_pairs={{0,1},{1,0},{2,3},{3,2},{4,5},{5,4},{6,7},{7,6},{8,9},{9,8},{10,11... | collective-permute-start | bytes 1572872 | tf_op jit(solution)/shard_map/ppermute | solution.py:383
  37.2 23.1 %collective-permute-start.5 = (bf16[16,128,128]{2,1,0:T(8,128)(2,1)S(1)}, bf16[16,128,128]{2,1,0:T(8,128)(2,1)S(1)}, u32[]{:S(2)}, u32[]{:S(2)}) collective-permute-start(bf16[16,128,128]{2,1,0:T(8,128)(2,1)S(1)} %all_to_all.15.refs_0_), channel_id=1, source_target_pairs={{0,32},{32,0},{64,96},{96,64},{1,33},{33,1},{65,97},{97,65},{2,34}... | collective-permute-start | bytes 1572872 | tf_op jit(solution)/shard_map/ppermute | solution.py:329
  42.3 22.3 %collective-permute-start.4 = (bf16[16,128,128]{2,1,0:T(8,128)(2,1)S(1)}, bf16[16,128,128]{2,1,0:T(8,128)(2,1)S(1)}, u32[]{:S(2)}, u32[]{:S(2)}) collective-permute-start(bf16[16,128,128]{2,1,0:T(8,128)(2,1)S(1)} %all_to_all.15.refs_0_), channel_id=1, source_target_pairs={{0,128},{128,256},{256,384},{384,0},{1,129},{129,257},{257,385},{3... | collective-permute-start | bytes 1572872 | tf_op jit(solution)/shard_map/ppermute | solution.py:330
  45.8 20.8 %collective-permute-start.1 = (bf16[16,128,128]{2,1,0:T(8,128)(2,1)S(1)}, bf16[16,128,128]{2,1,0:T(8,128)(2,1)S(1)}, u32[]{:S(2)}, u32[]{:S(2)}) collective-permute-start(bf16[16,128,128]{2,1,0:T(8,128)(2,1)S(1)} %all_to_all.15.refs_0_), channel_id=1, source_target_pairs={{0,384},{128,0},{256,128},{384,256},{1,385},{129,1},{257,129},{385... | collective-permute-start | bytes 1572872 | tf_op jit(solution)/shard_map/ppermute | solution.py:330
  50.5 16.1 %collective-permute-start.2 = (bf16[32,4096]{1,0:T(8,128)(2,1)S(1)}, bf16[32,4096]{1,0:T(8,128)(2,1)S(1)}, u32[]{:S(2)}, u32[]{:S(2)}) collective-permute-start(bf16[32,4096]{1,0:T(8,128)(2,1)S(1)} %get-tuple-element.30), channel_id=1, source_target_pairs={{0,32},{32,64},{64,96},{96,128},{128,160},{160,192},{192,224},{224... | collective-permute-start | bytes 786440 | tf_op jit(solution)/shard_map/ppermute | solution.py:399
  52.4 15.0 %collective-permute-start.3 = (bf16[32,4096]{1,0:T(8,128)(2,1)S(1)}, bf16[32,4096]{1,0:T(8,128)(2,1)S(1)}, u32[]{:S(2)}, u32[]{:S(2)}) collective-permute-start(bf16[32,4096]{1,0:T(8,128)(2,1)S(1)} %get-tuple-element.31), channel_id=1, source_target_pairs={{0,480},{32,0},{64,32},{96,64},{128,96},{160,128},{192,160},{224,1... | collective-permute-start | bytes 786440 | tf_op jit(solution)/shard_map/ppermute | solution.py:400
  60.3 15.3 %copy-start.2 = (bf16[16,128,128]{2,1,0:T(8,128)(2,1)}, bf16[16,128,128]{2,1,0:T(8,128)(2,1)S(1)}, u32[]{:S(2)}) copy-start(bf16[16,128,128]{2,1,0:T(8,128)(2,1)S(1)} %collective-permute-done.5.refs_2_) | copy-start | bytes 1572868
  60.3 9.0 %collective-permute-start.7 = (bf16[16,128,128]{2,1,0:T(8,128)(2,1)S(1)}, bf16[16,128,128]{2,1,0:T(8,128)(2,1)S(1)}, u32[]{:S(2)}, u32[]{:S(2)}) collective-permute-start(bf16[16,128,128]{2,1,0:T(8,128)(2,1)S(1)} %collective-permute-done.5.refs_2_), channel_id=1, source_target_pairs={{0,1},{1,0},{2,3},{3,2},{4,5},{5,4},{6,7},{7,6},{8,9},{9,8},{10,11... | collective-permute-start | bytes 1572872 | tf_op jit(solution)/shard_map/ppermute | solution.py:403
  64.7 10.9 %copy-start.4 = (bf16[16,128,128]{2,1,0:T(8,128)(2,1)}, bf16[16,128,128]{2,1,0:T(8,128)(2,1)S(1)}, u32[]{:S(2)}) copy-start(bf16[16,128,128]{2,1,0:T(8,128)(2,1)S(1)} %collective-permute-done.4.refs_1_) | copy-start | bytes 1572868
  64.7 4.7 %collective-permute-start.6 = (bf16[16,128,128]{2,1,0:T(8,128)(2,1)S(1)}, bf16[16,128,128]{2,1,0:T(8,128)(2,1)S(1)}, u32[]{:S(2)}, u32[]{:S(2)}) collective-permute-start(bf16[16,128,128]{2,1,0:T(8,128)(2,1)S(1)} %collective-permute-done.4.refs_1_), channel_id=1, source_target_pairs={{0,1},{1,0},{2,3},{3,2},{4,5},{5,4},{6,7},{7,6},{8,9},{9,8},{10,11... | collective-permute-start | bytes 1572872 | tf_op jit(solution)/shard_map/ppermute | solution.py:403
  66.6 9.0 %copy-start.6 = (bf16[16,128,128]{2,1,0:T(8,128)(2,1)}, bf16[16,128,128]{2,1,0:T(8,128)(2,1)S(1)}, u32[]{:S(2)}) copy-start(bf16[16,128,128]{2,1,0:T(8,128)(2,1)S(1)} %collective-permute-done.1.refs_3_) | copy-start | bytes 1572868
  67.4 3.8 %collective-permute-start.8 = (bf16[16,128,128]{2,1,0:T(8,128)(2,1)S(1)}, bf16[16,128,128]{2,1,0:T(8,128)(2,1)S(1)}, u32[]{:S(2)}, u32[]{:S(2)}) collective-permute-start(bf16[16,128,128]{2,1,0:T(8,128)(2,1)S(1)} %collective-permute-done.1.refs_3_), channel_id=1, source_target_pairs={{0,1},{1,0},{2,3},{3,2},{4,5},{5,4},{6,7},{7,6},{8,9},{9,8},{10,11... | collective-permute-start | bytes 1572872 | tf_op jit(solution)/shard_map/ppermute | solution.py:403
  75.6 6.3 %collective-permute-start.10 = (bf16[3,16,128,128]{3,2,1,0:T(8,128)(2,1)S(1)}, bf16[3,16,128,128]{3,2,1,0:T(8,128)(2,1)S(1)}, u32[]{:S(2)}, u32[]{:S(2)}) collective-permute-start(bf16[3,16,128,128]{3,2,1,0:T(8,128)(2,1)S(1)} %get-tuple-element.41), channel_id=1, source_target_pairs={{0,1},{1,0},{2,3},{3,2},{4,5},{5,4},{6,7},{7,6},{8,9},{9,8},{10,11... | collective-permute-start | bytes 4718600 | tf_op jit(solution)/shard_map/ppermute | solution.py:424
  77.7 16.5 %collective-permute-start.9 = (bf16[16,128,128]{2,1,0:T(8,128)(2,1)S(1)}, bf16[16,128,128]{2,1,0:T(8,128)(2,1)S(1)}, u32[]{:S(2)}, u32[]{:S(2)}) collective-permute-start(bf16[16,128,128]{2,1,0:T(8,128)(2,1)S(1)} %get-tuple-element.39), channel_id=1, source_target_pairs={{0,1},{1,0},{2,3},{3,2},{4,5},{5,4},{6,7},{7,6},{8,9},{9,8},{10,11... | collective-permute-start | bytes 1572872 | tf_op jit(solution)/shard_map/ppermute | solution.py:425
  82.5 18.1 %collective-permute-start.13 = (bf16[16,128,128]{2,1,0:T(8,128)(2,1)S(1)}, bf16[16,128,128]{2,1,0:T(8,128)(2,1)S(1)}, u32[]{:S(2)}, u32[]{:S(2)}) collective-permute-start(bf16[16,128,128]{2,1,0:T(8,128)(2,1)S(1)} %get-tuple-element.53), channel_id=1, source_target_pairs={{0,384},{128,0},{256,128},{384,256},{1,385},{129,1},{257,129},{385... | collective-permute-start | bytes 1572872 | tf_op jit(solution)/shard_map/ppermute | solution.py:330
  86.4 16.8 %collective-permute-start.12 = (bf16[16,128,128]{2,1,0:T(8,128)(2,1)S(1)}, bf16[16,128,128]{2,1,0:T(8,128)(2,1)S(1)}, u32[]{:S(2)}, u32[]{:S(2)}) collective-permute-start(bf16[16,128,128]{2,1,0:T(8,128)(2,1)S(1)} %get-tuple-element.54), channel_id=1, source_target_pairs={{0,128},{128,256},{256,384},{384,0},{1,129},{129,257},{257,385},{3... | collective-permute-start | bytes 1572872 | tf_op jit(solution)/shard_map/ppermute | solution.py:330
  88.3 15.7 %collective-permute-start.11 = (bf16[16,128,128]{2,1,0:T(8,128)(2,1)S(1)}, bf16[16,128,128]{2,1,0:T(8,128)(2,1)S(1)}, u32[]{:S(2)}, u32[]{:S(2)}) collective-permute-start(bf16[16,128,128]{2,1,0:T(8,128)(2,1)S(1)} %get-tuple-element.55), channel_id=1, source_target_pairs={{0,32},{32,0},{64,96},{96,64},{1,33},{33,1},{65,97},{97,65},{2,34}... | collective-permute-start | bytes 1572872 | tf_op jit(solution)/shard_map/ppermute | solution.py:329
  90.8 17.2 %collective-permute-start.14 = (bf16[32,256]{1,0:T(8,128)(2,1)S(1)}, bf16[32,256]{1,0:T(8,128)(2,1)S(1)}, u32[]{:S(2)}, u32[]{:S(2)}) collective-permute-start(bf16[32,256]{1,0:T(8,128)(2,1)S(1)} %get-tuple-element.42), channel_id=1, source_target_pairs={{0,32},{32,64},{64,96},{96,128},{128,160},{160,192},{192,224},{224... | collective-permute-start | bytes 49160 | tf_op jit(solution)/shard_map/ppermute | solution.py:443
  94.2 13.8 %collective-permute-start.15 = (bf16[32,256]{1,0:T(8,128)(2,1)S(1)}, bf16[32,256]{1,0:T(8,128)(2,1)S(1)}, u32[]{:S(2)}, u32[]{:S(2)}) collective-permute-start(bf16[32,256]{1,0:T(8,128)(2,1)S(1)} %get-tuple-element.43), channel_id=1, source_target_pairs={{0,480},{32,0},{64,32},{96,64},{128,96},{160,128},{192,160},{224,1... | collective-permute-start | bytes 49160 | tf_op jit(solution)/shard_map/ppermute | solution.py:442
  108.6 24.9 %all-to-all-start.1 = ((bf16[64,32,128]{2,1,0:T(8,128)(2,1)}), bf16[64,32,128]{2,1,0:T(8,128)(2,1)S(1)}, u32[]{:S(2)}, u32[]{:S(2)}) async-start(bf16[64,32,128]{2,1,0:T(8,128)(2,1)} %bitcast.7), calls=%async_computation.1 | async-start | bytes 1048576 | tf_op jit(solution)/shard_map/all_to_all | solution.py:454
  (14 other events, 26.9 us)

commit v6 on v5

--- a/solution.py
+++ b/solution.py
@@ -16,7 +16,8 @@
 ROWS = 192
 EDGE = 24
 PAD = 32
-EXT = ROWS + 2 * PAD
+SENT = 24
+EXT = ROWS + 2 * SENT
 STEPS = (2, 1, 3)
 BLOCKS = 16
 CHUNK = 4
@@ -70,7 +71,7 @@
     mean = jnp.sum(total, axis=-1, keepdims=True) * (1.0 / (2 * BLOCKS * HD))
     inverse = lax.rsqrt(mean + EPS)
     inverse_ref[...] = inverse
-    first, last = edge_chooser((PAD, ROWS), 1)
+    first, last = edge_chooser((SENT, ROWS), 1)
     first, last = as_weights(first), as_weights(last)
     for block in range(0, 2 * BLOCKS, CHUNK):
         columns = slice(block * HD, (block + CHUNK) * HD)
@@ -169,7 +170,7 @@
     place = lax.broadcasted_iota(jnp.int32, (1, EXT), 1)
     column = (place - ROWS) % HALO
     low = (place >= ROWS) & (place < ROWS + EDGE)
-    high = (place >= ROWS + PAD) & (place < ROWS + PAD + EDGE)
+    high = (place >= ROWS + SENT) & (place < ROWS + SENT + EDGE)
     usable = (
         (place < ROWS)
         | (low & (HALO - column <= band_ref[0, 0]))
@@ -190,10 +191,12 @@
     own_grads_ref[:, :HD] = d_query
     own_grads_ref[:, HD : 2 * HD] = d_keys[:ROWS]
     own_grads_ref[:, 2 * HD :] = d_values[:ROWS]
-    for ref, start in ((low_back_ref, ROWS), (high_back_ref, ROWS + PAD)):
-        ref[:, :HD] = d_keys[start : start + PAD].astype(BF16)
-        ref[:, HD:] = d_values[start : start + PAD].astype(BF16)
-    d_query_ext = jnp.concatenate([d_query, jnp.zeros((2 * PAD, HD), F32)], axis=0)
+    filler = jnp.zeros((PAD - SENT, HD), F32)
+    for ref, start in ((low_back_ref, ROWS), (high_back_ref, ROWS + SENT)):
+        for place, value in enumerate((d_keys, d_values)):
+            rows = jnp.concatenate([value[start : start + SENT], filler], axis=0)
+            ref[:, place * HD : (place + 1) * HD] = rows.astype(BF16)
+    d_query_ext = jnp.concatenate([d_query, jnp.zeros((2 * SENT, HD), F32)], axis=0)
     left_qkv = jnp.concatenate([d_query_ext.T, d_keys.T, d_values.T], axis=0).astype(BF16)
     left_out = attended.astype(F32).T.astype(BF16)
     left_qkv_ref[...] = left_qkv
@@ -388,8 +391,8 @@
         [
             ((ROWS, features), BF16),
             ((ROWS, 1), F32),
-            ((PAD, features), BF16),
-            ((PAD, features), BF16),
+            ((SENT, features), BF16),
+            ((SENT, features), BF16),
         ],
         [],
         200_000_000,

time: 150 us -> 149 us (level)
  waiting for transfers between devices: 17.8 us -> 16 us
  transfers between devices with their start and end apart: 17 -> 17, of which waited for: 7 -> 6; matrix products, arithmetic and copies ran while one was open for 0% -> 0% of each run, Pallas kernels for 6% -> 6%
where the time goes in v6:
time: 149 us; the launch traced here: 148 us
  starting transfers between devices  58.4 us (39%)
  blocking collectives  47 us (32%)
  waiting for transfers between devices  16 us (11%)
  Pallas kernels  14.4 us (10%)
  local copies, waits for them, and re-layouts  10 us (7%)
    all_to_all x1, blocking collectives, local(): lax.all_to_all(spread, ('y', 'zlo', 'zhi'), 0, 0, axis_index_groups=mirro...  31.9 us
    all_to_all x1, blocking collectives, local(): full = lax.all_to_all(piece, ('zlo', 'x'), 0, 0)  15.1 us
    pallas_call x7, Pallas kernels, call(): pl.pallas_call(body, in_specs=[scalars] * smem + [whole] * (len(operands)...  13.6 us
    ppermute x4, starting transfers between devices, send(): return lax.ppermute(value, 'x', shift_pairs(GROUPS, step))  12.9 us
    unnamed x42, local copies, waits for them, and re-layouts  10 us
    ppermute x1, starting transfers between devices, local(): high = lax.ppermute(first, TILE, backward)  7.83 us
    ppermute x2, starting transfers between devices, send(): return lax.ppermute(value, 'zlo', [(0, 1), (1, 0), (2, 3), (3, 2)])  7.07 us
    all_to_all x1, waiting for transfers between devices, local(): lax.all_to_all(line.reshape(64, 32, HD), ('x', 'y', 'zlo', 'zhi'), 0, 0,...  6.33 us
  transfers between devices with their start and end apart: 17, of which 6 were waited for; matrix products, arithmetic and copies ran while one was open for 0% of the time, Pallas kernels for 6%

profile of v6, /device:TPU:8, one launch (start us, length us, event | category | flops | bytes accessed | tf_op | source)
XLA Modules:
  0.0 147.5 jit_solution(13361683071296607732)
XLA Ops:
  3.4 31.9 %all_to_all.15.refs_0_ = bf16[16,128,128]{2,1,0:T(8,128)(2,1)S(1)} all-to-all(bf16[16,128,128]{2,1,0:T(8,128)(2,1)S(1)} %shard_map.76), channel_id=1, replica_groups={{0,4,8,12,16,20,24,28,98,102,106,110,114,118,122,126},{32,36,40,44,48,5..., dimensions={0} | all-to-all | bytes 1048576 | tf_op jit(solution)/shard_map/all_to_all | solution.py:381
  35.3 1.9 %collective-permute-start = (bf16[16,128,128]{2,1,0:T(8,128)(2,1)S(1)}, bf16[16,128,128]{2,1,0:T(8,128)(2,1)S(1)}, u32[]{:S(2)}, u32[]{:S(2)}) collective-permute-start(bf16[16,128,128]{2,1,0:T(8,128)(2,1)S(1)} %all_to_all.15.refs_0_), channel_id=1, source_target_pairs={{0,1},{1,0},{2,3},{3,2},{4,5},{5,4},{6,7},{7,6},{8,9},{9,8},{10,11... | collective-permute-start | bytes 1572872 | tf_op jit(solution)/shard_map/ppermute | solution.py:386
  37.2 5.2 %collective-permute-start.5 = (bf16[16,128,128]{2,1,0:T(8,128)(2,1)S(1)}, bf16[16,128,128]{2,1,0:T(8,128)(2,1)S(1)}, u32[]{:S(2)}, u32[]{:S(2)}) collective-permute-start(bf16[16,128,128]{2,1,0:T(8,128)(2,1)S(1)} %all_to_all.15.refs_0_), channel_id=1, source_target_pairs={{0,32},{32,0},{64,96},{96,64},{1,33},{33,1},{65,97},{97,65},{2,34}... | collective-permute-start | bytes 1572872 | tf_op jit(solution)/shard_map/ppermute | solution.py:332
  42.3 3.4 %collective-permute-start.4 = (bf16[16,128,128]{2,1,0:T(8,128)(2,1)S(1)}, bf16[16,128,128]{2,1,0:T(8,128)(2,1)S(1)}, u32[]{:S(2)}, u32[]{:S(2)}) collective-permute-start(bf16[16,128,128]{2,1,0:T(8,128)(2,1)S(1)} %all_to_all.15.refs_0_), channel_id=1, source_target_pairs={{0,128},{128,256},{256,384},{384,0},{1,129},{129,257},{257,385},{3... | collective-permute-start | bytes 1572872 | tf_op jit(solution)/shard_map/ppermute | solution.py:333
  45.8 3.7 %collective-permute-start.1 = (bf16[16,128,128]{2,1,0:T(8,128)(2,1)S(1)}, bf16[16,128,128]{2,1,0:T(8,128)(2,1)S(1)}, u32[]{:S(2)}, u32[]{:S(2)}) collective-permute-start(bf16[16,128,128]{2,1,0:T(8,128)(2,1)S(1)} %all_to_all.15.refs_0_), channel_id=1, source_target_pairs={{0,384},{128,0},{256,128},{384,256},{1,385},{129,1},{257,129},{385... | collective-permute-start | bytes 1572872 | tf_op jit(solution)/shard_map/ppermute | solution.py:333
  50.5 1.9 %collective-permute-start.2 = (bf16[24,4096]{1,0:T(8,128)(2,1)S(1)}, bf16[24,4096]{1,0:T(8,128)(2,1)S(1)}, u32[]{:S(2)}, u32[]{:S(2)}) collective-permute-start(bf16[24,4096]{1,0:T(8,128)(2,1)S(1)} %get-tuple-element.30), channel_id=1, source_target_pairs={{0,32},{32,64},{64,96},{96,128},{128,160},{160,192},{192,224},{224... | collective-permute-start | bytes 589832 | tf_op jit(solution)/shard_map/ppermute | solution.py:402
  52.4 7.8 %collective-permute-start.3 = (bf16[24,4096]{1,0:T(8,128)(2,1)S(1)}, bf16[24,4096]{1,0:T(8,128)(2,1)S(1)}, u32[]{:S(2)}, u32[]{:S(2)}) collective-permute-start(bf16[24,4096]{1,0:T(8,128)(2,1)S(1)} %get-tuple-element.31), channel_id=1, source_target_pairs={{0,480},{32,0},{64,32},{96,64},{128,96},{160,128},{192,160},{224,1... | collective-permute-start | bytes 589832 | tf_op jit(solution)/shard_map/ppermute | solution.py:403
  60.3 1.9 %collective-permute-start.7 = (bf16[16,128,128]{2,1,0:T(8,128)(2,1)S(1)}, bf16[16,128,128]{2,1,0:T(8,128)(2,1)S(1)}, u32[]{:S(2)}, u32[]{:S(2)}) collective-permute-start(bf16[16,128,128]{2,1,0:T(8,128)(2,1)S(1)} %collective-permute-done.5.refs_2_), channel_id=1, source_target_pairs={{0,1},{1,0},{2,3},{3,2},{4,5},{5,4},{6,7},{7,6},{8,9},{9,8},{10,11... | collective-permute-start | bytes 1572872 | tf_op jit(solution)/shard_map/ppermute | solution.py:406
  63.3 1.9 %collective-permute-start.6 = (bf16[16,128,128]{2,1,0:T(8,128)(2,1)S(1)}, bf16[16,128,128]{2,1,0:T(8,128)(2,1)S(1)}, u32[]{:S(2)}, u32[]{:S(2)}) collective-permute-start(bf16[16,128,128]{2,1,0:T(8,128)(2,1)S(1)} %collective-permute-done.4.refs_1_), channel_id=1, source_target_pairs={{0,1},{1,0},{2,3},{3,2},{4,5},{5,4},{6,7},{7,6},{8,9},{9,8},{10,11... | collective-permute-start | bytes 1572872 | tf_op jit(solution)/shard_map/ppermute | solution.py:406
  65.2 2.4 %collective-permute-start.8 = (bf16[16,128,128]{2,1,0:T(8,128)(2,1)S(1)}, bf16[16,128,128]{2,1,0:T(8,128)(2,1)S(1)}, u32[]{:S(2)}, u32[]{:S(2)}) collective-permute-start(bf16[16,128,128]{2,1,0:T(8,128)(2,1)S(1)} %collective-permute-done.1.refs_3_), channel_id=1, source_target_pairs={{0,1},{1,0},{2,3},{3,2},{4,5},{5,4},{6,7},{7,6},{8,9},{9,8},{10,11... | collective-permute-start | bytes 1572872 | tf_op jit(solution)/shard_map/ppermute | solution.py:406
  69.2 4.3 %shard_map.78 = (bf16[16,128,128]{2,1,0:T(8,128)(2,1)S(1)}, bf16[3,16,128,128]{3,2,1,0:T(8,128)(2,1)S(1)}, bf16[384,240]{1,0:T(8,128)(2,1)S(1)}, bf16[128,192]{1...) custom-call(s32[2]{0:T(128)S(1)} %pad_add_fusion.place_ref, ...), custom_call_target="tpu_custom_call" | custom-call | flops 3000000000 | bytes 12000000 | tf_op jit(solution)/shard_map/pallas_call | solution.py:313
  73.5 2.3 %collective-permute-start.10 = (bf16[3,16,128,128]{3,2,1,0:T(8,128)(2,1)S(1)}, bf16[3,16,128,128]{3,2,1,0:T(8,128)(2,1)S(1)}, u32[]{:S(2)}, u32[]{:S(2)}) collective-permute-start(bf16[3,16,128,128]{3,2,1,0:T(8,128)(2,1)S(1)} %get-tuple-element.41), channel_id=1, source_target_pairs={{0,1},{1,0},{2,3},{3,2},{4,5},{5,4},{6,7},{7,6},{8,9},{9,8},{10,11... | collective-permute-start | bytes 4718600 | tf_op jit(solution)/shard_map/ppermute | solution.py:427
  75.8 2.2 %collective-permute-start.9 = (bf16[16,128,128]{2,1,0:T(8,128)(2,1)S(1)}, bf16[16,128,128]{2,1,0:T(8,128)(2,1)S(1)}, u32[]{:S(2)}, u32[]{:S(2)}) collective-permute-start(bf16[16,128,128]{2,1,0:T(8,128)(2,1)S(1)} %get-tuple-element.39), channel_id=1, source_target_pairs={{0,1},{1,0},{2,3},{3,2},{4,5},{5,4},{6,7},{7,6},{8,9},{9,8},{10,11... | collective-permute-start | bytes 1572872 | tf_op jit(solution)/shard_map/ppermute | solution.py:428
  80.4 3.9 %collective-permute-start.13 = (bf16[16,128,128]{2,1,0:T(8,128)(2,1)S(1)}, bf16[16,128,128]{2,1,0:T(8,128)(2,1)S(1)}, u32[]{:S(2)}, u32[]{:S(2)}) collective-permute-start(bf16[16,128,128]{2,1,0:T(8,128)(2,1)S(1)} %get-tuple-element.53), channel_id=1, source_target_pairs={{0,384},{128,0},{256,128},{384,256},{1,385},{129,1},{257,129},{385... | collective-permute-start | bytes 1572872 | tf_op jit(solution)/shard_map/ppermute | solution.py:333
  84.3 1.9 %collective-permute-start.12 = (bf16[16,128,128]{2,1,0:T(8,128)(2,1)S(1)}, bf16[16,128,128]{2,1,0:T(8,128)(2,1)S(1)}, u32[]{:S(2)}, u32[]{:S(2)}) collective-permute-start(bf16[16,128,128]{2,1,0:T(8,128)(2,1)S(1)} %get-tuple-element.54), channel_id=1, source_target_pairs={{0,128},{128,256},{256,384},{384,0},{1,129},{129,257},{257,385},{3... | collective-permute-start | bytes 1572872 | tf_op jit(solution)/shard_map/ppermute | solution.py:333
  86.2 1.9 %collective-permute-start.11 = (bf16[16,128,128]{2,1,0:T(8,128)(2,1)S(1)}, bf16[16,128,128]{2,1,0:T(8,128)(2,1)S(1)}, u32[]{:S(2)}, u32[]{:S(2)}) collective-permute-start(bf16[16,128,128]{2,1,0:T(8,128)(2,1)S(1)} %get-tuple-element.55), channel_id=1, source_target_pairs={{0,32},{32,0},{64,96},{96,64},{1,33},{33,1},{65,97},{97,65},{2,34}... | collective-permute-start | bytes 1572872 | tf_op jit(solution)/shard_map/ppermute | solution.py:332
  88.2 3.9 %collective-permute-start.14 = (bf16[32,256]{1,0:T(8,128)(2,1)S(1)}, bf16[32,256]{1,0:T(8,128)(2,1)S(1)}, u32[]{:S(2)}, u32[]{:S(2)}) collective-permute-start(bf16[32,256]{1,0:T(8,128)(2,1)S(1)} %get-tuple-element.42), channel_id=1, source_target_pairs={{0,32},{32,64},{64,96},{96,128},{128,160},{160,192},{192,224},{224... | collective-permute-start | bytes 49160 | tf_op jit(solution)/shard_map/ppermute | solution.py:446
  92.1 6.1 %collective-permute-start.15 = (bf16[32,256]{1,0:T(8,128)(2,1)S(1)}, bf16[32,256]{1,0:T(8,128)(2,1)S(1)}, u32[]{:S(2)}, u32[]{:S(2)}) collective-permute-start(bf16[32,256]{1,0:T(8,128)(2,1)S(1)} %get-tuple-element.43), channel_id=1, source_target_pairs={{0,480},{32,0},{64,32},{96,64},{128,96},{160,128},{192,160},{224,1... | collective-permute-start | bytes 49160 | tf_op jit(solution)/shard_map/ppermute | solution.py:445
  98.2 3.1 %collective-permute-done.12.refs_3_ = bf16[16,128,128]{2,1,0:T(8,128)(2,1)S(1)} collective-permute-done((bf16[16,128,128]{2,1,0:T(8,128)(2,1)S(1)}, bf16[16,128,128]{2,1,0:T(8,128)(2,1)S(1)}, u32[]{:S(2)}, u32[]{:S(2)}) %collective-permute-start.12) | collective-permute-done | bytes 524320 | tf_op jit(solution)/shard_map/ppermute | solution.py:333
  103.4 3.1 %collective-permute-done.14.from_left_ref = bf16[32,256]{1,0:T(8,128)(2,1)S(1)} collective-permute-done((bf16[32,256]{1,0:T(8,128)(2,1)S(1)}, bf16[32,256]{1,0:T(8,128)(2,1)S(1)}, u32[]{:S(2)}, u32[]{:S(2)}) %collective-permute-start.14) | collective-permute-done | bytes 16416 | tf_op jit(solution)/shard_map/ppermute | solution.py:446
  107.1 5.9 %all-to-all-start.1 = ((bf16[64,32,128]{2,1,0:T(8,128)(2,1)}), bf16[64,32,128]{2,1,0:T(8,128)(2,1)S(1)}, u32[]{:S(2)}, u32[]{:S(2)}) async-start(bf16[64,32,128]{2,1,0:T(8,128)(2,1)} %bitcast.7), calls=%async_computation.1 | async-start | bytes 1048576 | tf_op jit(solution)/shard_map/all_to_all | solution.py:457
  120.7 4.5 %shard_map.81 = bf16[192,4096]{1,0:T(8,128)(2,1)} custom-call(s32[2]{0:T(128)S(1)} %copy-done.19, f32[192,384]{1,0:T(8,128)S(1)} %get-tuple-element.45.grads_ref, bf16[32,256]{1,0:T(8,128)(2,1)S(1)} %collective-permute-done.14.from_left_ref, bf16[32,256]{1,0:T(8,128)(2,1)S(1)} %copy-done.17, bf16[192,4096]{1,0:T(8,128)(2,1)S(1)} %bitcast.13, ...), custom_call_target="tpu_custom_call" | custom-call | flops 800000000 | bytes 8000000 | tf_op jit(solution)/shard_map/pallas_call | solution.py:313
  125.2 6.3 %all-to-all-done.1.pieces_ref = bf16[64,32,128]{2,1,0:T(8,128)(2,1)S(1)} async-done(((bf16[64,32,128]{2,1,0:T(8,128)(2,1)}), bf16[64,32,128]{2,1,0:T(8,128)(2,1)S(1)}, u32[]{:S(2)}, u32[]{:S(2)}) %all-to-all-start.1) | async-done | bytes 524320 | tf_op jit(solution)/shard_map/all_to_all | solution.py:457
  131.6 15.1 %all_to_all.16.full_ref = bf16[16,32,128]{2,1,0:T(8,128)(2,1)S(1)} all-to-all(bf16[16,32,128]{2,1,0:T(8,128)(2,1)S(1)} %shard_map.82), channel_id=1, replica_groups=mesh['x'=4,'zlo'=4,'y'=8,'zhi'=2,'core'=2] {'zlo','x'}, dimensions={0} | all-to-all | bytes 262144 | tf_op jit(solution)/shard_map/all_to_all | solution.py:477
  (64 shorter events, 19.7 us)
Async XLA Ops:
  0.6 48.8 %copy-start = (bf16[1,12,16,4096]{3,2,1,0:T(8,128)(2,1)S(1)}, bf16[1,12,16,4096]{3,2,1,0:T(8,128)(2,1)}, u32[]{:S(2)}) copy-start(bf16[1,12,16,4096]{3,2,1,0:T(8,128)(2,1)} %param.5) | copy-start | bytes 4718596
  2.5 75.5 %copy-start.18 = (s32[2]{0:T(128)}, s32[2]{0:T(128)S(1)}, u32[]{:S(2)}) copy-start(s32[2]{0:T(128)S(1)} %pad_add_fusion.place_ref) | copy-start | bytes 28
  2.5 66.7 %copy-start.1 = (bf16[1,12,16,4096]{3,2,1,0:T(8,128)(2,1)S(1)}, bf16[1,12,16,4096]{3,2,1,0:T(8,128)(2,1)}, u32[]{:S(2)}) copy-start(bf16[1,12,16,4096]{3,2,1,0:T(8,128)(2,1)} %param.9) | copy-start | bytes 4718596
  2.5 66.7 %copy-start.20 = (s32[1,2]{1,0:T(1,128)S(1)}, s32[1,2]{1,0:T(1,128)}, u32[]{:S(2)}) copy-start(s32[1,2]{1,0:T(1,128)} %band_ref.1) | copy-start | bytes 28
  35.3 14.1 %collective-permute-start = (bf16[16,128,128]{2,1,0:T(8,128)(2,1)S(1)}, bf16[16,128,128]{2,1,0:T(8,128)(2,1)S(1)}, u32[]{:S(2)}, u32[]{:S(2)}) collective-permute-start(bf16[16,128,128]{2,1,0:T(8,128)(2,1)S(1)} %all_to_all.15.refs_0_), channel_id=1, source_target_pairs={{0,1},{1,0},{2,3},{3,2},{4,5},{5,4},{6,7},{7,6},{8,9},{9,8},{10,11... | collective-permute-start | bytes 1572872 | tf_op jit(solution)/shard_map/ppermute | solution.py:386
  37.2 23.1 %collective-permute-start.5 = (bf16[16,128,128]{2,1,0:T(8,128)(2,1)S(1)}, bf16[16,128,128]{2,1,0:T(8,128)(2,1)S(1)}, u32[]{:S(2)}, u32[]{:S(2)}) collective-permute-start(bf16[16,128,128]{2,1,0:T(8,128)(2,1)S(1)} %all_to_all.15.refs_0_), channel_id=1, source_target_pairs={{0,32},{32,0},{64,96},{96,64},{1,33},{33,1},{65,97},{97,65},{2,34}... | collective-permute-start | bytes 1572872 | tf_op jit(solution)/shard_map/ppermute | solution.py:332
  42.3 20.9 %collective-permute-start.4 = (bf16[16,128,128]{2,1,0:T(8,128)(2,1)S(1)}, bf16[16,128,128]{2,1,0:T(8,128)(2,1)S(1)}, u32[]{:S(2)}, u32[]{:S(2)}) collective-permute-start(bf16[16,128,128]{2,1,0:T(8,128)(2,1)S(1)} %all_to_all.15.refs_0_), channel_id=1, source_target_pairs={{0,128},{128,256},{256,384},{384,0},{1,129},{129,257},{257,385},{3... | collective-permute-start | bytes 1572872 | tf_op jit(solution)/shard_map/ppermute | solution.py:333
  45.8 19.4 %collective-permute-start.1 = (bf16[16,128,128]{2,1,0:T(8,128)(2,1)S(1)}, bf16[16,128,128]{2,1,0:T(8,128)(2,1)S(1)}, u32[]{:S(2)}, u32[]{:S(2)}) collective-permute-start(bf16[16,128,128]{2,1,0:T(8,128)(2,1)S(1)} %all_to_all.15.refs_0_), channel_id=1, source_target_pairs={{0,384},{128,0},{256,128},{384,256},{1,385},{129,1},{257,129},{385... | collective-permute-start | bytes 1572872 | tf_op jit(solution)/shard_map/ppermute | solution.py:333
  50.5 14.7 %collective-permute-start.2 = (bf16[24,4096]{1,0:T(8,128)(2,1)S(1)}, bf16[24,4096]{1,0:T(8,128)(2,1)S(1)}, u32[]{:S(2)}, u32[]{:S(2)}) collective-permute-start(bf16[24,4096]{1,0:T(8,128)(2,1)S(1)} %get-tuple-element.30), channel_id=1, source_target_pairs={{0,32},{32,64},{64,96},{96,128},{128,160},{160,192},{192,224},{224... | collective-permute-start | bytes 589832 | tf_op jit(solution)/shard_map/ppermute | solution.py:402
  52.4 12.8 %collective-permute-start.3 = (bf16[24,4096]{1,0:T(8,128)(2,1)S(1)}, bf16[24,4096]{1,0:T(8,128)(2,1)S(1)}, u32[]{:S(2)}, u32[]{:S(2)}) collective-permute-start(bf16[24,4096]{1,0:T(8,128)(2,1)S(1)} %get-tuple-element.31), channel_id=1, source_target_pairs={{0,480},{32,0},{64,32},{96,64},{128,96},{160,128},{192,160},{224,1... | collective-permute-start | bytes 589832 | tf_op jit(solution)/shard_map/ppermute | solution.py:403
  60.3 13.2 %copy-start.2 = (bf16[16,128,128]{2,1,0:T(8,128)(2,1)}, bf16[16,128,128]{2,1,0:T(8,128)(2,1)S(1)}, u32[]{:S(2)}) copy-start(bf16[16,128,128]{2,1,0:T(8,128)(2,1)S(1)} %collective-permute-done.5.refs_2_) | copy-start | bytes 1572868
  60.3 7.3 %collective-permute-start.7 = (bf16[16,128,128]{2,1,0:T(8,128)(2,1)S(1)}, bf16[16,128,128]{2,1,0:T(8,128)(2,1)S(1)}, u32[]{:S(2)}, u32[]{:S(2)}) collective-permute-start(bf16[16,128,128]{2,1,0:T(8,128)(2,1)S(1)} %collective-permute-done.5.refs_2_), channel_id=1, source_target_pairs={{0,1},{1,0},{2,3},{3,2},{4,5},{5,4},{6,7},{7,6},{8,9},{9,8},{10,11... | collective-permute-start | bytes 1572872 | tf_op jit(solution)/shard_map/ppermute | solution.py:406
  63.3 10.2 %copy-start.4 = (bf16[16,128,128]{2,1,0:T(8,128)(2,1)}, bf16[16,128,128]{2,1,0:T(8,128)(2,1)S(1)}, u32[]{:S(2)}) copy-start(bf16[16,128,128]{2,1,0:T(8,128)(2,1)S(1)} %collective-permute-done.4.refs_1_) | copy-start | bytes 1572868
  63.3 4.4 %collective-permute-start.6 = (bf16[16,128,128]{2,1,0:T(8,128)(2,1)S(1)}, bf16[16,128,128]{2,1,0:T(8,128)(2,1)S(1)}, u32[]{:S(2)}, u32[]{:S(2)}) collective-permute-start(bf16[16,128,128]{2,1,0:T(8,128)(2,1)S(1)} %collective-permute-done.4.refs_1_), channel_id=1, source_target_pairs={{0,1},{1,0},{2,3},{3,2},{4,5},{5,4},{6,7},{7,6},{8,9},{9,8},{10,11... | collective-permute-start | bytes 1572872 | tf_op jit(solution)/shard_map/ppermute | solution.py:406
  65.2 8.3 %copy-start.6 = (bf16[16,128,128]{2,1,0:T(8,128)(2,1)}, bf16[16,128,128]{2,1,0:T(8,128)(2,1)S(1)}, u32[]{:S(2)}) copy-start(bf16[16,128,128]{2,1,0:T(8,128)(2,1)S(1)} %collective-permute-done.1.refs_3_) | copy-start | bytes 1572868
  65.2 3.9 %collective-permute-start.8 = (bf16[16,128,128]{2,1,0:T(8,128)(2,1)S(1)}, bf16[16,128,128]{2,1,0:T(8,128)(2,1)S(1)}, u32[]{:S(2)}, u32[]{:S(2)}) collective-permute-start(bf16[16,128,128]{2,1,0:T(8,128)(2,1)S(1)} %collective-permute-done.1.refs_3_), channel_id=1, source_target_pairs={{0,1},{1,0},{2,3},{3,2},{4,5},{5,4},{6,7},{7,6},{8,9},{9,8},{10,11... | collective-permute-start | bytes 1572872 | tf_op jit(solution)/shard_map/ppermute | solution.py:406
  73.5 6.3 %collective-permute-start.10 = (bf16[3,16,128,128]{3,2,1,0:T(8,128)(2,1)S(1)}, bf16[3,16,128,128]{3,2,1,0:T(8,128)(2,1)S(1)}, u32[]{:S(2)}, u32[]{:S(2)}) collective-permute-start(bf16[3,16,128,128]{3,2,1,0:T(8,128)(2,1)S(1)} %get-tuple-element.41), channel_id=1, source_target_pairs={{0,1},{1,0},{2,3},{3,2},{4,5},{5,4},{6,7},{7,6},{8,9},{9,8},{10,11... | collective-permute-start | bytes 4718600 | tf_op jit(solution)/shard_map/ppermute | solution.py:427
  75.8 16.3 %collective-permute-start.9 = (bf16[16,128,128]{2,1,0:T(8,128)(2,1)S(1)}, bf16[16,128,128]{2,1,0:T(8,128)(2,1)S(1)}, u32[]{:S(2)}, u32[]{:S(2)}) collective-permute-start(bf16[16,128,128]{2,1,0:T(8,128)(2,1)S(1)} %get-tuple-element.39), channel_id=1, source_target_pairs={{0,1},{1,0},{2,3},{3,2},{4,5},{5,4},{6,7},{7,6},{8,9},{9,8},{10,11... | collective-permute-start | bytes 1572872 | tf_op jit(solution)/shard_map/ppermute | solution.py:428
  80.4 17.9 %collective-permute-start.13 = (bf16[16,128,128]{2,1,0:T(8,128)(2,1)S(1)}, bf16[16,128,128]{2,1,0:T(8,128)(2,1)S(1)}, u32[]{:S(2)}, u32[]{:S(2)}) collective-permute-start(bf16[16,128,128]{2,1,0:T(8,128)(2,1)S(1)} %get-tuple-element.53), channel_id=1, source_target_pairs={{0,384},{128,0},{256,128},{384,256},{1,385},{129,1},{257,129},{385... | collective-permute-start | bytes 1572872 | tf_op jit(solution)/shard_map/ppermute | solution.py:333
  84.3 17.1 %collective-permute-start.12 = (bf16[16,128,128]{2,1,0:T(8,128)(2,1)S(1)}, bf16[16,128,128]{2,1,0:T(8,128)(2,1)S(1)}, u32[]{:S(2)}, u32[]{:S(2)}) collective-permute-start(bf16[16,128,128]{2,1,0:T(8,128)(2,1)S(1)} %get-tuple-element.54), channel_id=1, source_target_pairs={{0,128},{128,256},{256,384},{384,0},{1,129},{129,257},{257,385},{3... | collective-permute-start | bytes 1572872 | tf_op jit(solution)/shard_map/ppermute | solution.py:333
  86.2 16.0 %collective-permute-start.11 = (bf16[16,128,128]{2,1,0:T(8,128)(2,1)S(1)}, bf16[16,128,128]{2,1,0:T(8,128)(2,1)S(1)}, u32[]{:S(2)}, u32[]{:S(2)}) collective-permute-start(bf16[16,128,128]{2,1,0:T(8,128)(2,1)S(1)} %get-tuple-element.55), channel_id=1, source_target_pairs={{0,32},{32,0},{64,96},{96,64},{1,33},{33,1},{65,97},{97,65},{2,34}... | collective-permute-start | bytes 1572872 | tf_op jit(solution)/shard_map/ppermute | solution.py:332
  88.2 18.4 %collective-permute-start.14 = (bf16[32,256]{1,0:T(8,128)(2,1)S(1)}, bf16[32,256]{1,0:T(8,128)(2,1)S(1)}, u32[]{:S(2)}, u32[]{:S(2)}) collective-permute-start(bf16[32,256]{1,0:T(8,128)(2,1)S(1)} %get-tuple-element.42), channel_id=1, source_target_pairs={{0,32},{32,64},{64,96},{96,128},{128,160},{160,192},{192,224},{224... | collective-permute-start | bytes 49160 | tf_op jit(solution)/shard_map/ppermute | solution.py:446
  92.1 14.4 %collective-permute-start.15 = (bf16[32,256]{1,0:T(8,128)(2,1)S(1)}, bf16[32,256]{1,0:T(8,128)(2,1)S(1)}, u32[]{:S(2)}, u32[]{:S(2)}) collective-permute-start(bf16[32,256]{1,0:T(8,128)(2,1)S(1)} %get-tuple-element.43), channel_id=1, source_target_pairs={{0,480},{32,0},{64,32},{96,64},{128,96},{160,128},{192,160},{224,1... | collective-permute-start | bytes 49160 | tf_op jit(solution)/shard_map/ppermute | solution.py:445
  107.1 24.4 %all-to-all-start.1 = ((bf16[64,32,128]{2,1,0:T(8,128)(2,1)}), bf16[64,32,128]{2,1,0:T(8,128)(2,1)S(1)}, u32[]{:S(2)}, u32[]{:S(2)}) async-start(bf16[64,32,128]{2,1,0:T(8,128)(2,1)} %bitcast.7), calls=%async_computation.1 | async-start | bytes 1048576 | tf_op jit(solution)/shard_map/all_to_all | solution.py:457
  (14 other events, 26.0 us)
